TPU v7x, 32 devices: a whole 2x2x4 slice. The times are simulated.
32 devices in a mesh: ctx: 8 (over z, x), head: 4 (over y, core).
Axes of the slice: x: 2, y: 2, z: 4, core: 2. Of those that a mesh axis runs over, the one named last changes fastest.
Arguments:
- queries: bfloat16 [1024, 64, 576], P('ctx', 'head'), may hold values from -104 to 104
- latent: bfloat16 [1024, 576], P('ctx'), may hold values from -6 to 6
- cotangent: bfloat16 [1024, 64, 512], P('ctx', 'head'), may hold values from -6 to 6
- selection: int32 [1024, 8], P('ctx'), may hold values from -1 to 15, as said below
Outputs:
- attended: bfloat16 [1024, 64, 512], P('ctx', 'head')
- grad_queries: bfloat16 [1024, 64, 576], P('ctx', 'head')
- grad_latent: float32 [1024, 576], P('ctx')
Inputs may be any that keep to these rules, and one draw needn't show every extreme that they name: `selection`: row t lists distinct blocks, -1 in unused entries. It always lists the block of token t and never a later block. Call the 128 tokens of one index of the ctx axis a range. Besides blocks of its own range, a row lists at most one block of any other range; that range lies earlier, and all tokens of one 64-token block that list a block of a given range list the same one. So the tokens of one range list at most 2 blocks of another range. Rows of the last range always list a block of the first range. A row has unused entries only where fewer than 8 blocks are allowed by these rules.
All inputs are finite; a program needn't handle non-finite values.
Results may differ from a plain program's by a relative error of at most 0.03.
Values may be sent and summed in bfloat16 or wider, within the bound.
No kernel may reach another device: no remote copies, remote signals or barrier semaphores. Data moves between devices by JAX's collectives and lax.ppermute only.
A program may use at most 128 MiB of HBM per device.

v0:
```python
import jax
import jax.numpy as jnp
from jax import lax
from jax.sharding import PartitionSpec as P

BLOCK = 64


softmax_scale = 192.0 ** (-0.5)


def block_table(chosen, my_shard, shards, blocks_here):
    tok_rows = chosen.shape[0]
    block_count = shards * blocks_here
    picked = jnp.any(
        chosen[:, :, None] == jnp.arange(block_count, dtype=jnp.int32)[None, None, :], axis=1
    )
    grouped = picked.reshape(tok_rows, shards, blocks_here)
    own_chosen = lax.dynamic_index_in_dim(grouped, my_shard, 1, keepdims=False)
    others = jnp.arange(shards, dtype=jnp.int32) != my_shard
    per_peer = jnp.any(grouped, axis=2) & others[None, :]
    requested = jnp.any(grouped.reshape(blocks_here, BLOCK, shards, blocks_here), axis=1)
    wanted = jnp.sum(
        jnp.where(requested, jnp.arange(blocks_here, dtype=jnp.int32)[None, None, :], 0), axis=2
    )
    wanted = jnp.where(others[None, :], wanted, 0).T
    return (own_chosen, per_peer, wanted)


def attend(query_rows, grad_rows, key_rows, allowed):
    value_width = grad_rows.shape[1]
    latent_width = key_rows.shape[1]
    values = key_rows[:, :value_width]
    scores = jnp.dot(query_rows, key_rows.T, preferred_element_type=jnp.float32) * softmax_scale
    masked = jnp.where(allowed, scores, -jnp.inf)
    row_max = jnp.max(masked, axis=1, keepdims=True)
    row_sum = jnp.sum(jnp.exp(masked - row_max), axis=1, keepdims=True)
    log_total = row_max + jnp.log(row_sum)
    weights = jnp.exp(masked - log_total)
    weights_low = weights.astype(jnp.bfloat16)
    result = jnp.dot(weights_low, values, preferred_element_type=jnp.float32).astype(jnp.bfloat16)
    row_delta = jnp.sum(
        grad_rows.astype(jnp.float32) * result.astype(jnp.float32), axis=1, keepdims=True
    )
    grad_weights = jnp.dot(grad_rows, values.T, preferred_element_type=jnp.float32)
    grad_scores = (softmax_scale * weights * (grad_weights - row_delta)).astype(jnp.bfloat16)
    grad_query = jnp.dot(grad_scores, key_rows, preferred_element_type=jnp.float32).astype(
        jnp.bfloat16
    )
    grad_keys = jnp.dot(grad_scores.T, query_rows, preferred_element_type=jnp.float32)
    grad_values = jnp.dot(weights_low.T, grad_rows, preferred_element_type=jnp.float32)
    grad_keys = grad_keys + jnp.pad(grad_values, ((0, 0), (0, latent_width - value_width)))
    return (result, grad_query, grad_keys)


def body(queries, latent, cotangent, selection):
    tok_rows, head_count, latent_width = queries.shape
    value_width = cotangent.shape[2]
    shards = lax.axis_size("ctx")
    my_shard = lax.axis_index("ctx")
    blocks_here = tok_rows // BLOCK
    own_chosen, per_peer, wanted = block_table(selection, my_shard, shards, blocks_here)
    all_rows = lax.all_gather(latent, "ctx", axis=0, tiled=True)
    starts = (jnp.arange(shards, dtype=jnp.int32)[:, None] * blocks_here + wanted).reshape(-1)
    fetched = jnp.take(all_rows.reshape(shards * blocks_here, BLOCK, latent_width), starts, axis=0)
    fetched = fetched.reshape(shards, blocks_here, BLOCK, latent_width)
    position = jnp.arange(tok_rows, dtype=jnp.int32)
    own_keys = jnp.repeat(own_chosen, BLOCK, axis=1) & (position[None, :] <= position[:, None])

    def block_step(running, block_index):
        start = block_index * BLOCK
        query_rows = lax.dynamic_slice_in_dim(queries, start, BLOCK, 0).reshape(
            BLOCK * head_count, latent_width
        )
        grad_rows = lax.dynamic_slice_in_dim(cotangent, start, BLOCK, 0).reshape(
            BLOCK * head_count, value_width
        )
        slot_keys = lax.dynamic_index_in_dim(fetched, block_index, 1, keepdims=False).reshape(
            shards * BLOCK, latent_width
        )
        key_rows = jnp.concatenate([latent, slot_keys], axis=0)
        mask_own = lax.dynamic_slice_in_dim(own_keys, start, BLOCK, 0)
        mask_peer = jnp.repeat(lax.dynamic_slice_in_dim(per_peer, start, BLOCK, 0), BLOCK, axis=1)
        allowed = jnp.repeat(jnp.concatenate([mask_own, mask_peer], axis=1), head_count, axis=0)
        result, grad_query, grad_keys = attend(query_rows, grad_rows, key_rows, allowed)
        outputs = (
            result.reshape(BLOCK, head_count, value_width),
            grad_query.reshape(BLOCK, head_count, latent_width),
            grad_keys[tok_rows:].reshape(shards, BLOCK, latent_width),
        )
        return (running + grad_keys[:tok_rows], outputs)

    zeros_init = jnp.zeros((tok_rows, latent_width), jnp.float32)
    own_grad, (results, grad_blocks, slot_parts) = lax.scan(
        block_step, zeros_init, jnp.arange(blocks_here, dtype=jnp.int32)
    )
    attended = results.reshape(tok_rows, head_count, value_width)
    grad_queries = grad_blocks.reshape(tok_rows, head_count, latent_width)
    slot_grad = jnp.moveaxis(slot_parts, 0, 1)
    block_ids = jnp.arange(blocks_here, dtype=jnp.int32)
    spread = (wanted[:, :, None] == block_ids[None, None, :]).astype(jnp.float32)
    dense_grad = jnp.einsum(
        "rsj,rsbf->rjbf", spread, slot_grad, precision=lax.Precision.HIGHEST
    ).reshape(shards * tok_rows, latent_width)
    own_sum = lax.psum_scatter(dense_grad, "ctx", scatter_dimension=0, tiled=True)
    grad_latent = lax.psum(own_sum + own_grad, "head")
    return (attended, grad_queries, grad_latent)


def solution(mesh):
    placed = (P("ctx", "head", None), P("ctx", None), P("ctx", "head", None), P("ctx", None))
    return jax.shard_map(
        body,
        mesh=mesh,
        in_specs=placed,
        out_specs=(P("ctx", "head", None), P("ctx", "head", None), P("ctx", None)),
        check_vma=False,
    )
```

profile of v0, /device:TPU:0, one launch (start us, length us, event | category | flops | bytes accessed | tf_op | source)
XLA Modules:
  0.0 232.9 jit_solution(11640080513266951641)
XLA Ops:
  7.2 1.7 copy.58
  9.0 0.7 fusion.10
  9.9 0.4 reduce_or.29
  10.6 4.9 %copy.61 = bf16[128,16,576]{2,1,0:T(8,128)(2,1)} copy(bf16[128,16,576]{0,2,1:T(8,128)(2,1)} %param.6) | data formatting | bytes 4718592
  15.6 40.0 %all-gather.2.cloned.1.call-done = bf16[1024,576]{1,0:T(8,128)(2,1)} async-done(((bf16[128,576]{1,0:T(8,128)(2,1)}), bf16[1024,576]{1,0:T(8,128)(2,1)}) %all-gather.2.cloned.1.call-update) | async-done | bytes 1179664 | tf_op jit(solution)/shard_map/all_gather | solution.py:63
  55.5 2.1 gather_fusion
  57.7 1.3 broadcast_select_fusion
  59.0 53.1 %while.19 = (s32[]{:T(128)}, f32[128,576]{0,1:T(8,128)S(1)}, bf16[2,64,16,512]{3,2,1,0:T(8,128)(2,1)}, bf16[2,64,16,576]{3,2,1,0:T(8,128)(2,1)}, f32[2,8,64,576]...) while((s32[]{:T(128)}, f32[128,576]{0,1:T(8,128)S(1)}, ...), condition=%wide.region_8.9_spmd.clone, body=%wide.region_4.8_spmd.clone.sunk | while | flops 4296701952 | bytes 91184016 | solution.py:94
  59.0 0.6 dynamic_slice.66
  62.3 0.1 broadcast_in_dim.135
  62.5 0.2 reshape.146
  62.6 0.2 broadcast_in_dim.136
  62.8 0.8 copy.78
  63.6 1.2 constant_dynamic-slice_fusion.14
  64.7 1.3 constant_dynamic-slice_fusion.10
  66.0 1.4 constant_dynamic-slice_fusion.13
  67.5 1.3 fusion.40
  68.8 0.4 exponential_reduce_fusion.2
  69.2 1.1 multiply_reduce_fusion.2
  70.3 0.5 copy-done.4
  70.9 1.0 multiply_convert_fusion.2
  71.9 0.3 copy-done.5
  72.2 1.0 fusion.41
  73.3 1.2 pad_add_fusion.5
  74.5 2.3 convolution_convert_fusion.3
  76.8 1.7 copy.79
  78.5 1.3 slice.29
  79.8 1.7 copy.80
  81.5 1.2 constant_dynamic-update-slice_fusion.8
  82.7 1.0 copy-done
  83.7 0.2 constant_dynamic-update-slice_fusion.7
  84.0 1.5 copy-done.1
  85.5 0.6 dynamic_slice.66
  88.9 0.1 broadcast_in_dim.135
  89.0 0.2 reshape.146
  89.2 0.2 broadcast_in_dim.136
  89.3 0.8 copy.78
  90.1 1.2 constant_dynamic-slice_fusion.14
  91.3 1.3 constant_dynamic-slice_fusion.10
  92.6 1.4 constant_dynamic-slice_fusion.13
  94.0 1.3 fusion.40
  95.3 0.4 exponential_reduce_fusion.2
  95.7 1.1 multiply_reduce_fusion.2
  96.9 0.5 copy-done.4
  97.5 1.0 multiply_convert_fusion.2
  98.5 0.3 copy-done.5
  98.8 1.0 fusion.41
  99.8 1.2 pad_add_fusion.5
  101.0 2.3 convolution_convert_fusion.3
  103.3 1.7 copy.79
  105.1 1.3 slice.29
  106.4 1.7 copy.80
  108.0 1.2 constant_dynamic-update-slice_fusion.8
  109.2 1.0 copy-done
  110.3 0.2 constant_dynamic-update-slice_fusion.7
  110.5 1.5 copy-done.1
  112.0 7.9 %fusion.8 = f32[8,2,64,576]{3,1,2,0:T(2,128)S(1)} fusion(f32[8,2,64,576]{3,2,0,1:T(8,128)} %bitcast.84, s32[8,2]{1,0:T(8,128)S(1)} %get-tuple-element.296), kind=kOutput, calls=%fused_computation.28 | convolution fusion | flops 14155808 | bytes 4718656 | tf_op jit(solution)/shard_map/rsj,rsbf->rjbf/dot_general | solution.py:102
  120.0 1.8 copy.64
  121.9 0.2 copy.65
  122.0 68.8 %reduce-scatter.2.cloned.1.call-done = f32[128,576]{1,0:T(8,128)} async-done(((f32[1024,576]{1,0:T(8,128)}), f32[128,576]{1,0:T(8,128)}) %reduce-scatter.2.cloned.1.call-update) | async-done | bytes 294928 | tf_op jit(solution)/shard_map/reduce_scatter | solution.py:105
  190.8 1.7 add.87
  192.6 3.1 %copy.66 = bf16[128,16,576]{0,2,1:T(8,128)(2,1)} copy(bf16[128,16,576]{2,1,0:T(8,128)(2,1)S(1)} %bitcast.83) | data formatting | bytes 4718592
  195.7 28.8 %all-reduce.3.cloned.1.call-done = f32[128,576]{1,0:T(8,128)} async-done(((f32[128,576]{1,0:T(8,128)}), f32[128,576]{1,0:T(8,128)}) %all-reduce.3.cloned.1.call-update) | async-done | bytes 294928 | tf_op jit(solution)/shard_map/psum | solution.py:106
  224.5 1.8 copy.67
  (51 shorter events, 1.5 us)
Async XLA Ops:
  7.2 48.4 %all-gather.2.cloned.1.call-start = ((), (), s32[]{:S(2)}) async-start(), calls=%async_computation.1 | async-start | bytes 1474560 | tf_op jit(solution)/shard_map/all_gather | solution.py:63
  8.9 181.9 %reduce-scatter.2.cloned.1.call-start = ((), (), s32[]{:S(2)}) async-start(), calls=%async_computation.2 | async-start | bytes 2949120 | tf_op jit(solution)/shard_map/reduce_scatter | solution.py:105
  55.5 3.4 %copy-start.3 = (bf16[128,576]{1,0:T(8,128)(2,1)S(1)}, bf16[128,576]{1,0:T(8,128)(2,1)}, u32[]{:S(2)}) copy-start(bf16[128,576]{1,0:T(8,128)(2,1)} %copy.58) | copy-start | bytes 442372
  69.2 1.6 copy-start.4
  70.9 1.3 copy-start.5
  81.5 2.2 copy-start
  83.9 1.5 copy-start.1
  95.7 1.6 copy-start.4
  97.4 1.3 copy-start.5
  108.0 2.2 copy-start
  110.5 1.5 copy-start.1
  121.8 70.8 %copy-start.2 = (bf16[2,64,16,576]{3,2,1,0:T(8,128)(2,1)S(1)}, bf16[2,64,16,576]{3,2,1,0:T(8,128)(2,1)}, u32[]{:S(2)}) copy-start(bf16[2,64,16,576]{3,2,1,0:T(8,128)(2,1)} %get-tuple-element.156) | copy-start | bytes 7077892
  121.8 102.7 %all-reduce.3.cloned.1.call-start = ((), (), s32[]{:S(2)}) async-start(), calls=%async_computation.3 | async-start | bytes 655360 | tf_op jit(solution)/shard_map/psum | solution.py:106
Sparse Core Ops, SparseCore 0:
  10.8 44.7 all-gather.1
  121.9 68.8 reduce-scatter.1
  193.2 31.3 all-reduce.2
where the time goes:
time: 234 us; the launch traced here: 233 us
  waiting for transfers between devices  138 us (59%)
  local copies, waits for them, and re-layouts  46.7 us (20%)
  matrix products  23.9 us (10%)
  between operations  13.8 us (6%)
  loops' own time  5.48 us (2%)
  other arithmetic  5.27 us (2%)
    reduce_scatter x1, waiting for transfers between devices, body(): lax.psum_scatter(dense_grad, 'ctx', scatter_dimension=0, tiled=True)  68.8 us
    all_gather x1, waiting for transfers between devices, body(): all_rows = lax.all_gather(latent, 'ctx', axis=0, tiled=True)  40 us
    psum x1, waiting for transfers between devices, body(): grad_latent = lax.psum(own_sum + own_grad, 'head')  28.8 us
    unnamed x9, local copies, waits for them, and re-layouts  11.7 us
    dot_general x1, matrix products, body(): jnp.einsum('rsj,rsbf->rjbf', spread, slot_grad, precision=lax.Precision.H...  7.94 us
    while x16, local copies, waits for them, and re-layouts  6.66 us
    slice x4, local copies, waits for them, and re-layouts, block_step(): grad_keys[tok_rows:].reshape(shards, BLOCK, latent_width)  5.91 us
    another operation x1, loops' own time, body(): lax.scan(block_step, zeros_init, jnp.arange(blocks_here, dtype=jnp.int32))  5.48 us
  transfers between devices with their start and end apart: 3, of which 3 were waited for; matrix products, arithmetic and copies ran while one was open for 4% of the time, Pallas kernels for 0%

commit v1 on v0

v1 whole, which is shorter than its diff:
```python
import functools

import jax
import jax.numpy as jnp
from jax import lax
from jax.experimental import pallas as pl
from jax.experimental.pallas import tpu as pltpu
from jax.sharding import PartitionSpec as P

BLOCK = 64
TILE_ROWS = 512
MASKED = -1e30

softmax_scale = 192.0 ** (-0.5)

NT = (((1,), (1,)), ((), ()))
TN = (((0,), (0,)), ((), ()))


def dot(a, b, dims):
    return lax.dot_general(a, b, dims, preferred_element_type=jnp.float32)


def attention_kernel(n_far, blocks_here, heads, want_ref, q_ref, g_ref, own_ref, bias_ref, *rest):
    near = rest[:n_far]
    pair = rest[n_far : 2 * n_far]
    att_ref, gq_ref, keep_ref, send_ref, own_grad_ref = rest[2 * n_far : 2 * n_far + 5]
    scratch = rest[2 * n_far + 5 :]
    keys = scratch[:blocks_here]
    accs = scratch[blocks_here : 2 * blocks_here]
    dense_ref = scratch[2 * blocks_here]
    step = pl.program_id(0)
    steps = pl.num_programs(0)
    tile_rows = q_ref.shape[0]
    value_width = g_ref.shape[1]
    tiles_per_block = BLOCK * heads // tile_rows
    half = blocks_here // 2 * BLOCK
    far_rows = n_far * BLOCK
    my_half = want_ref[blocks_here, 0]

    @pl.when(step == 0)
    def _():
        for b in range(blocks_here):
            for k in range(n_far):
                block = want_ref[b, k]
                if half == BLOCK:
                    mine, other = near[k][...], pair[k][...]
                    side = block
                else:
                    offset = pl.multiple_of(lax.rem(block * BLOCK, half), BLOCK)
                    mine, other = near[k][pl.ds(offset, BLOCK), :], pair[k][pl.ds(offset, BLOCK), :]
                    side = lax.div(block * BLOCK, half)
                keys[b][k * BLOCK : (k + 1) * BLOCK, :] = jnp.where(side == my_half, mine, other)
            keys[b][far_rows:, :] = own_ref[: (b + 1) * BLOCK, :]
            accs[b][...] = jnp.zeros_like(accs[b])

    def tile(b):
        slots = n_far + b + 1
        query, grad = q_ref[...], g_ref[...]
        scores = dot(keys[b][...], query, NT) * softmax_scale
        scores = scores.reshape(slots, BLOCK, tile_rows) + bias_ref[:slots, :][:, None, :]
        first = lax.rem(step, tiles_per_block) * (tile_rows // heads)
        token = first + lax.div(lax.broadcasted_iota(jnp.int32, (1, BLOCK, tile_rows), 2), heads)
        place = lax.broadcasted_iota(jnp.int32, (1, BLOCK, tile_rows), 1)
        last = jnp.where(place <= token, scores[slots - 1 :], MASKED)
        scores = jnp.concatenate([scores[: slots - 1], last], axis=0).reshape(slots * BLOCK, tile_rows)
        top = jnp.max(scores, axis=0, keepdims=True)
        raised = jnp.exp(scores - top)
        total = jnp.sum(raised, axis=0, keepdims=True)
        grad_weights = dot(keys[b][:, :value_width], grad, NT)
        inverse = 1.0 / total
        weights = raised * inverse
        row_delta = jnp.sum(weights * grad_weights, axis=0, keepdims=True)
        grad_scores = (softmax_scale * weights * (grad_weights - row_delta)).astype(jnp.bfloat16)
        weights_low = weights.astype(jnp.bfloat16)
        accs[b][...] += dot(grad_scores, query, (((1,), (0,)), ((), ())))
        accs[b][:, :value_width] += dot(weights_low, grad, (((1,), (0,)), ((), ())))
        att_ref[...] = dot(weights_low, keys[b][:, :value_width], TN).astype(att_ref.dtype)
        gq_ref[...] = dot(grad_scores, keys[b][...], TN).astype(gq_ref.dtype)

    for b in range(blocks_here):
        pl.when(lax.div(step, tiles_per_block) == b)(functools.partial(tile, b))

    @pl.when(step == steps - 1)
    def _():
        dense_ref[...] = jnp.zeros_like(dense_ref)
        for b in range(blocks_here):
            for k in range(n_far):
                offset = pl.multiple_of(want_ref[b, k] * BLOCK, BLOCK)
                dense_ref[k, pl.ds(offset, BLOCK), :] += accs[b][k * BLOCK : (k + 1) * BLOCK, :]
        mine = pl.multiple_of(my_half * half, half)
        other = pl.multiple_of((1 - my_half) * half, half)
        for k in range(n_far):
            keep_ref[k, :, :] = dense_ref[k, pl.ds(mine, half), :].astype(keep_ref.dtype)
            send_ref[k, :, :] = dense_ref[k, pl.ds(other, half), :].astype(send_ref.dtype)
        for j in range(blocks_here):
            part = accs[j][far_rows + j * BLOCK : far_rows + (j + 1) * BLOCK, :]
            for b in range(j + 1, blocks_here):
                part = part + accs[b][far_rows + j * BLOCK : far_rows + (j + 1) * BLOCK, :]
            own_grad_ref[j * BLOCK : (j + 1) * BLOCK, :] = part


def attention(want, query_rows, grad_rows, own, bias, near, pair, heads, blocks_here):
    n_far = len(near)
    rows, latent_width = query_rows.shape
    value_width = grad_rows.shape[1]
    half = own.shape[0] // 2
    tile_rows = min(TILE_ROWS, BLOCK * heads)
    whole = lambda shape: pl.BlockSpec(shape, lambda i: (0,) * len(shape))
    by_tile = lambda width: pl.BlockSpec((tile_rows, width), lambda i: (i, 0))
    in_specs = [
        pl.BlockSpec(memory_space=pltpu.SMEM),
        by_tile(latent_width),
        by_tile(value_width),
        whole(own.shape),
        pl.BlockSpec((bias.shape[0], tile_rows), lambda i: (0, i)),
    ] + [whole((half, latent_width))] * (2 * n_far)
    out_shape = (
        jax.ShapeDtypeStruct((rows, value_width), jnp.bfloat16),
        jax.ShapeDtypeStruct((rows, latent_width), jnp.bfloat16),
        jax.ShapeDtypeStruct((n_far, half, latent_width), jnp.bfloat16),
        jax.ShapeDtypeStruct((n_far, half, latent_width), jnp.bfloat16),
        jax.ShapeDtypeStruct(own.shape, jnp.float32),
    )
    out_specs = (
        by_tile(value_width),
        by_tile(latent_width),
        whole((n_far, half, latent_width)),
        whole((n_far, half, latent_width)),
        whole(own.shape),
    )
    key_counts = [(n_far + b + 1) * BLOCK for b in range(blocks_here)]
    scratch = [pltpu.VMEM((count, latent_width), jnp.bfloat16) for count in key_counts]
    scratch += [pltpu.VMEM((count, latent_width), jnp.float32) for count in key_counts]
    scratch += [pltpu.VMEM((n_far, own.shape[0], latent_width), jnp.float32)]
    macs = rows * key_counts[-1] * 3 * (latent_width + value_width)
    return pl.pallas_call(
        functools.partial(attention_kernel, n_far, blocks_here, heads),
        grid=(rows // tile_rows,),
        in_specs=in_specs,
        out_specs=out_specs,
        out_shape=out_shape,
        scratch_shapes=scratch,
        compiler_params=pltpu.CompilerParams(vmem_limit_bytes=56 * 1024 * 1024),
        cost_estimate=pl.CostEstimate(
            flops=2 * macs,
            bytes_accessed=4 * rows * (latent_width + value_width),
            transcendentals=rows * key_counts[-1],
        ),
        name="attention",
    )(want, query_rows, grad_rows, own, bias, *near, *pair)


def slot_table(chosen, my_shard, shards, blocks_here):
    tok_rows = chosen.shape[0]
    valid = chosen >= 0
    owner = jnp.where(valid, chosen // blocks_here, -1)
    inside = jnp.where(valid, chosen % blocks_here, 0)
    target = my_shard - 1 - jnp.arange(shards - 1, dtype=jnp.int32)
    hit = (owner[None] == target[:, None, None]) & valid[None]
    far = jnp.any(hit, axis=2)
    want = jnp.max(
        jnp.where(hit, inside[None], 0).reshape(shards - 1, blocks_here, -1), axis=2
    ).T
    local = my_shard * blocks_here + jnp.arange(blocks_here, dtype=jnp.int32)
    near = jnp.any(chosen[None] == local[:, None, None], axis=2)
    allowed = jnp.concatenate([far, near], axis=0)
    return jnp.where(allowed, 0.0, MASKED).astype(jnp.float32), want.astype(jnp.int32)


def body(queries, latent, cotangent, selection):
    tok_rows, heads, latent_width = queries.shape
    value_width = cotangent.shape[2]
    shards = lax.axis_size("ctx")
    groups = lax.axis_size("head")
    my_shard = lax.axis_index("ctx")
    my_half = lax.axis_index("head") % 2
    blocks_here = tok_rows // BLOCK
    half = tok_rows // 2
    partner = [(i, i ^ 1) for i in range(groups)]

    part = lax.dynamic_slice_in_dim(latent, my_half * half, half, 0)
    near = [
        lax.ppermute(part, "ctx", [(i, i + k) for i in range(shards - k)]) for k in range(1, shards)
    ]
    pair = [lax.ppermute(rows, "head", partner) for rows in near]

    bias, want = slot_table(selection, my_shard, shards, blocks_here)
    bias = jnp.repeat(bias, heads, axis=1)
    want = jnp.concatenate([want, jnp.full((1, shards - 1), my_half, jnp.int32)], axis=0)
    attended, grad_queries, keep, send, own_grad = attention(
        want,
        queries.reshape(tok_rows * heads, latent_width),
        cotangent.reshape(tok_rows * heads, value_width),
        latent,
        bias,
        near,
        pair,
        heads,
        blocks_here,
    )

    got = lax.ppermute(send, "head", partner)
    own_keep = lax.dynamic_slice_in_dim(own_grad, my_half * half, half, 0)
    own_send = lax.dynamic_slice_in_dim(own_grad, (1 - my_half) * half, half, 0)
    total = own_keep + lax.ppermute(own_send, "head", partner)
    for k in range(1, shards):
        summed = (keep[k - 1].astype(jnp.float32) + got[k - 1].astype(jnp.float32)).astype(jnp.bfloat16)
        moved = lax.ppermute(summed, "ctx", [(i + k, i) for i in range(shards - k)])
        total = total + moved.astype(jnp.float32)
    low = total.astype(jnp.bfloat16)
    summed = low.astype(jnp.float32)
    for j in range(1, groups // 2):
        moved = lax.ppermute(low, "head", [(i, (i + 2 * j) % groups) for i in range(groups)])
        summed = summed + moved.astype(jnp.float32)
    other = lax.ppermute(summed, "head", partner)
    grad_latent = jnp.where(
        my_half == 0,
        jnp.concatenate([summed, other], axis=0),
        jnp.concatenate([other, summed], axis=0),
    )
    return (
        attended.reshape(tok_rows, heads, value_width),
        grad_queries.reshape(tok_rows, heads, latent_width),
        grad_latent,
    )


def solution(mesh):
    placed = (P("ctx", "head", None), P("ctx", None), P("ctx", "head", None), P("ctx", None))
    return jax.shard_map(
        body,
        mesh=mesh,
        in_specs=placed,
        out_specs=(P("ctx", "head", None), P("ctx", "head", None), P("ctx", None)),
        check_vma=False,
    )
```

time: 234 us -> 89.5 us (0.38)
  waiting for transfers between devices: 138 us -> 22 us
  local copies, waits for them, and re-layouts: 46.7 us -> 14.4 us
  starting transfers between devices: 0.12 us -> 30.3 us
  matrix products: 23.9 us -> 0 us
  Pallas kernels: 0 us -> 16.2 us
  between operations: 13.8 us -> 1.09 us
  loops' own time: 5.48 us -> 0 us
    reduce_scatter x1 -> x0, waiting for transfers between devices: 68.8 us -> none  [body(): lax.psum_scatter(dense_grad, 'ctx', scatter_dimension=0, tiled=True)]
    all_gather x1 -> x0, waiting for transfers between devices: 40 us -> none  [body(): all_rows = lax.all_gather(latent, 'ctx', axis=0, tiled=True)]
    ppermute x0 -> x25, starting transfers between devices: none -> 30.3 us  [the longest x7 17.3 us: body(): lax.ppermute(part, 'ctx', [(i, i + k) for i in range(shards - k)])]
    psum x1 -> x0, waiting for transfers between devices: 28.8 us -> none  [body(): grad_latent = lax.psum(own_sum + own_grad, 'head')]
    dot_general x13 -> x0, matrix products: 23.9 us -> none  [the longest x1 7.94 us: body(): jnp.einsum('rsj,rsbf->rjbf', spread, slot_grad, precision=lax.Precision.H...]
    ppermute x0 -> x25, waiting for transfers between devices: none -> 22 us  [the longest x7 18.4 us: body(): moved = lax.ppermute(summed, 'ctx', [(i + k, i) for i in range(shards - k)])]
    pallas_call x0 -> x1, Pallas kernels: none -> 16.2 us  [attention(): pl.pallas_call(functools.partial(attention_kernel, n_far, blocks_here, he...]
    dynamic_slice x14 -> x2, local copies, waits for them, and re-layouts: 9.32 us -> 1.18 us  [the longest x1 1.17 us: body(): own_send = lax.dynamic_slice_in_dim(own_grad, (1 - my_half) * half, half, 0)]
  transfers between devices with their start and end apart: 3 -> 25, of which waited for: 3 -> 8; matrix products, arithmetic and copies ran while one was open for 4% -> 17% of each run, Pallas kernels for 0% -> 0%
where the time goes in v1:
time: 89.5 us; the launch traced here: 88.8 us
  starting transfers between devices  30.3 us (34%)
  waiting for transfers between devices  22 us (25%)
  Pallas kernels  16.2 us (18%)
  local copies, waits for them, and re-layouts  14.4 us (16%)
  other arithmetic  4.88 us (5%)
  between operations  1.09 us (1%)
    ppermute x7, waiting for transfers between devices, body(): moved = lax.ppermute(summed, 'ctx', [(i + k, i) for i in range(shards - k)])  18.4 us
    ppermute x7, starting transfers between devices, body(): lax.ppermute(part, 'ctx', [(i, i + k) for i in range(shards - k)])  17.3 us
    pallas_call x1, Pallas kernels, attention(): pl.pallas_call(functools.partial(attention_kernel, n_far, blocks_here, he...  16.2 us
    unnamed x36, local copies, waits for them, and re-layouts  10.6 us
    ppermute x7, starting transfers between devices, body(): moved = lax.ppermute(summed, 'ctx', [(i + k, i) for i in range(shards - k)])  9.02 us
    ppermute x1, waiting for transfers between devices, body(): lax.ppermute(low, 'head', [(i, (i + 2 * j) % groups) for i in range(group...  2.93 us
  transfers between devices with their start and end apart: 25, of which 8 were waited for; matrix products, arithmetic and copies ran while one was open for 17% of the time, Pallas kernels for 0%

profile of v1, /device:TPU:0, one launch (start us, length us, event | category | flops | bytes accessed | tf_op | source)
XLA Modules:
  0.0 88.8 jit_solution(7782362246521726621)
XLA Ops:
  0.6 1.1 %copy.32.own_ref = bf16[128,576]{1,0:T(8,128)(2,1)S(1)} copy(bf16[128,576]{0,1:T(8,128)(2,1)} %param.5) | data formatting | bytes 294912 | tf_op args[1]
  1.7 0.0 copy-start.1
  1.7 5.9 %collective-permute-start.3 = (bf16[64,576]{1,0:T(8,128)(2,1)S(1)}, bf16[64,576]{1,0:T(8,128)(2,1)S(1)}, u32[]{:S(2)}, u32[]{:S(2)}) collective-permute-start(bf16[64,576]{1,0:T(8,128)(2,1)S(1)} %constant_dynamic-slice_fusion.1), channel_id=1, source_target_pairs={{0,16},{4,20},{8,24},{12,28},{1,17},{5,21},{9,25},{13,29},{2,18},{... | collective-permute-start | bytes 221192 | tf_op jit(solution)/shard_map/ppermute | solution.py:184
  7.7 2.2 %collective-permute-start.4 = (bf16[64,576]{1,0:T(8,128)(2,1)S(1)}, bf16[64,576]{1,0:T(8,128)(2,1)S(1)}, u32[]{:S(2)}, u32[]{:S(2)}) collective-permute-start(bf16[64,576]{1,0:T(8,128)(2,1)S(1)} %constant_dynamic-slice_fusion.1), channel_id=1, source_target_pairs={{0,20},{4,24},{8,28},{1,21},{5,25},{9,29},{2,22},{6,26},{10,30},{3... | collective-permute-start | bytes 221192 | tf_op jit(solution)/shard_map/ppermute | solution.py:184
  9.9 1.4 %collective-permute-start.5 = (bf16[64,576]{1,0:T(8,128)(2,1)S(1)}, bf16[64,576]{1,0:T(8,128)(2,1)S(1)}, u32[]{:S(2)}, u32[]{:S(2)}) collective-permute-start(bf16[64,576]{1,0:T(8,128)(2,1)S(1)} %constant_dynamic-slice_fusion.1), channel_id=1, source_target_pairs={{0,24},{4,28},{1,25},{5,29},{2,26},{6,30},{3,27},{7,31}} | collective-permute-start | bytes 221192 | tf_op jit(solution)/shard_map/ppermute | solution.py:184
  11.3 2.2 %collective-permute-start.6 = (bf16[64,576]{1,0:T(8,128)(2,1)S(1)}, bf16[64,576]{1,0:T(8,128)(2,1)S(1)}, u32[]{:S(2)}, u32[]{:S(2)}) collective-permute-start(bf16[64,576]{1,0:T(8,128)(2,1)S(1)} %constant_dynamic-slice_fusion.1), channel_id=1, source_target_pairs={{0,28},{1,29},{2,30},{3,31}} | collective-permute-start | bytes 221192 | tf_op jit(solution)/shard_map/ppermute | solution.py:184
  13.5 1.8 %collective-permute-start = (bf16[64,576]{1,0:T(8,128)(2,1)S(1)}, bf16[64,576]{1,0:T(8,128)(2,1)S(1)}, u32[]{:S(2)}, u32[]{:S(2)}) collective-permute-start(bf16[64,576]{1,0:T(8,128)(2,1)S(1)} %constant_dynamic-slice_fusion.1), channel_id=1, source_target_pairs={{0,4},{4,8},{8,12},{12,16},{16,20},{20,24},{24,28},{1,5},{5,9},{9,... | collective-permute-start | bytes 221192 | tf_op jit(solution)/shard_map/ppermute | solution.py:184
  15.4 0.7 fusion.8
  16.1 0.7 broadcast_compare_fusion
  16.8 0.1 copy.26
  16.9 0.1 eq.42
  17.0 0.1 copy.28
  17.1 0.1 broadcast_in_dim.35
  17.2 0.1 copy.27
  17.3 0.1 and.33
  17.4 0.1 and_reduce_fusion
  17.5 0.3 fusion.7
  17.8 0.1 copy.29
  17.9 0.6 concatenate.12.want_ref
  18.5 0.0 collective-permute-done.3.rest_3_
  18.5 1.5 %collective-permute-start.1 = (bf16[64,576]{1,0:T(8,128)(2,1)S(1)}, bf16[64,576]{1,0:T(8,128)(2,1)S(1)}, u32[]{:S(2)}, u32[]{:S(2)}) collective-permute-start(bf16[64,576]{1,0:T(8,128)(2,1)S(1)} %constant_dynamic-slice_fusion.1), channel_id=1, source_target_pairs={{0,8},{4,12},{8,16},{12,20},{16,24},{20,28},{1,9},{5,13},{9,17},{1... | collective-permute-start | bytes 221192 | tf_op jit(solution)/shard_map/ppermute | solution.py:184
  20.0 0.0 collective-permute-done.4.rest_4_
  20.0 2.2 %collective-permute-start.2 = (bf16[64,576]{1,0:T(8,128)(2,1)S(1)}, bf16[64,576]{1,0:T(8,128)(2,1)S(1)}, u32[]{:S(2)}, u32[]{:S(2)}) collective-permute-start(bf16[64,576]{1,0:T(8,128)(2,1)S(1)} %constant_dynamic-slice_fusion.1), channel_id=1, source_target_pairs={{0,12},{4,16},{8,20},{12,24},{16,28},{1,13},{5,17},{9,21},{13,25},... | collective-permute-start | bytes 221192 | tf_op jit(solution)/shard_map/ppermute | solution.py:184
  22.3 0.1 collective-permute-start.10
  22.4 0.5 collective-permute-start.11
  22.9 0.8 compare_reduce_fusion
  23.7 0.2 collective-permute-start.12
  23.8 0.4 collective-permute-start.13
  24.3 0.1 collective-permute-done.2.rest_2_
  24.3 0.0 collective-permute-start.7
  24.4 0.5 collective-permute-start.8
  24.9 0.1 collective-permute-start.9
  24.9 0.2 broadcast_in_dim.40
  25.2 1.0 %reshape.70.bias_ref = f32[9,2048]{1,0:T(8,128)} reshape(f32[9,128,16]{2,1,0:T(8,128)S(1)} %broadcast_in_dim.40) | data formatting | bytes 147456 | tf_op jit(solution)/shard_map/reshape | solution.py:189
  26.2 4.9 %copy.30 = bf16[128,16,576]{2,1,0:T(8,128)(2,1)} copy(bf16[128,16,576]{0,2,1:T(8,128)(2,1)} %param.4) | data formatting | bytes 4718592 | tf_op args[0]
  31.2 0.5 copy-done.11
  31.8 0.0 copy-done.12
  31.8 0.0 copy-done.13
  31.8 0.0 copy-done.14
  31.8 0.1 copy-done.15
  31.9 16.2 %attention.1 = (bf16[2048,512]{1,0:T(8,128)(2,1)}, bf16[2048,576]{1,0:T(8,128)(2,1)}, bf16[7,64,576]{2,1,0:T(8,128)(2,1)}, bf16[7,64,576]{2,1,0:T(8,128)(2,1)}, f32[128,576]{1,0:T(8,128)}) custom-call(s32[3,7]{1,0:T(4,128)} %concatenate.12.want_ref, bf16[2048,576]{1,0:T(8,128)(2,1)} %bitcast.20, bf16[2048,512]{1,0:T(8,128)(2,1)} %bitcast.22, ...), custom_call_target="tpu_custom_call" | custom-call | flops 7700742144 | bytes 8912896 | tf_op jit(solution)/shard_map/attention/pallas_call | solution.py:137
  48.1 0.5 collective-permute-start.15
  48.6 1.2 %constant_dynamic-slice_fusion = f32[64,576]{1,0:T(8,128)S(1)} fusion(f32[128,576]{1,0:T(8,128)} %get-tuple-element.10, s32[]{:T(128)S(6)} %select_n.58), kind=kLoop, calls=%fused_computation.33 | loop fusion | bytes 294916 | tf_op jit(solution)/shard_map/dynamic_slice | solution.py:205
  49.7 0.1 collective-permute-start.14
  49.8 0.6 collective-permute-done.15
  50.4 1.3 %fusion = (bf16[64,576]{1,0:T(8,128)(2,1)S(1)}, bf16[64,576]{1,0:T(8,128)(2,1)S(1)}, bf16[64,576]{1,0:T(8,128)(2,1)S(1)}, bf16[64,576]{1,0:T(8,128)(2,1)S(1)}, b...) fusion(bf16[7,64,576]{2,1,0:T(8,128)(2,1)S(1)} %collective-permute-done.15, ...), kind=kLoop, calls=%fused_computation.10 | loop fusion | flops 1032192 | bytes 1548288 | tf_op jit(solution)/shard_map/convert_element_type | solution.py:208
  51.7 1.3 %collective-permute-start.16 = (bf16[64,576]{1,0:T(8,128)(2,1)S(1)}, bf16[64,576]{1,0:T(8,128)(2,1)S(1)}, u32[]{:S(2)}, u32[]{:S(2)}) collective-permute-start(bf16[64,576]{1,0:T(8,128)(2,1)S(1)} %get-tuple-element.22), channel_id=1, source_target_pairs={{4,0},{8,4},{12,8},{16,12},{20,16},{24,20},{28,24},{5,1},{9,5},{13... | collective-permute-start | bytes 221192 | tf_op jit(solution)/shard_map/ppermute | solution.py:209
  53.0 1.3 %collective-permute-start.17 = (bf16[64,576]{1,0:T(8,128)(2,1)S(1)}, bf16[64,576]{1,0:T(8,128)(2,1)S(1)}, u32[]{:S(2)}, u32[]{:S(2)}) collective-permute-start(bf16[64,576]{1,0:T(8,128)(2,1)S(1)} %get-tuple-element.28), channel_id=1, source_target_pairs={{8,0},{12,4},{16,8},{20,12},{24,16},{28,20},{9,1},{13,5},{17,9},{2... | collective-permute-start | bytes 221192 | tf_op jit(solution)/shard_map/ppermute | solution.py:209
  54.3 1.3 %collective-permute-start.18 = (bf16[64,576]{1,0:T(8,128)(2,1)S(1)}, bf16[64,576]{1,0:T(8,128)(2,1)S(1)}, u32[]{:S(2)}, u32[]{:S(2)}) collective-permute-start(bf16[64,576]{1,0:T(8,128)(2,1)S(1)} %get-tuple-element.27), channel_id=1, source_target_pairs={{12,0},{16,4},{20,8},{24,12},{28,16},{13,1},{17,5},{21,9},{25,13},... | collective-permute-start | bytes 221192 | tf_op jit(solution)/shard_map/ppermute | solution.py:209
  55.6 1.3 %collective-permute-start.19 = (bf16[64,576]{1,0:T(8,128)(2,1)S(1)}, bf16[64,576]{1,0:T(8,128)(2,1)S(1)}, u32[]{:S(2)}, u32[]{:S(2)}) collective-permute-start(bf16[64,576]{1,0:T(8,128)(2,1)S(1)} %get-tuple-element.26), channel_id=1, source_target_pairs={{16,0},{20,4},{24,8},{28,12},{17,1},{21,5},{25,9},{29,13},{18,2},{... | collective-permute-start | bytes 221192 | tf_op jit(solution)/shard_map/ppermute | solution.py:209
  56.9 1.3 %collective-permute-start.20 = (bf16[64,576]{1,0:T(8,128)(2,1)S(1)}, bf16[64,576]{1,0:T(8,128)(2,1)S(1)}, u32[]{:S(2)}, u32[]{:S(2)}) collective-permute-start(bf16[64,576]{1,0:T(8,128)(2,1)S(1)} %get-tuple-element.25), channel_id=1, source_target_pairs={{20,0},{24,4},{28,8},{21,1},{25,5},{29,9},{22,2},{26,6},{30,10},{2... | collective-permute-start | bytes 221192 | tf_op jit(solution)/shard_map/ppermute | solution.py:209
  58.2 2.9 %collective-permute-done.16 = bf16[64,576]{1,0:T(8,128)(2,1)S(1)} collective-permute-done((bf16[64,576]{1,0:T(8,128)(2,1)S(1)}, bf16[64,576]{1,0:T(8,128)(2,1)S(1)}, u32[]{:S(2)}, u32[]{:S(2)}) %collective-permute-start.16) | collective-permute-done | bytes 73760 | tf_op jit(solution)/shard_map/ppermute | solution.py:209
  61.1 1.3 %collective-permute-start.21 = (bf16[64,576]{1,0:T(8,128)(2,1)S(1)}, bf16[64,576]{1,0:T(8,128)(2,1)S(1)}, u32[]{:S(2)}, u32[]{:S(2)}) collective-permute-start(bf16[64,576]{1,0:T(8,128)(2,1)S(1)} %get-tuple-element.24), channel_id=1, source_target_pairs={{24,0},{28,4},{25,1},{29,5},{26,2},{30,6},{27,3},{31,7}} | collective-permute-start | bytes 221192 | tf_op jit(solution)/shard_map/ppermute | solution.py:209
  62.3 1.8 %collective-permute-done.17 = bf16[64,576]{1,0:T(8,128)(2,1)S(1)} collective-permute-done((bf16[64,576]{1,0:T(8,128)(2,1)S(1)}, bf16[64,576]{1,0:T(8,128)(2,1)S(1)}, u32[]{:S(2)}, u32[]{:S(2)}) %collective-permute-start.17) | collective-permute-done | bytes 73760 | tf_op jit(solution)/shard_map/ppermute | solution.py:209
  64.2 1.3 %collective-permute-start.22 = (bf16[64,576]{1,0:T(8,128)(2,1)S(1)}, bf16[64,576]{1,0:T(8,128)(2,1)S(1)}, u32[]{:S(2)}, u32[]{:S(2)}) collective-permute-start(bf16[64,576]{1,0:T(8,128)(2,1)S(1)} %get-tuple-element.23), channel_id=1, source_target_pairs={{28,0},{29,1},{30,2},{31,3}} | collective-permute-start | bytes 221192 | tf_op jit(solution)/shard_map/ppermute | solution.py:209
  65.4 0.6 collective-permute-done.18
  66.1 10.3 %collective-permute-done.19 = bf16[64,576]{1,0:T(8,128)(2,1)S(1)} collective-permute-done((bf16[64,576]{1,0:T(8,128)(2,1)S(1)}, bf16[64,576]{1,0:T(8,128)(2,1)S(1)}, u32[]{:S(2)}, u32[]{:S(2)}) %collective-permute-start.19) | collective-permute-done | bytes 73760 | tf_op jit(solution)/shard_map/ppermute | solution.py:209
  76.4 2.8 %collective-permute-done.20 = bf16[64,576]{1,0:T(8,128)(2,1)S(1)} collective-permute-done((bf16[64,576]{1,0:T(8,128)(2,1)S(1)}, bf16[64,576]{1,0:T(8,128)(2,1)S(1)}, u32[]{:S(2)}, u32[]{:S(2)}) %collective-permute-start.20) | collective-permute-done | bytes 73760 | tf_op jit(solution)/shard_map/ppermute | solution.py:209
  79.2 1.0 %add_convert_fusion = bf16[64,576]{1,0:T(8,128)(2,1)S(1)} fusion(bf16[64,576]{1,0:T(8,128)(2,1)S(1)} %collective-permute-done.22, bf16[64,576]{1,0:T(8,128)(2,1)S(1)} %collective-permute-done.21, bf16[64,576]{1,0:T(8,128)(2,1)S(1)} %collective-permute-done.20, bf16[64,576]{1,0:T(8,128)(2,1)S(1)} %collective-permute-done.19, ...), kind=kLoop, calls=%fused_computation.2 | loop fusion | flops 589824 | bytes 884740 | tf_op jit(solution)/shard_map/convert_element_type | solution.py:211
  80.2 1.6 %collective-permute-start.23 = (bf16[64,576]{1,0:T(8,128)(2,1)S(1)}, bf16[64,576]{1,0:T(8,128)(2,1)S(1)}, u32[]{:S(2)}, u32[]{:S(2)}) collective-permute-start(bf16[64,576]{1,0:T(8,128)(2,1)S(1)} %add_convert_fusion), channel_id=1, source_target_pairs={{0,2},{1,3},{2,0},{3,1},{4,6},{5,7},{6,4},{7,5},{8,10},{9,11},{10,... | collective-permute-start | bytes 221192 | tf_op jit(solution)/shard_map/ppermute | solution.py:214
  81.8 2.9 %collective-permute-done.23 = bf16[64,576]{1,0:T(8,128)(2,1)S(1)} collective-permute-done((bf16[64,576]{1,0:T(8,128)(2,1)S(1)}, bf16[64,576]{1,0:T(8,128)(2,1)S(1)}, u32[]{:S(2)}, u32[]{:S(2)}) %collective-permute-start.23) | collective-permute-done | bytes 73760 | tf_op jit(solution)/shard_map/ppermute | solution.py:214
  84.7 0.1 collective-permute-start.24
  84.8 3.1 %copy.33 = bf16[128,16,576]{0,2,1:T(8,128)(2,1)} copy(bf16[128,16,576]{2,1,0:T(8,128)(2,1)S(1)} %bitcast.19) | data formatting | bytes 4718592
  88.0 0.9 copy.34
  (47 shorter events, 0.2 us)
Async XLA Ops:
  1.7 29.3 %copy-start.1 = (bf16[128,576]{1,0:T(8,128)(2,1)}, bf16[128,576]{1,0:T(8,128)(2,1)S(1)}, u32[]{:S(2)}) copy-start(bf16[128,576]{1,0:T(8,128)(2,1)S(1)} %copy.32.own_ref) | copy-start | bytes 442372
  1.7 16.8 %collective-permute-start.3 = (bf16[64,576]{1,0:T(8,128)(2,1)S(1)}, bf16[64,576]{1,0:T(8,128)(2,1)S(1)}, u32[]{:S(2)}, u32[]{:S(2)}) collective-permute-start(bf16[64,576]{1,0:T(8,128)(2,1)S(1)} %constant_dynamic-slice_fusion.1), channel_id=1, source_target_pairs={{0,16},{4,20},{8,24},{12,28},{1,17},{5,21},{9,25},{13,29},{2,18},{... | collective-permute-start | bytes 221192 | tf_op jit(solution)/shard_map/ppermute | solution.py:184
  7.7 12.3 %collective-permute-start.4 = (bf16[64,576]{1,0:T(8,128)(2,1)S(1)}, bf16[64,576]{1,0:T(8,128)(2,1)S(1)}, u32[]{:S(2)}, u32[]{:S(2)}) collective-permute-start(bf16[64,576]{1,0:T(8,128)(2,1)S(1)} %constant_dynamic-slice_fusion.1), channel_id=1, source_target_pairs={{0,20},{4,24},{8,28},{1,21},{5,25},{9,29},{2,22},{6,26},{10,30},{3... | collective-permute-start | bytes 221192 | tf_op jit(solution)/shard_map/ppermute | solution.py:184
  9.9 12.4 %collective-permute-start.5 = (bf16[64,576]{1,0:T(8,128)(2,1)S(1)}, bf16[64,576]{1,0:T(8,128)(2,1)S(1)}, u32[]{:S(2)}, u32[]{:S(2)}) collective-permute-start(bf16[64,576]{1,0:T(8,128)(2,1)S(1)} %constant_dynamic-slice_fusion.1), channel_id=1, source_target_pairs={{0,24},{4,28},{1,25},{5,29},{2,26},{6,30},{3,27},{7,31}} | collective-permute-start | bytes 221192 | tf_op jit(solution)/shard_map/ppermute | solution.py:184
  11.3 11.1 %collective-permute-start.6 = (bf16[64,576]{1,0:T(8,128)(2,1)S(1)}, bf16[64,576]{1,0:T(8,128)(2,1)S(1)}, u32[]{:S(2)}, u32[]{:S(2)}) collective-permute-start(bf16[64,576]{1,0:T(8,128)(2,1)S(1)} %constant_dynamic-slice_fusion.1), channel_id=1, source_target_pairs={{0,28},{1,29},{2,30},{3,31}} | collective-permute-start | bytes 221192 | tf_op jit(solution)/shard_map/ppermute | solution.py:184
  13.5 10.1 %collective-permute-start = (bf16[64,576]{1,0:T(8,128)(2,1)S(1)}, bf16[64,576]{1,0:T(8,128)(2,1)S(1)}, u32[]{:S(2)}, u32[]{:S(2)}) collective-permute-start(bf16[64,576]{1,0:T(8,128)(2,1)S(1)} %constant_dynamic-slice_fusion.1), channel_id=1, source_target_pairs={{0,4},{4,8},{8,12},{12,16},{16,20},{20,24},{24,28},{1,5},{5,9},{9,... | collective-permute-start | bytes 221192 | tf_op jit(solution)/shard_map/ppermute | solution.py:184
  18.5 12.5 %copy-start.2 = (bf16[64,576]{1,0:T(8,128)(2,1)}, bf16[64,576]{1,0:T(8,128)(2,1)S(1)}, u32[]{:S(2)}) copy-start(bf16[64,576]{1,0:T(8,128)(2,1)S(1)} %collective-permute-done.3.rest_3_) | copy-start | bytes 221188
  18.5 5.3 %collective-permute-start.1 = (bf16[64,576]{1,0:T(8,128)(2,1)S(1)}, bf16[64,576]{1,0:T(8,128)(2,1)S(1)}, u32[]{:S(2)}, u32[]{:S(2)}) collective-permute-start(bf16[64,576]{1,0:T(8,128)(2,1)S(1)} %constant_dynamic-slice_fusion.1), channel_id=1, source_target_pairs={{0,8},{4,12},{8,16},{12,20},{16,24},{20,28},{1,9},{5,13},{9,17},{1... | collective-permute-start | bytes 221192 | tf_op jit(solution)/shard_map/ppermute | solution.py:184
  20.0 11.0 %copy-start.3 = (bf16[64,576]{1,0:T(8,128)(2,1)}, bf16[64,576]{1,0:T(8,128)(2,1)S(1)}, u32[]{:S(2)}) copy-start(bf16[64,576]{1,0:T(8,128)(2,1)S(1)} %collective-permute-done.4.rest_4_) | copy-start | bytes 221188
  20.0 4.3 %collective-permute-start.2 = (bf16[64,576]{1,0:T(8,128)(2,1)S(1)}, bf16[64,576]{1,0:T(8,128)(2,1)S(1)}, u32[]{:S(2)}, u32[]{:S(2)}) collective-permute-start(bf16[64,576]{1,0:T(8,128)(2,1)S(1)} %constant_dynamic-slice_fusion.1), channel_id=1, source_target_pairs={{0,12},{4,16},{8,20},{12,24},{16,28},{1,13},{5,17},{9,21},{13,25},... | collective-permute-start | bytes 221192 | tf_op jit(solution)/shard_map/ppermute | solution.py:184
  22.3 8.8 %copy-start.4 = (bf16[64,576]{1,0:T(8,128)(2,1)}, bf16[64,576]{1,0:T(8,128)(2,1)S(1)}, u32[]{:S(2)}) copy-start(bf16[64,576]{1,0:T(8,128)(2,1)S(1)} %collective-permute-done.5.rest_5_) | copy-start | bytes 221188
  22.3 2.1 %collective-permute-start.10 = (bf16[64,576]{1,0:T(8,128)(2,1)S(1)}, bf16[64,576]{1,0:T(8,128)(2,1)S(1)}, u32[]{:S(2)}, u32[]{:S(2)}) collective-permute-start(bf16[64,576]{1,0:T(8,128)(2,1)S(1)} %collective-permute-done.3.rest_3_), channel_id=1, source_target_pairs={{0,1},{1,0},{2,3},{3,2},{4,5},{5,4},{6,7},{7,6},{8,9},{9,8},{10,11... | collective-permute-start | bytes 221192 | tf_op jit(solution)/shard_map/ppermute | solution.py:186
  22.4 8.7 %copy-start.5 = (bf16[64,576]{1,0:T(8,128)(2,1)}, bf16[64,576]{1,0:T(8,128)(2,1)S(1)}, u32[]{:S(2)}) copy-start(bf16[64,576]{1,0:T(8,128)(2,1)S(1)} %collective-permute-done.6.rest_6_) | copy-start | bytes 221188
  22.4 2.4 %collective-permute-start.11 = (bf16[64,576]{1,0:T(8,128)(2,1)S(1)}, bf16[64,576]{1,0:T(8,128)(2,1)S(1)}, u32[]{:S(2)}, u32[]{:S(2)}) collective-permute-start(bf16[64,576]{1,0:T(8,128)(2,1)S(1)} %collective-permute-done.4.rest_4_), channel_id=1, source_target_pairs={{0,1},{1,0},{2,3},{3,2},{4,5},{5,4},{6,7},{7,6},{8,9},{9,8},{10,11... | collective-permute-start | bytes 221192 | tf_op jit(solution)/shard_map/ppermute | solution.py:186
  23.7 7.4 %copy-start.6 = (bf16[64,576]{1,0:T(8,128)(2,1)}, bf16[64,576]{1,0:T(8,128)(2,1)S(1)}, u32[]{:S(2)}) copy-start(bf16[64,576]{1,0:T(8,128)(2,1)S(1)} %collective-permute-done.rest_0_) | copy-start | bytes 221188
  23.7 7.4 %collective-permute-start.12 = (bf16[64,576]{1,0:T(8,128)(2,1)S(1)}, bf16[64,576]{1,0:T(8,128)(2,1)S(1)}, u32[]{:S(2)}, u32[]{:S(2)}) collective-permute-start(bf16[64,576]{1,0:T(8,128)(2,1)S(1)} %collective-permute-done.5.rest_5_), channel_id=1, source_target_pairs={{0,1},{1,0},{2,3},{3,2},{4,5},{5,4},{6,7},{7,6},{8,9},{9,8},{10,11... | collective-permute-start | bytes 221192 | tf_op jit(solution)/shard_map/ppermute | solution.py:186
  23.8 7.2 %copy-start.7 = (bf16[64,576]{1,0:T(8,128)(2,1)}, bf16[64,576]{1,0:T(8,128)(2,1)S(1)}, u32[]{:S(2)}) copy-start(bf16[64,576]{1,0:T(8,128)(2,1)S(1)} %collective-permute-done.1.rest_1_) | copy-start | bytes 221188
  23.8 7.3 %collective-permute-start.13 = (bf16[64,576]{1,0:T(8,128)(2,1)S(1)}, bf16[64,576]{1,0:T(8,128)(2,1)S(1)}, u32[]{:S(2)}, u32[]{:S(2)}) collective-permute-start(bf16[64,576]{1,0:T(8,128)(2,1)S(1)} %collective-permute-done.6.rest_6_), channel_id=1, source_target_pairs={{0,1},{1,0},{2,3},{3,2},{4,5},{5,4},{6,7},{7,6},{8,9},{9,8},{10,11... | collective-permute-start | bytes 221192 | tf_op jit(solution)/shard_map/ppermute | solution.py:186
  24.3 6.8 %copy-start.8 = (bf16[64,576]{1,0:T(8,128)(2,1)}, bf16[64,576]{1,0:T(8,128)(2,1)S(1)}, u32[]{:S(2)}) copy-start(bf16[64,576]{1,0:T(8,128)(2,1)S(1)} %collective-permute-done.2.rest_2_) | copy-start | bytes 221188
  24.3 6.8 %collective-permute-start.7 = (bf16[64,576]{1,0:T(8,128)(2,1)S(1)}, bf16[64,576]{1,0:T(8,128)(2,1)S(1)}, u32[]{:S(2)}, u32[]{:S(2)}) collective-permute-start(bf16[64,576]{1,0:T(8,128)(2,1)S(1)} %collective-permute-done.rest_0_), channel_id=1, source_target_pairs={{0,1},{1,0},{2,3},{3,2},{4,5},{5,4},{6,7},{7,6},{8,9},{9,8},{10,11... | collective-permute-start | bytes 221192 | tf_op jit(solution)/shard_map/ppermute | solution.py:186
  24.4 6.7 %copy-start.9 = (bf16[64,576]{1,0:T(8,128)(2,1)}, bf16[64,576]{1,0:T(8,128)(2,1)S(1)}, u32[]{:S(2)}) copy-start(bf16[64,576]{1,0:T(8,128)(2,1)S(1)} %collective-permute-done.10.rest_10_) | copy-start | bytes 221188
  24.4 6.8 %collective-permute-start.8 = (bf16[64,576]{1,0:T(8,128)(2,1)S(1)}, bf16[64,576]{1,0:T(8,128)(2,1)S(1)}, u32[]{:S(2)}, u32[]{:S(2)}) collective-permute-start(bf16[64,576]{1,0:T(8,128)(2,1)S(1)} %collective-permute-done.1.rest_1_), channel_id=1, source_target_pairs={{0,1},{1,0},{2,3},{3,2},{4,5},{5,4},{6,7},{7,6},{8,9},{9,8},{10,11... | collective-permute-start | bytes 221192 | tf_op jit(solution)/shard_map/ppermute | solution.py:186
  24.8 6.3 %copy-start.10 = (bf16[64,576]{1,0:T(8,128)(2,1)}, bf16[64,576]{1,0:T(8,128)(2,1)S(1)}, u32[]{:S(2)}) copy-start(bf16[64,576]{1,0:T(8,128)(2,1)S(1)} %collective-permute-done.11.rest_11_) | copy-start | bytes 221188
  24.9 6.4 %collective-permute-start.9 = (bf16[64,576]{1,0:T(8,128)(2,1)S(1)}, bf16[64,576]{1,0:T(8,128)(2,1)S(1)}, u32[]{:S(2)}, u32[]{:S(2)}) collective-permute-start(bf16[64,576]{1,0:T(8,128)(2,1)S(1)} %collective-permute-done.2.rest_2_), channel_id=1, source_target_pairs={{0,1},{1,0},{2,3},{3,2},{4,5},{5,4},{6,7},{7,6},{8,9},{9,8},{10,11... | collective-permute-start | bytes 221192 | tf_op jit(solution)/shard_map/ppermute | solution.py:186
  31.1 0.6 copy-start.11
  31.2 0.6 copy-start.12
  31.2 0.7 copy-start.13
  31.2 0.7 copy-start.14
  31.2 0.7 copy-start.15
  48.1 36.7 %copy-start = (bf16[2048,576]{1,0:T(8,128)(2,1)S(1)}, bf16[2048,576]{1,0:T(8,128)(2,1)}, u32[]{:S(2)}) copy-start(bf16[2048,576]{1,0:T(8,128)(2,1)} %get-tuple-element.9) | copy-start | bytes 7077892
  48.1 2.3 %collective-permute-start.15 = (bf16[7,64,576]{2,1,0:T(8,128)(2,1)}, bf16[7,64,576]{2,1,0:T(8,128)(2,1)S(1)}, u32[]{:S(2)}, u32[]{:S(2)}) collective-permute-start(bf16[7,64,576]{2,1,0:T(8,128)(2,1)} %get-tuple-element.12), channel_id=1, source_target_pairs={{0,1},{1,0},{2,3},{3,2},{4,5},{5,4},{6,7},{7,6},{8,9},{9,8},{10,11... | collective-permute-start | bytes 1548296 | tf_op jit(solution)/shard_map/ppermute | solution.py:203
  49.7 7.1 %collective-permute-start.14 = (f32[64,576]{1,0:T(8,128)S(1)}, f32[64,576]{1,0:T(8,128)S(1)}, u32[]{:S(2)}, u32[]{:S(2)}) collective-permute-start(f32[64,576]{1,0:T(8,128)S(1)} %constant_dynamic-slice_fusion), channel_id=1, source_target_pairs={{0,1},{1,0},{2,3},{3,2},{4,5},{5,4},{6,7},{7,6},{8,9},{9,8},{10,11... | collective-permute-start | bytes 442376 | tf_op jit(solution)/shard_map/ppermute | solution.py:206
  51.7 9.4 %collective-permute-start.16 = (bf16[64,576]{1,0:T(8,128)(2,1)S(1)}, bf16[64,576]{1,0:T(8,128)(2,1)S(1)}, u32[]{:S(2)}, u32[]{:S(2)}) collective-permute-start(bf16[64,576]{1,0:T(8,128)(2,1)S(1)} %get-tuple-element.22), channel_id=1, source_target_pairs={{4,0},{8,4},{12,8},{16,12},{20,16},{24,20},{28,24},{5,1},{9,5},{13... | collective-permute-start | bytes 221192 | tf_op jit(solution)/shard_map/ppermute | solution.py:209
  53.0 11.2 %collective-permute-start.17 = (bf16[64,576]{1,0:T(8,128)(2,1)S(1)}, bf16[64,576]{1,0:T(8,128)(2,1)S(1)}, u32[]{:S(2)}, u32[]{:S(2)}) collective-permute-start(bf16[64,576]{1,0:T(8,128)(2,1)S(1)} %get-tuple-element.28), channel_id=1, source_target_pairs={{8,0},{12,4},{16,8},{20,12},{24,16},{28,20},{9,1},{13,5},{17,9},{2... | collective-permute-start | bytes 221192 | tf_op jit(solution)/shard_map/ppermute | solution.py:209
  54.3 11.8 %collective-permute-start.18 = (bf16[64,576]{1,0:T(8,128)(2,1)S(1)}, bf16[64,576]{1,0:T(8,128)(2,1)S(1)}, u32[]{:S(2)}, u32[]{:S(2)}) collective-permute-start(bf16[64,576]{1,0:T(8,128)(2,1)S(1)} %get-tuple-element.27), channel_id=1, source_target_pairs={{12,0},{16,4},{20,8},{24,12},{28,16},{13,1},{17,5},{21,9},{25,13},... | collective-permute-start | bytes 221192 | tf_op jit(solution)/shard_map/ppermute | solution.py:209
  55.6 20.9 %collective-permute-start.19 = (bf16[64,576]{1,0:T(8,128)(2,1)S(1)}, bf16[64,576]{1,0:T(8,128)(2,1)S(1)}, u32[]{:S(2)}, u32[]{:S(2)}) collective-permute-start(bf16[64,576]{1,0:T(8,128)(2,1)S(1)} %get-tuple-element.26), channel_id=1, source_target_pairs={{16,0},{20,4},{24,8},{28,12},{17,1},{21,5},{25,9},{29,13},{18,2},{... | collective-permute-start | bytes 221192 | tf_op jit(solution)/shard_map/ppermute | solution.py:209
  56.9 22.3 %collective-permute-start.20 = (bf16[64,576]{1,0:T(8,128)(2,1)S(1)}, bf16[64,576]{1,0:T(8,128)(2,1)S(1)}, u32[]{:S(2)}, u32[]{:S(2)}) collective-permute-start(bf16[64,576]{1,0:T(8,128)(2,1)S(1)} %get-tuple-element.25), channel_id=1, source_target_pairs={{20,0},{24,4},{28,8},{21,1},{25,5},{29,9},{22,2},{26,6},{30,10},{2... | collective-permute-start | bytes 221192 | tf_op jit(solution)/shard_map/ppermute | solution.py:209
  61.1 18.1 %collective-permute-start.21 = (bf16[64,576]{1,0:T(8,128)(2,1)S(1)}, bf16[64,576]{1,0:T(8,128)(2,1)S(1)}, u32[]{:S(2)}, u32[]{:S(2)}) collective-permute-start(bf16[64,576]{1,0:T(8,128)(2,1)S(1)} %get-tuple-element.24), channel_id=1, source_target_pairs={{24,0},{28,4},{25,1},{29,5},{26,2},{30,6},{27,3},{31,7}} | collective-permute-start | bytes 221192 | tf_op jit(solution)/shard_map/ppermute | solution.py:209
  64.2 15.0 %collective-permute-start.22 = (bf16[64,576]{1,0:T(8,128)(2,1)S(1)}, bf16[64,576]{1,0:T(8,128)(2,1)S(1)}, u32[]{:S(2)}, u32[]{:S(2)}) collective-permute-start(bf16[64,576]{1,0:T(8,128)(2,1)S(1)} %get-tuple-element.23), channel_id=1, source_target_pairs={{28,0},{29,1},{30,2},{31,3}} | collective-permute-start | bytes 221192 | tf_op jit(solution)/shard_map/ppermute | solution.py:209
  80.2 4.5 %collective-permute-start.23 = (bf16[64,576]{1,0:T(8,128)(2,1)S(1)}, bf16[64,576]{1,0:T(8,128)(2,1)S(1)}, u32[]{:S(2)}, u32[]{:S(2)}) collective-permute-start(bf16[64,576]{1,0:T(8,128)(2,1)S(1)} %add_convert_fusion), channel_id=1, source_target_pairs={{0,2},{1,3},{2,0},{3,1},{4,6},{5,7},{6,4},{7,5},{8,10},{9,11},{10,... | collective-permute-start | bytes 221192 | tf_op jit(solution)/shard_map/ppermute | solution.py:214
  84.7 3.2 %collective-permute-start.24 = (f32[64,576]{1,0:T(8,128)S(1)}, f32[64,576]{1,0:T(8,128)S(1)}, u32[]{:S(2)}, u32[]{:S(2)}) collective-permute-start(f32[64,576]{1,0:T(8,128)S(1)} %convert_add_fusion), channel_id=1, source_target_pairs={{0,1},{1,0},{2,3},{3,2},{4,5},{5,4},{6,7},{7,6},{8,9},{9,8},{10,11... | collective-permute-start | bytes 442376 | tf_op jit(solution)/shard_map/ppermute | solution.py:216

commit v2 on v0

v2 whole, which is shorter than its diff:
```python
import functools

import jax
import jax.numpy as jnp
from jax import lax
from jax.experimental import pallas as pl
from jax.experimental.pallas import tpu as pltpu
from jax.sharding import PartitionSpec as P

BLOCK = 64
SCORE_ROWS = 512
OUT_ROWS = 1024
MASKED = -1e30
WIDE_ROWS = 256
VMEM_BYTES = 32 * 1024 * 1024
WIDE_BYTES = 60 * 1024 * 1024
UNROLLED = 1 << 21

softmax_scale = 192.0 ** (-0.5)
EXP2_SCALE = softmax_scale * 1.4426950408889634

NN = (((1,), (0,)), ((), ()))
NT = (((1,), (1,)), ((), ()))
TN = (((0,), (0,)), ((), ()))


def dot(a, b, dims):
    return lax.dot_general(a, b, dims, preferred_element_type=jnp.float32)


def per_block(blocks_here, tile_rows, heads, tile):
    which = lax.div(pl.program_id(0), BLOCK * heads // tile_rows)
    for b in range(blocks_here):
        pl.when(which == b)(functools.partial(tile, b))


def spread_slots(dense_ref, acc_ref, want_ref, slots):
    dense_ref[...] = jnp.zeros_like(dense_ref)
    for b in range(acc_ref.shape[0]):
        for at, slot in enumerate(slots):
            offset = pl.multiple_of(want_ref[b, slot] * BLOCK, BLOCK)
            dense_ref[at, pl.ds(offset, BLOCK), :] += acc_ref[b, slot * BLOCK : (slot + 1) * BLOCK, :]


def write_halves(dense_ref, at, my_half, keep_ref, send_ref):
    half = keep_ref.shape[1]
    mine = pl.multiple_of(my_half * half, half)
    other = pl.multiple_of((1 - my_half) * half, half)
    for i in range(keep_ref.shape[0]):
        keep_ref[i, :, :] = dense_ref[at + i, pl.ds(mine, half), :].astype(keep_ref.dtype)
        send_ref[i, :, :] = dense_ref[at + i, pl.ds(other, half), :].astype(send_ref.dtype)


def table_kernel(n_far, heads, place_ref, chosen_ref, bias_ref, want_ref):
    tok_rows = chosen_ref.shape[1]
    blocks_here = tok_rows // BLOCK
    my_shard = place_ref[0]
    chosen = chosen_ref[...]
    valid = chosen >= 0
    owner = jnp.where(valid, lax.div(chosen, blocks_here), -1)
    inside = chosen - owner * blocks_here
    allowed = []
    for slot in range(n_far):
        target = place_ref[2 + slot]
        hit = (owner == target) & valid & (target != my_shard)
        allowed.append(jnp.max(hit.astype(jnp.float32), axis=0, keepdims=True))
        want = jnp.max(jnp.where(hit, inside, 0), axis=0, keepdims=True)
        for b in range(blocks_here):
            want_ref[b, slot] = jnp.max(want[:, b * BLOCK : (b + 1) * BLOCK])
        want_ref[blocks_here, slot] = place_ref[1]
    for j in range(blocks_here):
        hit = valid & (chosen == my_shard * blocks_here + j)
        allowed.append(jnp.max(hit.astype(jnp.float32), axis=0, keepdims=True))
    rows = tok_rows * heads
    token = lax.div(lax.broadcasted_iota(jnp.int32, (tok_rows, rows), 1), heads)
    spread = token == lax.broadcasted_iota(jnp.int32, (tok_rows, rows), 0)
    allowed = jnp.concatenate(allowed, axis=0).astype(jnp.bfloat16)
    by_row = dot(allowed, jnp.where(spread, 1.0, 0.0).astype(jnp.bfloat16), NN)
    bias_ref[...] = jnp.where(by_row > 0.5, 0.0, MASKED)


def join_kernel(*refs):
    out_ref = refs[-1]
    for i, ref in enumerate(refs[:-1]):
        out_ref[i : i + 1, :, :] = ref[...]


def place_slots(keys_ref, want_ref, first_slot, mine_ref, other_ref, skip, my_half, half):
    for b in range(keys_ref.shape[0]):
        for slot in range(mine_ref.shape[0] - skip):
            block = want_ref[b, first_slot + slot]
            offset = pl.multiple_of(lax.rem(block * BLOCK, half), BLOCK)
            mine = mine_ref[skip + slot, pl.ds(offset, BLOCK), :]
            other = other_ref[skip + slot, pl.ds(offset, BLOCK), :]
            picked = jnp.where(lax.div(block * BLOCK, half) == my_half, mine, other)
            keys_ref[b, slot * BLOCK : (slot + 1) * BLOCK, :] = picked


def each_tile(blocks_here, heads, tile_rows, steps, run):
    block_rows = BLOCK * heads
    if steps == 1:
        run([(b, b * block_rows + at, at) for b in range(blocks_here) for at in range(0, block_rows, tile_rows)])
        return
    step = pl.program_id(0)
    at = lax.rem(step, block_rows // tile_rows) * tile_rows
    for b in range(blocks_here):
        pl.when(lax.div(step, block_rows // tile_rows) == b)(functools.partial(run, [(b, 0, at)]))


def early_kernel(n_cross, blocks_here, heads, tile_rows, steps, want_ref, q_ref, g_ref, own_ref, mine_ref, other_ref, keys_ref, scores_ref, gw_ref, grad_ref):
    value_width = g_ref.shape[1]
    half = blocks_here // 2 * BLOCK
    n_direct = mine_ref.shape[0] - 1

    def start():
        place_slots(keys_ref, want_ref, n_cross, mine_ref, other_ref, 1, want_ref[blocks_here, 0], half)
        for b in range(blocks_here):
            keys_ref[b, n_direct * BLOCK :, :] = own_ref[...]

    def run(tiles):
        for b, local, _ in tiles:
            count = (n_direct + b + 1) * BLOCK
            here = slice(local, local + tile_rows)
            scores_ref[:count, here] = dot(keys_ref[b, :count, :], q_ref[here, :], NT)
            gw_ref[:count, here] = dot(keys_ref[b, :count, :value_width], g_ref[here, :], NT)

    at_step(0, steps, start)
    grad_ref[...] = g_ref[...]
    each_tile(blocks_here, heads, tile_rows, steps, run)


def at_step(which, steps, fn):
    if steps == 1:
        fn()
    else:
        pl.when(pl.program_id(0) == which)(fn)


def score_kernel(n_far, n_cross, blocks_here, heads, tile_rows, steps, want_ref, q_ref, g_ref, bias_ref, early_keys_ref, early_scores_ref, early_gw_ref, mine_ref, other_ref, weights_ref, grads_ref, keys_ref, keep_ref, send_ref, late_keep_ref, late_send_ref, acc_ref, dense_ref):
    value_width = g_ref.shape[1]
    half = blocks_here // 2 * BLOCK
    cross_rows = n_cross * BLOCK
    my_half = want_ref[blocks_here, 0]
    far_rows = n_far * BLOCK

    def start():
        place_slots(keys_ref, want_ref, 0, mine_ref, other_ref, 0, my_half, half)
        keys_ref[:, cross_rows:, :] = early_keys_ref[...]
        if steps > 1:
            acc_ref[...] = jnp.zeros_like(acc_ref)

    def window(tile):
        b, local, _ = tile
        return n_far + b + 1, slice(local, local + tile_rows)

    def products(tile):
        here = window(tile)[1]
        keys = keys_ref[tile[0], :cross_rows, :]
        scores = dot(keys, q_ref[here, :], NT)
        grad_weights = dot(keys[:, :value_width], g_ref[here, :], NT)
        return scores, grad_weights

    def finish(tile, scores, grad_weights):
        b, _, at = tile
        slots, here = window(tile)
        count = slots * BLOCK
        early = count - cross_rows
        scores = jnp.concatenate([scores, early_scores_ref[:early, here]], axis=0)
        grad_weights = jnp.concatenate([grad_weights, early_gw_ref[:early, here]], axis=0)
        scores = scores.reshape(slots, BLOCK, tile_rows)
        token = lax.div(at, heads) + lax.div(lax.broadcasted_iota(jnp.int32, (1, BLOCK, tile_rows), 2), heads)
        place = lax.broadcasted_iota(jnp.int32, (1, BLOCK, tile_rows), 1)
        last = jnp.where(place <= token, scores[slots - 1 :], MASKED)
        scores = jnp.concatenate([scores[: slots - 1], last], axis=0)
        bias = bias_ref[:slots, here]
        top = jnp.max(jnp.max(scores, axis=1) * EXP2_SCALE + bias, axis=0, keepdims=True)
        raised = jnp.exp2(scores * EXP2_SCALE + (bias - top)[:, None, :]).reshape(count, tile_rows)
        total = jnp.sum(raised, axis=0, keepdims=True)
        weights = raised * (1.0 / total)
        row_delta = jnp.sum(weights * grad_weights, axis=0, keepdims=True)
        grad_scores = (weights * (grad_weights - row_delta)).astype(jnp.bfloat16)
        weights_low = weights.astype(jnp.bfloat16)
        weights_ref[:count, here] = weights_low
        grads_ref[:count, here] = grad_scores
        query_part = dot(grad_scores[:far_rows], q_ref[here, :], NN) * softmax_scale
        grad_part = dot(weights_low[:far_rows], g_ref[here, :], NN)
        if steps == 1 and at == 0:
            acc_ref[b, :, :] = query_part
        else:
            acc_ref[b, :, :] += query_part
        acc_ref[b, :, :value_width] += grad_part

    def run(tiles):
        ready = products(tiles[0])
        for i, tile in enumerate(tiles):
            coming = products(tiles[i + 1]) if i + 1 < len(tiles) else None
            finish(tile, *ready)
            ready = coming

    def end():
        spread_slots(dense_ref, acc_ref, want_ref, list(range(1, n_cross)) + [0] + list(range(n_cross, n_far)))
        write_halves(dense_ref, 0, my_half, keep_ref, send_ref)
        write_halves(dense_ref, n_cross - 1, my_half, late_keep_ref, late_send_ref)

    at_step(0, steps, start)
    each_tile(blocks_here, heads, tile_rows, steps, run)
    at_step(steps - 1, steps, end)


def grad_kernel(n_far, blocks_here, heads, want_ref, q_ref, g_ref, weights_ref, grads_ref, keep_ref, send_ref, acc_ref, dense_ref):
    value_width = g_ref.shape[1]
    start = n_far * BLOCK
    block_rows = BLOCK * heads
    for b in range(blocks_here):
        count = (b + 1) * BLOCK
        here = slice(b * block_rows, (b + 1) * block_rows)
        acc_ref[b, :count, :] = dot(grads_ref[start : start + count, here], q_ref[here, :], NN) * softmax_scale
        acc_ref[b, :count, :value_width] += dot(weights_ref[start : start + count, here], g_ref[here, :], NN)
    for j in range(blocks_here):
        rows = slice(j * BLOCK, (j + 1) * BLOCK)
        part = acc_ref[j, rows, :]
        for b in range(j + 1, blocks_here):
            part = part + acc_ref[b, rows, :]
        dense_ref[0, rows, :] = part
    write_halves(dense_ref, 0, want_ref[blocks_here, 0], keep_ref, send_ref)


def out_kernel(n_far, blocks_here, heads, keys_ref, weights_ref, grads_ref, att_ref, gq_ref):
    tile_rows, value_width = att_ref.shape

    def tile(b):
        count = (n_far + b + 1) * BLOCK
        att_ref[...] = dot(weights_ref[:count, :], keys_ref[b, :count, :value_width], TN).astype(att_ref.dtype)
        product = dot(grads_ref[:count, :], keys_ref[b, :count, :], TN)
        gq_ref[...] = (product * softmax_scale).astype(gq_ref.dtype)

    per_block(blocks_here, tile_rows, heads, tile)


def whole(shape):
    return pl.BlockSpec(shape, lambda i: (0,) * len(shape))


def rows_of(tile_rows, width):
    return pl.BlockSpec((tile_rows, width), lambda i: (i, 0))


def lanes_of(count, tile_rows):
    return pl.BlockSpec((count, tile_rows), lambda i: (0, i))


def call(kernel, grid, in_specs, out_specs, out_shape, scratch, macs, moved, name):
    return pl.pallas_call(
        kernel,
        grid=(grid,),
        in_specs=in_specs,
        out_specs=out_specs,
        out_shape=out_shape,
        scratch_shapes=scratch,
        compiler_params=pltpu.CompilerParams(vmem_limit_bytes=VMEM_BYTES),
        cost_estimate=pl.CostEstimate(flops=2 * macs, bytes_accessed=moved, transcendentals=0),
        name=name,
    )


def whole_call(kernel, in_specs, out_specs, out_shape, scratch, macs, moved, name, steps=1):
    in_vmem = pl.BlockSpec(memory_space=pltpu.VMEM)
    if steps == 1:
        in_specs, out_specs, grid = [in_vmem] * len(in_specs), (in_vmem,) * len(out_specs), {}
    else:
        grid = {"grid": (steps,)}
    return pl.pallas_call(
        kernel,
        in_specs=[pl.BlockSpec(memory_space=pltpu.SMEM)] + list(in_specs),
        out_specs=tuple(out_specs),
        out_shape=out_shape,
        scratch_shapes=scratch,
        compiler_params=pltpu.CompilerParams(
            vmem_limit_bytes=VMEM_BYTES if steps == 1 else WIDE_BYTES
        ),
        cost_estimate=pl.CostEstimate(flops=2 * macs, bytes_accessed=moved, transcendentals=0),
        name=name,
        **grid,
    )


def tiling(rows, keys, heads):
    if rows * keys <= UNROLLED:
        return min(SCORE_ROWS, BLOCK * heads), 1
    tile_rows = min(WIDE_ROWS, BLOCK * heads)
    return tile_rows, rows // tile_rows


def table_call(place, chosen, n_far, heads):
    tok_rows = chosen.shape[1]
    blocks_here = tok_rows // BLOCK
    smem = pl.BlockSpec(memory_space=pltpu.SMEM)
    in_vmem = pl.BlockSpec(memory_space=pltpu.VMEM)
    return pl.pallas_call(
        functools.partial(table_kernel, n_far, heads),
        in_specs=[smem, in_vmem],
        out_specs=(in_vmem, smem),
        out_shape=(
            jax.ShapeDtypeStruct((n_far + blocks_here, tok_rows * heads), jnp.float32),
            jax.ShapeDtypeStruct((blocks_here + 1, n_far), jnp.int32),
        ),
        compiler_params=pltpu.CompilerParams(vmem_limit_bytes=VMEM_BYTES),
        name="table",
    )(place, chosen)


def join_call(pieces):
    in_vmem = pl.BlockSpec(memory_space=pltpu.VMEM)
    return pl.pallas_call(
        join_kernel,
        in_specs=[in_vmem] * len(pieces),
        out_specs=in_vmem,
        out_shape=jax.ShapeDtypeStruct((len(pieces),) + pieces[0].shape[1:], pieces[0].dtype),
        compiler_params=pltpu.CompilerParams(vmem_limit_bytes=VMEM_BYTES),
        name="join",
    )(*pieces)


def early_call(want, query_rows, grad_rows, own, mine, other, n_cross, n_far, heads):
    rows, width = query_rows.shape
    value_width = grad_rows.shape[1]
    tok_rows = own.shape[0]
    blocks_here = tok_rows // BLOCK
    keys = (mine.shape[0] - 1) * BLOCK + tok_rows
    tile_rows, steps = tiling(rows, n_far * BLOCK + tok_rows, heads)
    key_shape = (blocks_here, keys, width)
    by_row = [rows_of(tile_rows, width), rows_of(tile_rows, value_width)]
    return whole_call(
        functools.partial(early_kernel, n_cross, blocks_here, heads, tile_rows, steps),
        by_row + [whole(own.shape), whole(mine.shape), whole(other.shape)],
        [whole(key_shape), lanes_of(keys, tile_rows), lanes_of(keys, tile_rows), by_row[1]],
        (
            jax.ShapeDtypeStruct(key_shape, jnp.bfloat16),
            jax.ShapeDtypeStruct((keys, rows), jnp.float32),
            jax.ShapeDtypeStruct((keys, rows), jnp.float32),
            jax.ShapeDtypeStruct((rows, value_width), jnp.bfloat16),
        ),
        [],
        rows * keys * (width + value_width),
        rows * (width + value_width) * 4,
        "early_scores",
        steps,
    )(want, query_rows, grad_rows, own, mine, other)


def score_call(want, query_rows, grad_rows, bias, early, mine, other, n_far, heads, tok_rows):
    rows, width = query_rows.shape
    value_width = grad_rows.shape[1]
    blocks_here = tok_rows // BLOCK
    n_cross = mine.shape[0]
    keys = n_far * BLOCK + tok_rows
    tile_rows, steps = tiling(rows, keys, heads)
    now = jax.ShapeDtypeStruct((n_cross - 1, tok_rows // 2, width), jnp.bfloat16)
    late = jax.ShapeDtypeStruct((n_far - n_cross + 1, tok_rows // 2, width), jnp.bfloat16)
    early_keys = early[0].shape[1]
    key_shape = (blocks_here, keys, width)
    return whole_call(
        functools.partial(score_kernel, n_far, n_cross, blocks_here, heads, tile_rows, steps),
        [
            rows_of(tile_rows, width),
            rows_of(tile_rows, value_width),
            lanes_of(bias.shape[0], tile_rows),
            whole(early[0].shape),
            lanes_of(early_keys, tile_rows),
            lanes_of(early_keys, tile_rows),
            whole(mine.shape),
            whole(other.shape),
        ],
        [lanes_of(keys, tile_rows), lanes_of(keys, tile_rows), whole(key_shape)]
        + [whole(s.shape) for s in (now, now, late, late)],
        (
            jax.ShapeDtypeStruct((keys, rows), jnp.bfloat16),
            jax.ShapeDtypeStruct((keys, rows), jnp.bfloat16),
            jax.ShapeDtypeStruct(key_shape, jnp.bfloat16),
            now,
            now,
            late,
            late,
        ),
        [
            pltpu.VMEM((blocks_here, n_far * BLOCK, width), jnp.float32),
            pltpu.VMEM((n_far, tok_rows, width), jnp.float32),
        ],
        rows * keys * 2 * (width + value_width),
        rows * (width + value_width) * 4,
        "scores",
        steps,
    )(want, query_rows, grad_rows, bias, *early, mine, other)


def grad_call(want, query_rows, grad_rows, weights, grads, n_far, heads, tok_rows):
    rows, width = query_rows.shape
    value_width = grad_rows.shape[1]
    blocks_here = tok_rows // BLOCK
    half = jax.ShapeDtypeStruct((1, tok_rows // 2, width), jnp.bfloat16)
    return whole_call(
        functools.partial(grad_kernel, n_far, blocks_here, heads),
        [None] * 4,
        [None] * 2,
        (half, half),
        [
            pltpu.VMEM((blocks_here, tok_rows, width), jnp.float32),
            pltpu.VMEM((1, tok_rows, width), jnp.float32),
        ],
        rows * tok_rows * (width + value_width),
        rows * (width + value_width) * 4,
        "own_grads",
    )(want, query_rows, grad_rows, weights, grads)


def out_call(keys, weights, grads, n_far, heads, value_width):
    blocks_here, count, width = keys.shape
    rows = weights.shape[1]
    tile_rows = min(OUT_ROWS if rows * count <= UNROLLED else WIDE_ROWS, BLOCK * heads)
    return call(
        functools.partial(out_kernel, n_far, blocks_here, heads),
        rows // tile_rows,
        [whole(keys.shape), lanes_of(count, tile_rows), lanes_of(count, tile_rows)],
        (rows_of(tile_rows, value_width), rows_of(tile_rows, width)),
        (
            jax.ShapeDtypeStruct((rows, value_width), jnp.bfloat16),
            jax.ShapeDtypeStruct((rows, width), jnp.bfloat16),
        ),
        [],
        rows * count * (width + value_width),
        rows * (width + value_width) * 4,
        "outputs",
    )(keys, weights, grads)


def body(queries, latent, cotangent, selection):
    tok_rows, heads, width = queries.shape
    value_width = cotangent.shape[2]
    shards = lax.axis_size("ctx")
    groups = lax.axis_size("head")
    my_shard = lax.axis_index("ctx")
    my_half = lax.axis_index("head") % 2
    blocks_here = tok_rows // BLOCK
    half = tok_rows // 2
    lines = shards // 2
    partner = [(i, i ^ 1) for i in range(groups)]
    across = [(i, i ^ 1) for i in range(shards)]

    def swap(rows):
        return lax.ppermute(rows, "head", partner)

    def up(rows, hops):
        return lax.ppermute(rows, "ctx", [(i, i + 2 * hops) for i in range(shards - 2 * hops)])

    def down(rows, hops):
        return lax.ppermute(rows, "ctx", [(i + 2 * hops, i) for i in range(shards - 2 * hops)])

    offsets = sorted(range(1, lines), key=lambda k: (k != 2, k))
    cross_target = (my_shard ^ 1) - 2 * jnp.array([0] + offsets, jnp.int32)
    direct_target = my_shard - 2 * jnp.array(offsets, jnp.int32)
    n_cross, n_far = lines, shards - 1
    place = jnp.concatenate(
        [jnp.stack([my_shard, my_half]).astype(jnp.int32), cross_target, direct_target]
    )
    grad_rows = cotangent.reshape(tok_rows * heads, value_width)

    held = lax.dynamic_slice_in_dim(latent, my_half * half, half, 0)[None]
    pieces = [held] + [up(held, k) for k in offsets]
    bias, want = table_call(place, selection.T, n_far, heads)
    *pieces, bias, want, queries = lax.optimization_barrier((*pieces, bias, want, queries))
    mine = join_call(pieces)
    mine, queries = lax.optimization_barrier((mine, queries))
    cross = lax.ppermute(mine, "ctx", across)
    query_rows = queries.reshape(tok_rows * heads, width)
    *early, grad_rows = early_call(
        want, query_rows, grad_rows, latent, mine, swap(mine), n_cross, n_far, heads
    )
    cross, early[1] = lax.optimization_barrier((cross, early[1]))
    weights, grads, keys, keep, send, late_keep, late_send = score_call(
        want, query_rows, grad_rows, bias, early, cross, swap(cross), n_far, heads, tok_rows
    )

    moving = (keep.astype(jnp.float32) + swap(send).astype(jnp.float32)).astype(jnp.bfloat16)
    moving, weights, late_send = lax.optimization_barrier((moving, weights, late_send))
    arrived = lax.ppermute(moving, "ctx", across)
    attended, grad_queries = out_call(keys, weights, grads, n_far, heads, value_width)
    late = late_keep.astype(jnp.float32) + swap(late_send).astype(jnp.float32)
    total = (late[1:] + arrived.astype(jnp.float32)).astype(jnp.bfloat16)
    late_own = late[:1].astype(jnp.bfloat16)
    total, late_own, grad_queries, weights = lax.optimization_barrier((total, late_own, grad_queries, weights))
    grad_queries = grad_queries.reshape(tok_rows, heads, width).transpose(1, 2, 0)
    moved = [down(total[i : i + 1], k) for i, k in enumerate(offsets)]
    keep, send = grad_call(want, query_rows, grad_rows, weights, grads, n_far, heads, tok_rows)
    total = keep.astype(jnp.float32) + swap(send).astype(jnp.float32)
    total = total + lax.ppermute(late_own, "ctx", across).astype(jnp.float32)
    for part in moved:
        total = total + part.astype(jnp.float32)
    low = total[0].astype(jnp.bfloat16)
    low, grad_queries = lax.optimization_barrier((low, grad_queries))
    summed = low.astype(jnp.float32)
    for j in range(1, groups // 2):
        moved = lax.ppermute(low, "head", [(i, (i + 2 * j) % groups) for i in range(groups)])
        summed = summed + moved.astype(jnp.float32)
    rest = swap(summed)
    grad_latent = jnp.where(
        my_half == 0,
        jnp.concatenate([summed, rest], axis=0),
        jnp.concatenate([rest, summed], axis=0),
    )
    return (
        attended.reshape(tok_rows, heads, value_width),
        grad_queries.transpose(2, 0, 1),
        grad_latent,
    )


def solution(mesh):
    placed = (P("ctx", "head", None), P("ctx", None), P("ctx", "head", None), P("ctx", None))
    return jax.shard_map(
        body,
        mesh=mesh,
        in_specs=placed,
        out_specs=(P("ctx", "head", None), P("ctx", "head", None), P("ctx", None)),
        check_vma=False,
    )
```

time: 234 us -> 69 us (0.29)
  waiting for transfers between devices: 138 us -> 12.1 us
  local copies, waits for them, and re-layouts: 46.7 us -> 16 us
  matrix products: 23.9 us -> 0 us
  starting transfers between devices: 0.12 us -> 19.6 us
  Pallas kernels: 0 us -> 18.1 us
  between operations: 13.8 us -> 0.9 us
  loops' own time: 5.48 us -> 0 us
  other arithmetic: 5.27 us -> 1.7 us
    reduce_scatter x1 -> x0, waiting for transfers between devices: 68.8 us -> none  [body(): lax.psum_scatter(dense_grad, 'ctx', scatter_dimension=0, tiled=True)]
    all_gather x1 -> x0, waiting for transfers between devices: 40 us -> none  [body(): all_rows = lax.all_gather(latent, 'ctx', axis=0, tiled=True)]
    psum x1 -> x0, waiting for transfers between devices: 28.8 us -> none  [body(): grad_latent = lax.psum(own_sum + own_grad, 'head')]
    dot_general x13 -> x0, matrix products: 23.9 us -> none  [the longest x1 7.94 us: body(): jnp.einsum('rsj,rsbf->rjbf', spread, slot_grad, precision=lax.Precision.H...]
    ppermute x0 -> x16, starting transfers between devices: none -> 19.6 us  [the longest x3 10.7 us: up(): lax.ppermute(rows, 'ctx', [(i, i + 2 * hops) for i in range(shards - 2 *...]
    pallas_call x0 -> x6, Pallas kernels: none -> 18.1 us  [the longest x1 7.63 us: score_call(): whole_call(functools.partial(score_kernel, n_far, n_cross, blocks_here, h...]
    ppermute x0 -> x16, waiting for transfers between devices: none -> 12.1 us  [the longest x6 4.58 us: swap(): return lax.ppermute(rows, 'head', partner)]
    dynamic_slice x14 -> x2, local copies, waits for them, and re-layouts: 9.32 us -> 1.16 us  [body(): held = lax.dynamic_slice_in_dim(latent, my_half * half, half, 0)[None]]
  transfers between devices with their start and end apart: 3 -> 16, of which waited for: 3 -> 7; matrix products, arithmetic and copies ran while one was open for 4% -> 16% of each run, Pallas kernels for 0% -> 13%
where the time goes in v2:
time: 69 us; the launch traced here: 68.5 us
  starting transfers between devices  19.6 us (28%)
  Pallas kernels  18.1 us (26%)
  local copies, waits for them, and re-layouts  16 us (23%)
  waiting for transfers between devices  12.1 us (18%)
  other arithmetic  1.7 us (2%)
  between operations  0.9 us (1%)
    ppermute x3, starting transfers between devices, up(): lax.ppermute(rows, 'ctx', [(i, i + 2 * hops) for i in range(shards - 2 *...  10.7 us
    pallas_call x1, Pallas kernels, score_call(): whole_call(functools.partial(score_kernel, n_far, n_cross, blocks_here, h...  7.63 us
    unnamed x12, local copies, waits for them, and re-layouts  6.2 us
    pallas_call x1, Pallas kernels, out_call(): call(functools.partial(out_kernel, n_far, blocks_here, heads), rows // ti...  5.11 us
    reshape x1, local copies, waits for them, and re-layouts, body(): grad_queries.reshape(tok_rows, heads, width).transpose(1, 2, 0)  4.68 us
    ppermute x6, waiting for transfers between devices, swap(): return lax.ppermute(rows, 'head', partner)  4.58 us
    optimization_barrier x1, local copies, waits for them, and re-layouts, body(): mine, queries = lax.optimization_barrier((mine, queries))  3.92 us
    ppermute x3, starting transfers between devices, down(): lax.ppermute(rows, 'ctx', [(i + 2 * hops, i) for i in range(shards - 2 *...  3.88 us
  transfers between devices with their start and end apart: 16, of which 7 were waited for; matrix products, arithmetic and copies ran while one was open for 16% of the time, Pallas kernels for 13%

profile of v2, /device:TPU:0, one launch (start us, length us, event | category | flops | bytes accessed | tf_op | source)
XLA Modules:
  0.0 68.5 jit_solution(15462028679306304423)
XLA Ops:
  0.6 1.0 %constant_dynamic-slice_fusion = bf16[64,576]{0,1:T(8,128)(2,1)S(1)} fusion(bf16[128,576]{0,1:T(8,128)(2,1)} %param.7, s32[]{:T(128)S(6)} %select_n.19), kind=kLoop, calls=%fused_computation.12 | loop fusion | bytes 147460 | tf_op jit(solution)/shard_map/dynamic_slice | solution.py:467
  1.7 0.1 copy.9
  1.8 7.0 %collective-permute-start.2 = (bf16[1,64,576]{2,1,0:T(8,128)(2,1)S(1)}, bf16[1,64,576]{2,1,0:T(8,128)(2,1)S(1)}, u32[]{:S(2)}, u32[]{:S(2)}) collective-permute-start(bf16[1,64,576]{2,1,0:T(8,128)(2,1)S(1)} %bitcast.17), channel_id=1, source_target_pairs={{0,24},{4,28},{1,25},{5,29},{2,26},{6,30},{3,27},{7,31}} | collective-permute-start | bytes 221192 | tf_op jit(solution)/shard_map/ppermute | solution.py:453
  8.8 1.3 %collective-permute-start.1 = (bf16[1,64,576]{2,1,0:T(8,128)(2,1)S(1)}, bf16[1,64,576]{2,1,0:T(8,128)(2,1)S(1)}, u32[]{:S(2)}, u32[]{:S(2)}) collective-permute-start(bf16[1,64,576]{2,1,0:T(8,128)(2,1)S(1)} %bitcast.18), channel_id=1, source_target_pairs={{0,8},{4,12},{8,16},{12,20},{16,24},{20,28},{1,9},{5,13},{9,17},{1... | collective-permute-start | bytes 221192 | tf_op jit(solution)/shard_map/ppermute | solution.py:453
  10.1 2.5 %collective-permute-start = (bf16[1,64,576]{2,1,0:T(8,128)(2,1)S(1)}, bf16[1,64,576]{2,1,0:T(8,128)(2,1)S(1)}, u32[]{:S(2)}, u32[]{:S(2)}) collective-permute-start(bf16[1,64,576]{2,1,0:T(8,128)(2,1)S(1)} %bitcast.19), channel_id=1, source_target_pairs={{0,16},{4,20},{8,24},{12,28},{1,17},{5,21},{9,25},{13,29},{2,18},{... | collective-permute-start | bytes 221192 | tf_op jit(solution)/shard_map/ppermute | solution.py:453
  12.6 0.7 broadcast_add_fusion
  13.2 0.7 broadcast_add_fusion.1
  13.9 0.1 pad_add_fusion.place_ref
  14.0 0.0 copy-start.2
  14.0 0.7 %copy-done.2 = s32[128,8]{0,1:T(8,128)S(1)} copy-done((s32[128,8]{0,1:T(8,128)S(1)}, s32[128,8]{0,1:T(8,128)}, u32[]{:S(2)}) %copy-start.2) | copy-done | bytes 4120
  14.7 1.4 %table.1 = (f32[9,2048]{1,0:T(8,128)S(1)}, s32[3,7]{1,0:T(4,128)S(1)}) custom-call(s32[9]{0:T(128)S(1)} %pad_add_fusion.place_ref, s32[8,128]{1,0:T(8,128)S(1)} %bitcast.21), custom_call_target="tpu_custom_call" | custom-call | tf_op jit(solution)/shard_map/table/pallas_call | solution.py:299
  16.0 0.0 copy-start.3
  16.1 0.0 collective-permute-done.2.refs_3_
  16.1 0.0 collective-permute-done.1.refs_2_
  16.1 0.0 collective-permute-done.refs_1_
  16.1 0.1 collective-permute-start.3
  16.2 0.5 copy-done.3
  16.7 1.5 %collective-permute-start.4 = (bf16[4,64,576]{2,1,0:T(8,128)(2,1)S(1)}, bf16[4,64,576]{2,1,0:T(8,128)(2,1)}, u32[]{:S(2)}, u32[]{:S(2)}) collective-permute-start(bf16[4,64,576]{2,1,0:T(8,128)(2,1)S(1)} %join.1.mine_ref), channel_id=1, source_target_pairs={{0,4},{4,0},{8,12},{12,8},{16,20},{20,16},{24,28},{28,24},{1,5},{5... | collective-permute-start | bytes 884744 | tf_op jit(solution)/shard_map/ppermute | solution.py:473
  18.2 1.1 %copy.11.own_ref = bf16[128,576]{1,0:T(8,128)(2,1)S(1)} copy(bf16[128,576]{0,1:T(8,128)(2,1)} %param.7) | data formatting | bytes 294912 | tf_op args[1]
  19.3 3.9 %copy.10 = bf16[128,16,576]{2,1,0:T(8,128)(2,1)S(1)} copy(bf16[128,16,576]{0,2,1:T(8,128)(2,1)} %param.6) | data formatting | bytes 4718592 | tf_op jit(solution)/shard_map/optimization_barrier | solution.py:472
  23.2 0.0 collective-permute-done.3.other_ref
  23.2 0.0 copy-start.1
  23.2 1.6 %copy-done.1 = bf16[128,16,512]{2,1,0:T(8,128)(2,1)S(1)} copy-done((bf16[128,16,512]{2,1,0:T(8,128)(2,1)S(1)}, bf16[128,16,512]{2,1,0:T(8,128)(2,1)}, u32[]{:S(2)}) %copy-start.1) | copy-done | bytes 2097176
  24.8 0.0 copy-start.4
  24.8 2.4 %early_scores.1 = (bf16[2,320,576]{2,1,0:T(8,128)(2,1)S(1)}, f32[320,2048]{1,0:T(8,128)S(1)}, f32[320,2048]{1,0:T(8,128)S(1)}, bf16[2048,512]{1,0:T(8,128)(2,1)S(1)}) custom-call(s32[3,7]{1,0:T(4,128)S(1)} %get-tuple-element.42.want_ref, bf16[2048,576]{1,0:T(8,128)(2,1)S(1)} %bitcast.12, bf16[2048,512]{1,0:T(8,128)(2,1)S(1)} %bitcast.16, ...), custom_call_target="tpu_custom_call" | custom-call | flops 1426063360 | bytes 8912896 | tf_op jit(solution)/shard_map/early_scores/pallas_call | solution.py:333
  27.2 0.0 collective-permute-done.4.mine_ref
  27.3 0.1 collective-permute-start.5
  27.3 1.8 %collective-permute-done.5.other_ref = bf16[4,64,576]{2,1,0:T(8,128)(2,1)S(1)} collective-permute-done((bf16[4,64,576]{2,1,0:T(8,128)(2,1)}, bf16[4,64,576]{2,1,0:T(8,128)(2,1)S(1)}, u32[]{:S(2)}, u32[]{:S(2)}) %collective-permute-start.5) | collective-permute-done | bytes 294944 | tf_op jit(solution)/shard_map/ppermute | solution.py:450
  29.2 0.0 copy-done.4
  29.2 7.6 %scores.1 = (bf16[576,2048]{1,0:T(8,128)(2,1)S(1)}, bf16[576,2048]{1,0:T(8,128)(2,1)S(1)}, bf16[2,576,576]{2,1,0:T(8,128)(2,1)S(1)}, bf16[3,64,576]{2,1,0:T(8,12...) custom-call(s32[3,7]{1,0:T(4,128)S(1)} %get-tuple-element.42.want_ref, ...), custom_call_target="tpu_custom_call" | custom-call | flops 5133828096 | bytes 8912896 | tf_op jit(solution)/shard_map/scores/pallas_call | solution.py:362
  36.8 0.2 collective-permute-start.6
  37.0 1.4 %collective-permute-done.6 = bf16[3,64,576]{2,1,0:T(8,128)(2,1)S(1)} collective-permute-done((bf16[3,64,576]{2,1,0:T(8,128)(2,1)S(1)}, bf16[3,64,576]{2,1,0:T(8,128)(2,1)S(1)}, u32[]{:S(2)}, u32[]{:S(2)}) %collective-permute-start.6) | collective-permute-done | bytes 221216 | tf_op jit(solution)/shard_map/ppermute | solution.py:450
  38.4 0.1 add_convert_fusion
  38.5 0.2 collective-permute-start.7
  38.7 0.6 collective-permute-start.8
  39.3 5.1 %outputs.1 = (bf16[2048,512]{1,0:T(8,128)(2,1)}, bf16[2048,576]{1,0:T(8,128)(2,1)S(1)}) custom-call(bf16[2,576,576]{2,1,0:T(8,128)(2,1)S(1)} %get-tuple-element.57.keys_ref, bf16[576,2048]{1,0:T(8,128)(2,1)S(1)} %get-tuple-element.69.weights_ref, bf16[576,2048]{1,0:T(8,128)(2,1)S(1)} %get-tuple-element.63.grads_ref), custom_call_target="tpu_custom_call" | custom-call | flops 2566914048 | bytes 8912896 | tf_op jit(solution)/shard_map/outputs/pallas_call | solution.py:420
  44.4 0.0 copy-start
  44.4 1.5 %copy-done = bf16[2048,576]{1,0:T(8,128)(2,1)} copy-done((bf16[2048,576]{1,0:T(8,128)(2,1)}, bf16[2048,576]{1,0:T(8,128)(2,1)S(1)}, u32[]{:S(2)}) %copy-start) | copy-done | bytes 2359320
  45.9 0.0 collective-permute-done.7
  45.9 0.1 convert_add_fusion
  46.0 0.9 %collective-permute-done.8 = bf16[3,64,576]{2,1,0:T(8,128)(2,1)S(1)} collective-permute-done((bf16[3,64,576]{2,1,0:T(8,128)(2,1)S(1)}, bf16[3,64,576]{2,1,0:T(8,128)(2,1)S(1)}, u32[]{:S(2)}, u32[]{:S(2)}) %collective-permute-start.8) | collective-permute-done | bytes 221216 | tf_op jit(solution)/shard_map/ppermute | solution.py:485
  46.9 0.1 fusion
  46.9 1.5 %own_grads.1 = (bf16[1,64,576]{2,1,0:T(8,128)(2,1)S(1)}, bf16[1,64,576]{2,1,0:T(8,128)(2,1)S(1)}) custom-call(s32[3,7]{1,0:T(4,128)S(1)} %get-tuple-element.42.want_ref, bf16[2048,576]{1,0:T(8,128)(2,1)S(1)} %bitcast.14, bf16[2048,512]{1,0:T(8,128)(2,1)S(1)} %get-tuple-element.50.g_ref, bf16[576,2048]{1,0:T(8,128)(2,1)S(1)} %get-tuple-element.69.weights_ref, ...), custom_call_target="tpu_custom_call" | custom-call | flops 570425344 | bytes 8912896 | tf_op jit(solution)/shard_map/own_grads/pallas_call | solution.py:401
  48.5 0.1 collective-permute-start.9
  48.6 0.7 collective-permute-start.10
  49.2 1.3 %collective-permute-start.11 = (bf16[1,64,576]{2,1,0:T(8,128)(2,1)S(1)}, bf16[1,64,576]{2,1,0:T(8,128)(2,1)S(1)}, u32[]{:S(2)}, u32[]{:S(2)}) collective-permute-start(bf16[1,64,576]{2,1,0:T(8,128)(2,1)S(1)} %get-tuple-element.80), channel_id=1, source_target_pairs={{16,0},{20,4},{24,8},{28,12},{17,1},{21,5},{25,9},{29,13},{18,2},{... | collective-permute-start | bytes 221192 | tf_op jit(solution)/shard_map/ppermute | solution.py:456
  50.5 1.3 %collective-permute-start.13 = (bf16[1,64,576]{2,1,0:T(8,128)(2,1)S(1)}, bf16[1,64,576]{2,1,0:T(8,128)(2,1)S(1)}, u32[]{:S(2)}, u32[]{:S(2)}) collective-permute-start(bf16[1,64,576]{2,1,0:T(8,128)(2,1)S(1)} %get-tuple-element.81), channel_id=1, source_target_pairs={{24,0},{28,4},{25,1},{29,5},{26,2},{30,6},{27,3},{31,7}} | collective-permute-start | bytes 221192 | tf_op jit(solution)/shard_map/ppermute | solution.py:456
  51.8 1.3 %collective-permute-start.12 = (bf16[1,64,576]{2,1,0:T(8,128)(2,1)S(1)}, bf16[1,64,576]{2,1,0:T(8,128)(2,1)S(1)}, u32[]{:S(2)}, u32[]{:S(2)}) collective-permute-start(bf16[1,64,576]{2,1,0:T(8,128)(2,1)S(1)} %get-tuple-element.82), channel_id=1, source_target_pairs={{8,0},{12,4},{16,8},{20,12},{24,16},{28,20},{9,1},{13,5},{17,9},{2... | collective-permute-start | bytes 221192 | tf_op jit(solution)/shard_map/ppermute | solution.py:456
  53.1 4.7 %copy.12 = bf16[128,16,576]{0,2,1:T(8,128)(2,1)} copy(bf16[128,16,576]{2,1,0:T(8,128)(2,1)} %bitcast.15) | data formatting | bytes 4718592 | tf_op jit(solution)/shard_map/reshape | solution.py:491
  57.8 0.0 collective-permute-done.9
  57.8 0.0 collective-permute-done.10
  57.8 2.0 %collective-permute-done.11 = bf16[1,64,576]{2,1,0:T(8,128)(2,1)S(1)} collective-permute-done((bf16[1,64,576]{2,1,0:T(8,128)(2,1)S(1)}, bf16[1,64,576]{2,1,0:T(8,128)(2,1)S(1)}, u32[]{:S(2)}, u32[]{:S(2)}) %collective-permute-start.11) | collective-permute-done | bytes 73760 | tf_op jit(solution)/shard_map/ppermute | solution.py:456
  59.9 0.0 collective-permute-done.13
  59.9 1.6 %collective-permute-done.12 = bf16[1,64,576]{2,1,0:T(8,128)(2,1)S(1)} collective-permute-done((bf16[1,64,576]{2,1,0:T(8,128)(2,1)S(1)}, bf16[1,64,576]{2,1,0:T(8,128)(2,1)S(1)}, u32[]{:S(2)}, u32[]{:S(2)}) %collective-permute-start.12) | collective-permute-done | bytes 73760 | tf_op jit(solution)/shard_map/ppermute | solution.py:456
  61.5 0.1 fusion.1
  61.6 1.6 %collective-permute-start.14 = (bf16[64,576]{1,0:T(8,128)(2,1)S(1)}, bf16[64,576]{1,0:T(8,128)(2,1)S(1)}, u32[]{:S(2)}, u32[]{:S(2)}) collective-permute-start(bf16[64,576]{1,0:T(8,128)(2,1)S(1)} %fusion.1), channel_id=1, source_target_pairs={{0,2},{1,3},{2,0},{3,1},{4,6},{5,7},{6,4},{7,5},{8,10},{9,11},{10,... | collective-permute-start | bytes 221192 | tf_op jit(solution)/shard_map/ppermute | solution.py:502
  63.2 2.9 %collective-permute-done.14 = bf16[64,576]{1,0:T(8,128)(2,1)S(1)} collective-permute-done((bf16[64,576]{1,0:T(8,128)(2,1)S(1)}, bf16[64,576]{1,0:T(8,128)(2,1)S(1)}, u32[]{:S(2)}, u32[]{:S(2)}) %collective-permute-start.14) | collective-permute-done | bytes 73760 | tf_op jit(solution)/shard_map/ppermute | solution.py:502
  66.1 0.1 collective-permute-start.15
  66.2 1.4 %collective-permute-done.15 = f32[64,576]{1,0:T(8,128)S(1)} collective-permute-done((f32[64,576]{1,0:T(8,128)S(1)}, f32[64,576]{1,0:T(8,128)S(1)}, u32[]{:S(2)}, u32[]{:S(2)}) %collective-permute-start.15) | collective-permute-done | bytes 147488 | tf_op jit(solution)/shard_map/ppermute | solution.py:450
  67.6 0.9 %copy.13 = f32[128,576]{0,1:T(8,128)} copy(f32[128,576]{1,0:T(8,128)S(1)} %maximum_select_fusion) | data formatting | bytes 589824
  (5 shorter events, 0.1 us)
Async XLA Ops:
  1.8 14.2 %collective-permute-start.2 = (bf16[1,64,576]{2,1,0:T(8,128)(2,1)S(1)}, bf16[1,64,576]{2,1,0:T(8,128)(2,1)S(1)}, u32[]{:S(2)}, u32[]{:S(2)}) collective-permute-start(bf16[1,64,576]{2,1,0:T(8,128)(2,1)S(1)} %bitcast.17), channel_id=1, source_target_pairs={{0,24},{4,28},{1,25},{5,29},{2,26},{6,30},{3,27},{7,31}} | collective-permute-start | bytes 221192 | tf_op jit(solution)/shard_map/ppermute | solution.py:453
  8.8 7.3 %collective-permute-start.1 = (bf16[1,64,576]{2,1,0:T(8,128)(2,1)S(1)}, bf16[1,64,576]{2,1,0:T(8,128)(2,1)S(1)}, u32[]{:S(2)}, u32[]{:S(2)}) collective-permute-start(bf16[1,64,576]{2,1,0:T(8,128)(2,1)S(1)} %bitcast.18), channel_id=1, source_target_pairs={{0,8},{4,12},{8,16},{12,20},{16,24},{20,28},{1,9},{5,13},{9,17},{1... | collective-permute-start | bytes 221192 | tf_op jit(solution)/shard_map/ppermute | solution.py:453
  10.1 6.0 %collective-permute-start = (bf16[1,64,576]{2,1,0:T(8,128)(2,1)S(1)}, bf16[1,64,576]{2,1,0:T(8,128)(2,1)S(1)}, u32[]{:S(2)}, u32[]{:S(2)}) collective-permute-start(bf16[1,64,576]{2,1,0:T(8,128)(2,1)S(1)} %bitcast.19), channel_id=1, source_target_pairs={{0,16},{4,20},{8,24},{12,28},{1,17},{5,21},{9,25},{13,29},{2,18},{... | collective-permute-start | bytes 221192 | tf_op jit(solution)/shard_map/ppermute | solution.py:453
  14.0 0.7 %copy-start.2 = (s32[128,8]{0,1:T(8,128)S(1)}, s32[128,8]{0,1:T(8,128)}, u32[]{:S(2)}) copy-start(s32[128,8]{0,1:T(8,128)} %param.9) | copy-start | bytes 12292
  16.0 0.7 copy-start.3
  16.1 7.1 %collective-permute-start.3 = (bf16[4,64,576]{2,1,0:T(8,128)(2,1)S(1)}, bf16[4,64,576]{2,1,0:T(8,128)(2,1)S(1)}, u32[]{:S(2)}, u32[]{:S(2)}) collective-permute-start(bf16[4,64,576]{2,1,0:T(8,128)(2,1)S(1)} %join.1.mine_ref), channel_id=1, source_target_pairs={{0,1},{1,0},{2,3},{3,2},{4,5},{5,4},{6,7},{7,6},{8,9},{9,8},{10,11... | collective-permute-start | bytes 884744 | tf_op jit(solution)/shard_map/ppermute | solution.py:450
  16.7 10.5 %collective-permute-start.4 = (bf16[4,64,576]{2,1,0:T(8,128)(2,1)S(1)}, bf16[4,64,576]{2,1,0:T(8,128)(2,1)}, u32[]{:S(2)}, u32[]{:S(2)}) collective-permute-start(bf16[4,64,576]{2,1,0:T(8,128)(2,1)S(1)} %join.1.mine_ref), channel_id=1, source_target_pairs={{0,4},{4,0},{8,12},{12,8},{16,20},{20,16},{24,28},{28,24},{1,5},{5... | collective-permute-start | bytes 884744 | tf_op jit(solution)/shard_map/ppermute | solution.py:473
  23.2 1.6 %copy-start.1 = (bf16[128,16,512]{2,1,0:T(8,128)(2,1)S(1)}, bf16[128,16,512]{2,1,0:T(8,128)(2,1)}, u32[]{:S(2)}) copy-start(bf16[128,16,512]{2,1,0:T(8,128)(2,1)} %param.8) | copy-start | bytes 6291460
  24.8 4.4 %copy-start.4 = (f32[9,2048]{1,0:T(8,128)S(1)}, f32[9,2048]{1,0:T(8,128)}, u32[]{:S(2)}) copy-start(f32[9,2048]{1,0:T(8,128)} %copy-done.3) | copy-start | bytes 221188
  27.3 1.9 %collective-permute-start.5 = (bf16[4,64,576]{2,1,0:T(8,128)(2,1)}, bf16[4,64,576]{2,1,0:T(8,128)(2,1)S(1)}, u32[]{:S(2)}, u32[]{:S(2)}) collective-permute-start(bf16[4,64,576]{2,1,0:T(8,128)(2,1)} %collective-permute-done.4.mine_ref), channel_id=1, source_target_pairs={{0,1},{1,0},{2,3},{3,2},{4,5},{5,4},{6,7},{7,6},{8,9},{9,8},{10,11... | collective-permute-start | bytes 884744 | tf_op jit(solution)/shard_map/ppermute | solution.py:450
  36.8 1.6 %collective-permute-start.6 = (bf16[3,64,576]{2,1,0:T(8,128)(2,1)S(1)}, bf16[3,64,576]{2,1,0:T(8,128)(2,1)S(1)}, u32[]{:S(2)}, u32[]{:S(2)}) collective-permute-start(bf16[3,64,576]{2,1,0:T(8,128)(2,1)S(1)} %get-tuple-element.59), channel_id=1, source_target_pairs={{0,1},{1,0},{2,3},{3,2},{4,5},{5,4},{6,7},{7,6},{8,9},{9,8},{10,11... | collective-permute-start | bytes 663560 | tf_op jit(solution)/shard_map/ppermute | solution.py:450
  38.5 7.4 %collective-permute-start.7 = (bf16[4,64,576]{2,1,0:T(8,128)(2,1)S(1)}, bf16[4,64,576]{2,1,0:T(8,128)(2,1)S(1)}, u32[]{:S(2)}, u32[]{:S(2)}) collective-permute-start(bf16[4,64,576]{2,1,0:T(8,128)(2,1)S(1)} %get-tuple-element.66), channel_id=1, source_target_pairs={{0,1},{1,0},{2,3},{3,2},{4,5},{5,4},{6,7},{7,6},{8,9},{9,8},{10,11... | collective-permute-start | bytes 884744 | tf_op jit(solution)/shard_map/ppermute | solution.py:450
  38.7 8.2 %collective-permute-start.8 = (bf16[3,64,576]{2,1,0:T(8,128)(2,1)S(1)}, bf16[3,64,576]{2,1,0:T(8,128)(2,1)S(1)}, u32[]{:S(2)}, u32[]{:S(2)}) collective-permute-start(bf16[3,64,576]{2,1,0:T(8,128)(2,1)S(1)} %add_convert_fusion), channel_id=1, source_target_pairs={{0,4},{4,0},{8,12},{12,8},{16,20},{20,16},{24,28},{28,24},{1,5},{5... | collective-permute-start | bytes 663560 | tf_op jit(solution)/shard_map/ppermute | solution.py:485
  44.4 1.5 %copy-start = (bf16[2048,576]{1,0:T(8,128)(2,1)}, bf16[2048,576]{1,0:T(8,128)(2,1)S(1)}, u32[]{:S(2)}) copy-start(bf16[2048,576]{1,0:T(8,128)(2,1)S(1)} %get-tuple-element.74) | copy-start | bytes 7077892
  48.5 9.3 %collective-permute-start.9 = (bf16[1,64,576]{2,1,0:T(8,128)(2,1)S(1)}, bf16[1,64,576]{2,1,0:T(8,128)(2,1)S(1)}, u32[]{:S(2)}, u32[]{:S(2)}) collective-permute-start(bf16[1,64,576]{2,1,0:T(8,128)(2,1)S(1)} %get-tuple-element.71), channel_id=1, source_target_pairs={{0,1},{1,0},{2,3},{3,2},{4,5},{5,4},{6,7},{7,6},{8,9},{9,8},{10,11... | collective-permute-start | bytes 221192 | tf_op jit(solution)/shard_map/ppermute | solution.py:450
  48.6 9.3 %collective-permute-start.10 = (bf16[1,64,576]{2,1,0:T(8,128)(2,1)S(1)}, bf16[1,64,576]{2,1,0:T(8,128)(2,1)S(1)}, u32[]{:S(2)}, u32[]{:S(2)}) collective-permute-start(bf16[1,64,576]{2,1,0:T(8,128)(2,1)S(1)} %slice.27), channel_id=1, source_target_pairs={{0,4},{4,0},{8,12},{12,8},{16,20},{20,16},{24,28},{28,24},{1,5},{5... | collective-permute-start | bytes 221192 | tf_op jit(solution)/shard_map/ppermute | solution.py:495
  49.2 10.6 %collective-permute-start.11 = (bf16[1,64,576]{2,1,0:T(8,128)(2,1)S(1)}, bf16[1,64,576]{2,1,0:T(8,128)(2,1)S(1)}, u32[]{:S(2)}, u32[]{:S(2)}) collective-permute-start(bf16[1,64,576]{2,1,0:T(8,128)(2,1)S(1)} %get-tuple-element.80), channel_id=1, source_target_pairs={{16,0},{20,4},{24,8},{28,12},{17,1},{21,5},{25,9},{29,13},{18,2},{... | collective-permute-start | bytes 221192 | tf_op jit(solution)/shard_map/ppermute | solution.py:456
  50.5 9.3 %collective-permute-start.13 = (bf16[1,64,576]{2,1,0:T(8,128)(2,1)S(1)}, bf16[1,64,576]{2,1,0:T(8,128)(2,1)S(1)}, u32[]{:S(2)}, u32[]{:S(2)}) collective-permute-start(bf16[1,64,576]{2,1,0:T(8,128)(2,1)S(1)} %get-tuple-element.81), channel_id=1, source_target_pairs={{24,0},{28,4},{25,1},{29,5},{26,2},{30,6},{27,3},{31,7}} | collective-permute-start | bytes 221192 | tf_op jit(solution)/shard_map/ppermute | solution.py:456
  51.8 9.7 %collective-permute-start.12 = (bf16[1,64,576]{2,1,0:T(8,128)(2,1)S(1)}, bf16[1,64,576]{2,1,0:T(8,128)(2,1)S(1)}, u32[]{:S(2)}, u32[]{:S(2)}) collective-permute-start(bf16[1,64,576]{2,1,0:T(8,128)(2,1)S(1)} %get-tuple-element.82), channel_id=1, source_target_pairs={{8,0},{12,4},{16,8},{20,12},{24,16},{28,20},{9,1},{13,5},{17,9},{2... | collective-permute-start | bytes 221192 | tf_op jit(solution)/shard_map/ppermute | solution.py:456
  61.6 4.5 %collective-permute-start.14 = (bf16[64,576]{1,0:T(8,128)(2,1)S(1)}, bf16[64,576]{1,0:T(8,128)(2,1)S(1)}, u32[]{:S(2)}, u32[]{:S(2)}) collective-permute-start(bf16[64,576]{1,0:T(8,128)(2,1)S(1)} %fusion.1), channel_id=1, source_target_pairs={{0,2},{1,3},{2,0},{3,1},{4,6},{5,7},{6,4},{7,5},{8,10},{9,11},{10,... | collective-permute-start | bytes 221192 | tf_op jit(solution)/shard_map/ppermute | solution.py:502
  66.1 1.5 %collective-permute-start.15 = (f32[64,576]{1,0:T(8,128)S(1)}, f32[64,576]{1,0:T(8,128)S(1)}, u32[]{:S(2)}, u32[]{:S(2)}) collective-permute-start(f32[64,576]{1,0:T(8,128)S(1)} %convert_add_fusion.1), channel_id=1, source_target_pairs={{0,1},{1,0},{2,3},{3,2},{4,5},{5,4},{6,7},{7,6},{8,9},{9,8},{10,11... | collective-permute-start | bytes 442376 | tf_op jit(solution)/shard_map/ppermute | solution.py:450

commit v3 on v2

--- a/solution.py
+++ b/solution.py
@@ -44,11 +44,11 @@
 
 def write_halves(dense_ref, at, my_half, keep_ref, send_ref):
     half = keep_ref.shape[1]
-    mine = pl.multiple_of(my_half * half, half)
-    other = pl.multiple_of((1 - my_half) * half, half)
     for i in range(keep_ref.shape[0]):
-        keep_ref[i, :, :] = dense_ref[at + i, pl.ds(mine, half), :].astype(keep_ref.dtype)
-        send_ref[i, :, :] = dense_ref[at + i, pl.ds(other, half), :].astype(send_ref.dtype)
+        turned = dense_ref[at + i, :, :].astype(keep_ref.dtype).T
+        first, second = turned[:half, :], turned[half:, :]
+        keep_ref[i, :, :] = jnp.where(my_half == 0, first, second)
+        send_ref[i, :, :] = jnp.where(my_half == 0, second, first)
 
 
 def table_kernel(n_far, heads, place_ref, chosen_ref, bias_ref, want_ref):
@@ -85,15 +85,16 @@
         out_ref[i : i + 1, :, :] = ref[...]
 
 
-def place_slots(keys_ref, want_ref, first_slot, mine_ref, other_ref, skip, my_half, half):
-    for b in range(keys_ref.shape[0]):
-        for slot in range(mine_ref.shape[0] - skip):
-            block = want_ref[b, first_slot + slot]
-            offset = pl.multiple_of(lax.rem(block * BLOCK, half), BLOCK)
-            mine = mine_ref[skip + slot, pl.ds(offset, BLOCK), :]
-            other = other_ref[skip + slot, pl.ds(offset, BLOCK), :]
-            picked = jnp.where(lax.div(block * BLOCK, half) == my_half, mine, other)
-            keys_ref[b, slot * BLOCK : (slot + 1) * BLOCK, :] = picked
+def place_slots(keys_ref, rows_ref, want_ref, first_slot, mine_ref, other_ref, skip, my_half):
+    for slot in range(mine_ref.shape[0] - skip):
+        mine, other = mine_ref[skip + slot, :, :], other_ref[skip + slot, :, :]
+        turned = jnp.concatenate(
+            [jnp.where(my_half == 0, mine, other), jnp.where(my_half == 0, other, mine)], axis=0
+        )
+        rows_ref[slot, :, :] = turned.T
+        for b in range(keys_ref.shape[0]):
+            offset = pl.multiple_of(want_ref[b, first_slot + slot] * BLOCK, BLOCK)
+            keys_ref[b, slot * BLOCK : (slot + 1) * BLOCK, :] = rows_ref[slot, pl.ds(offset, BLOCK), :]
 
 
 def each_tile(blocks_here, heads, tile_rows, steps, run):
@@ -107,15 +108,15 @@
         pl.when(lax.div(step, block_rows // tile_rows) == b)(functools.partial(run, [(b, 0, at)]))
 
 
-def early_kernel(n_cross, blocks_here, heads, tile_rows, steps, want_ref, q_ref, g_ref, own_ref, mine_ref, other_ref, keys_ref, scores_ref, gw_ref, grad_ref):
+def early_kernel(n_cross, blocks_here, heads, tile_rows, steps, want_ref, q_ref, g_ref, own_ref, mine_ref, other_ref, keys_ref, scores_ref, gw_ref, grad_ref, rows_ref):
     value_width = g_ref.shape[1]
-    half = blocks_here // 2 * BLOCK
     n_direct = mine_ref.shape[0] - 1
 
     def start():
-        place_slots(keys_ref, want_ref, n_cross, mine_ref, other_ref, 1, want_ref[blocks_here, 0], half)
+        place_slots(keys_ref, rows_ref, want_ref, n_cross, mine_ref, other_ref, 1, want_ref[blocks_here, 0])
+        own = own_ref[...].T
         for b in range(blocks_here):
-            keys_ref[b, n_direct * BLOCK :, :] = own_ref[...]
+            keys_ref[b, n_direct * BLOCK :, :] = own
 
     def run(tiles):
         for b, local, _ in tiles:
@@ -136,15 +137,14 @@
         pl.when(pl.program_id(0) == which)(fn)
 
 
-def score_kernel(n_far, n_cross, blocks_here, heads, tile_rows, steps, want_ref, q_ref, g_ref, bias_ref, early_keys_ref, early_scores_ref, early_gw_ref, mine_ref, other_ref, weights_ref, grads_ref, keys_ref, keep_ref, send_ref, late_keep_ref, late_send_ref, acc_ref, dense_ref):
+def score_kernel(n_far, n_cross, blocks_here, heads, tile_rows, steps, want_ref, q_ref, g_ref, bias_ref, early_keys_ref, early_scores_ref, early_gw_ref, mine_ref, other_ref, weights_ref, grads_ref, keys_ref, keep_ref, send_ref, late_keep_ref, late_send_ref, acc_ref, dense_ref, rows_ref):
     value_width = g_ref.shape[1]
-    half = blocks_here // 2 * BLOCK
     cross_rows = n_cross * BLOCK
     my_half = want_ref[blocks_here, 0]
     far_rows = n_far * BLOCK
 
     def start():
-        place_slots(keys_ref, want_ref, 0, mine_ref, other_ref, 0, my_half, half)
+        place_slots(keys_ref, rows_ref, want_ref, 0, mine_ref, other_ref, 0, my_half)
         keys_ref[:, cross_rows:, :] = early_keys_ref[...]
         if steps > 1:
             acc_ref[...] = jnp.zeros_like(acc_ref)
@@ -163,28 +163,46 @@
     def finish(tile, scores, grad_weights):
         b, _, at = tile
         slots, here = window(tile)
-        count = slots * BLOCK
-        early = count - cross_rows
-        scores = jnp.concatenate([scores, early_scores_ref[:early, here]], axis=0)
-        grad_weights = jnp.concatenate([grad_weights, early_gw_ref[:early, here]], axis=0)
-        scores = scores.reshape(slots, BLOCK, tile_rows)
-        token = lax.div(at, heads) + lax.div(lax.broadcasted_iota(jnp.int32, (1, BLOCK, tile_rows), 2), heads)
-        place = lax.broadcasted_iota(jnp.int32, (1, BLOCK, tile_rows), 1)
-        last = jnp.where(place <= token, scores[slots - 1 :], MASKED)
-        scores = jnp.concatenate([scores[: slots - 1], last], axis=0)
-        bias = bias_ref[:slots, here]
-        top = jnp.max(jnp.max(scores, axis=1) * EXP2_SCALE + bias, axis=0, keepdims=True)
-        raised = jnp.exp2(scores * EXP2_SCALE + (bias - top)[:, None, :]).reshape(count, tile_rows)
-        total = jnp.sum(raised, axis=0, keepdims=True)
-        weights = raised * (1.0 / total)
-        row_delta = jnp.sum(weights * grad_weights, axis=0, keepdims=True)
-        grad_scores = (weights * (grad_weights - row_delta)).astype(jnp.bfloat16)
-        weights_low = weights.astype(jnp.bfloat16)
-        weights_ref[:count, here] = weights_low
-        grads_ref[:count, here] = grad_scores
-        query_part = dot(grad_scores[:far_rows], q_ref[here, :], NN) * softmax_scale
-        grad_part = dot(weights_low[:far_rows], g_ref[here, :], NN)
-        if steps == 1 and at == 0:
+        early = slots * BLOCK - cross_rows
+        token = lax.div(at, heads) + lax.div(lax.broadcasted_iota(jnp.int32, (BLOCK, tile_rows), 1), heads)
+        place = lax.broadcasted_iota(jnp.int32, (BLOCK, tile_rows), 0)
+        last = jnp.where(place <= token, early_scores_ref[early - BLOCK : early, here], MASKED)
+        pieces = [
+            (0, cross_rows, scores, grad_weights),
+            (
+                cross_rows,
+                early - BLOCK,
+                early_scores_ref[: early - BLOCK, here],
+                early_gw_ref[: early - BLOCK, here],
+            ),
+            (cross_rows + early - BLOCK, BLOCK, last, early_gw_ref[early - BLOCK : early, here]),
+        ]
+        pieces = [
+            (first, count, s.reshape(-1, BLOCK, tile_rows), gw) for first, count, s, gw in pieces if count
+        ]
+        biases = [bias_ref[first // BLOCK : (first + count) // BLOCK, here] for first, count, _, _ in pieces]
+        tops = [
+            jnp.max(jnp.max(s, axis=1) * EXP2_SCALE + bias, axis=0, keepdims=True)
+            for (_, _, s, _), bias in zip(pieces, biases)
+        ]
+        top = functools.reduce(jnp.maximum, tops)
+        raised = [
+            jnp.exp2(s * EXP2_SCALE + (bias - top)[:, None, :]).reshape(-1, tile_rows)
+            for (_, _, s, _), bias in zip(pieces, biases)
+        ]
+        total = sum(jnp.sum(r, axis=0, keepdims=True) for r in raised)
+        dots = sum(jnp.sum(r * gw, axis=0, keepdims=True) for r, (_, _, _, gw) in zip(raised, pieces))
+        inverse = 1.0 / total
+        row_delta = dots * inverse
+        for r, (first, count, _, gw) in zip(raised, pieces):
+            weights = r * inverse
+            weights_ref[first : first + count, here] = weights.astype(jnp.bfloat16)
+            grads_ref[first : first + count, here] = (weights * (gw - row_delta)).astype(jnp.bfloat16)
+
+    def gather(b, here):
+        query_part = dot(grads_ref[:far_rows, here], q_ref[here, :], NN) * softmax_scale
+        grad_part = dot(weights_ref[:far_rows, here], g_ref[here, :], NN)
+        if steps == 1:
             acc_ref[b, :, :] = query_part
         else:
             acc_ref[b, :, :] += query_part
@@ -193,14 +211,19 @@
     def run(tiles):
         ready = products(tiles[0])
         for i, tile in enumerate(tiles):
-            coming = products(tiles[i + 1]) if i + 1 < len(tiles) else None
+            last = i + 1 == len(tiles)
+            coming = None if last else products(tiles[i + 1])
             finish(tile, *ready)
             ready = coming
+            b, local, _ = tile
+            if last or tiles[i + 1][0] != b:
+                first = min(t[1] for t in tiles if t[0] == b)
+                gather(b, slice(first, local + tile_rows))
 
     def end():
-        spread_slots(dense_ref, acc_ref, want_ref, list(range(1, n_cross)) + [0] + list(range(n_cross, n_far)))
+        spread_slots(dense_ref, acc_ref, want_ref, range(n_far))
         write_halves(dense_ref, 0, my_half, keep_ref, send_ref)
-        write_halves(dense_ref, n_cross - 1, my_half, late_keep_ref, late_send_ref)
+        write_halves(dense_ref, n_cross, my_half, late_keep_ref, late_send_ref)
 
     at_step(0, steps, start)
     each_tile(blocks_here, heads, tile_rows, steps, run)
@@ -324,7 +347,7 @@
 def early_call(want, query_rows, grad_rows, own, mine, other, n_cross, n_far, heads):
     rows, width = query_rows.shape
     value_width = grad_rows.shape[1]
-    tok_rows = own.shape[0]
+    tok_rows = own.shape[1]
     blocks_here = tok_rows // BLOCK
     keys = (mine.shape[0] - 1) * BLOCK + tok_rows
     tile_rows, steps = tiling(rows, n_far * BLOCK + tok_rows, heads)
@@ -340,7 +363,7 @@
             jax.ShapeDtypeStruct((keys, rows), jnp.float32),
             jax.ShapeDtypeStruct((rows, value_width), jnp.bfloat16),
         ),
-        [],
+        [pltpu.VMEM((mine.shape[0] - 1, tok_rows, width), jnp.bfloat16)],
         rows * keys * (width + value_width),
         rows * (width + value_width) * 4,
         "early_scores",
@@ -355,8 +378,8 @@
     n_cross = mine.shape[0]
     keys = n_far * BLOCK + tok_rows
     tile_rows, steps = tiling(rows, keys, heads)
-    now = jax.ShapeDtypeStruct((n_cross - 1, tok_rows // 2, width), jnp.bfloat16)
-    late = jax.ShapeDtypeStruct((n_far - n_cross + 1, tok_rows // 2, width), jnp.bfloat16)
+    now = jax.ShapeDtypeStruct((n_cross, width // 2, tok_rows), jnp.bfloat16)
+    late = jax.ShapeDtypeStruct((n_far - n_cross, width // 2, tok_rows), jnp.bfloat16)
     early_keys = early[0].shape[1]
     key_shape = (blocks_here, keys, width)
     return whole_call(
@@ -385,6 +408,7 @@
         [
             pltpu.VMEM((blocks_here, n_far * BLOCK, width), jnp.float32),
             pltpu.VMEM((n_far, tok_rows, width), jnp.float32),
+            pltpu.VMEM((n_cross, tok_rows, width), jnp.bfloat16),
         ],
         rows * keys * 2 * (width + value_width),
         rows * (width + value_width) * 4,
@@ -397,7 +421,7 @@
     rows, width = query_rows.shape
     value_width = grad_rows.shape[1]
     blocks_here = tok_rows // BLOCK
-    half = jax.ShapeDtypeStruct((1, tok_rows // 2, width), jnp.bfloat16)
+    half = jax.ShapeDtypeStruct((1, width // 2, tok_rows), jnp.bfloat16)
     return whole_call(
         functools.partial(grad_kernel, n_far, blocks_here, heads),
         [None] * 4,
@@ -441,7 +465,7 @@
     my_shard = lax.axis_index("ctx")
     my_half = lax.axis_index("head") % 2
     blocks_here = tok_rows // BLOCK
-    half = tok_rows // 2
+    half = width // 2
     lines = shards // 2
     partner = [(i, i ^ 1) for i in range(groups)]
     across = [(i, i ^ 1) for i in range(shards)]
@@ -464,7 +488,8 @@
     )
     grad_rows = cotangent.reshape(tok_rows * heads, value_width)
 
-    held = lax.dynamic_slice_in_dim(latent, my_half * half, half, 0)[None]
+    turned = latent.T
+    held = lax.dynamic_slice_in_dim(turned, my_half * half, half, 0)[None]
     pieces = [held] + [up(held, k) for k in offsets]
     bias, want = table_call(place, selection.T, n_far, heads)
     *pieces, bias, want, queries = lax.optimization_barrier((*pieces, bias, want, queries))
@@ -473,7 +498,7 @@
     cross = lax.ppermute(mine, "ctx", across)
     query_rows = queries.reshape(tok_rows * heads, width)
     *early, grad_rows = early_call(
-        want, query_rows, grad_rows, latent, mine, swap(mine), n_cross, n_far, heads
+        want, query_rows, grad_rows, turned, mine, swap(mine), n_cross, n_far, heads
     )
     cross, early[1] = lax.optimization_barrier((cross, early[1]))
     weights, grads, keys, keep, send, late_keep, late_send = score_call(
@@ -482,20 +507,20 @@
 
     moving = (keep.astype(jnp.float32) + swap(send).astype(jnp.float32)).astype(jnp.bfloat16)
     moving, weights, late_send = lax.optimization_barrier((moving, weights, late_send))
-    arrived = lax.ppermute(moving, "ctx", across)
+    arrived = lax.ppermute(moving, "ctx", across).astype(jnp.float32)
+    late_send, weights = lax.optimization_barrier((swap(late_send), weights))
+    own_keep, own_send = grad_call(want, query_rows, grad_rows, weights, grads, n_far, heads, tok_rows)
+    own_send, weights = lax.optimization_barrier((own_send, weights))
+    late = late_keep.astype(jnp.float32) + late_send.astype(jnp.float32)
+    own = own_keep.astype(jnp.float32) + swap(own_send).astype(jnp.float32)
     attended, grad_queries = out_call(keys, weights, grads, n_far, heads, value_width)
-    late = late_keep.astype(jnp.float32) + swap(late_send).astype(jnp.float32)
-    total = (late[1:] + arrived.astype(jnp.float32)).astype(jnp.bfloat16)
-    late_own = late[:1].astype(jnp.bfloat16)
-    total, late_own, grad_queries, weights = lax.optimization_barrier((total, late_own, grad_queries, weights))
+    leaving = [(late[i] + arrived[i + 1]).astype(jnp.bfloat16) for i in range(n_far - n_cross)]
+    total = own[0] + arrived[0]
+    *leaving, total, grad_queries = lax.optimization_barrier((*leaving, total, grad_queries))
     grad_queries = grad_queries.reshape(tok_rows, heads, width).transpose(1, 2, 0)
-    moved = [down(total[i : i + 1], k) for i, k in enumerate(offsets)]
-    keep, send = grad_call(want, query_rows, grad_rows, weights, grads, n_far, heads, tok_rows)
-    total = keep.astype(jnp.float32) + swap(send).astype(jnp.float32)
-    total = total + lax.ppermute(late_own, "ctx", across).astype(jnp.float32)
-    for part in moved:
+    for part in [down(rows, k) for rows, k in zip(leaving, offsets)]:
         total = total + part.astype(jnp.float32)
-    low = total[0].astype(jnp.bfloat16)
+    low = total.astype(jnp.bfloat16)
     low, grad_queries = lax.optimization_barrier((low, grad_queries))
     summed = low.astype(jnp.float32)
     for j in range(1, groups // 2):
@@ -510,7 +535,7 @@
     return (
         attended.reshape(tok_rows, heads, value_width),
         grad_queries.transpose(2, 0, 1),
-        grad_latent,
+        grad_latent.T,
     )
 
 

time: 69 us -> 65.4 us (0.948)
  local copies, waits for them, and re-layouts: 16 us -> 10.2 us
  other arithmetic: 1.7 us -> 2.45 us
  waiting for transfers between devices: 12.1 us -> 12.8 us
    unnamed x12 -> x6, local copies, waits for them, and re-layouts: 6.2 us -> 2.28 us
    reshape x1, local copies, waits for them, and re-layouts: 4.68 us -> 3.1 us  [body(): grad_queries.reshape(tok_rows, heads, width).transpose(1, 2, 0)]
    dynamic_slice x2 -> x0, local copies, waits for them, and re-layouts: 1.16 us -> none  [body(): held = lax.dynamic_slice_in_dim(latent, my_half * half, half, 0)[None]]
    ppermute x3, waiting for transfers between devices: 3.67 us -> 4.82 us  [down(): lax.ppermute(rows, 'ctx', [(i + 2 * hops, i) for i in range(shards - 2 *...]
    broadcast_in_dim x0 -> x1, local copies, waits for them, and re-layouts: none -> 0.89 us  [body(): held = lax.dynamic_slice_in_dim(turned, my_half * half, half, 0)[None]]
    transpose x0 -> x1, other arithmetic: none -> 0.73 us  [body(): return (attended.reshape(tok_rows, heads, value_width), grad_queries.tran...]
  transfers between devices with their start and end apart: 16 -> 15, of which waited for: 7 -> 8; matrix products, arithmetic and copies ran while one was open for 16% -> 13% of each run, Pallas kernels for 13% -> 17%
where the time goes in v3:
time: 65.4 us; the launch traced here: 65 us
  starting transfers between devices  20.1 us (31%)
  Pallas kernels  18.6 us (28%)
  waiting for transfers between devices  12.8 us (20%)
  local copies, waits for them, and re-layouts  10.2 us (16%)
  other arithmetic  2.45 us (4%)
  between operations  0.87 us (1%)
    ppermute x3, starting transfers between devices, up(): lax.ppermute(rows, 'ctx', [(i, i + 2 * hops) for i in range(shards - 2 *...  10.7 us
    pallas_call x1, Pallas kernels, score_call(): whole_call(functools.partial(score_kernel, n_far, n_cross, blocks_here, h...  7.71 us
    pallas_call x1, Pallas kernels, out_call(): call(functools.partial(out_kernel, n_far, blocks_here, heads), rows // ti...  5.3 us
    ppermute x3, waiting for transfers between devices, down(): lax.ppermute(rows, 'ctx', [(i + 2 * hops, i) for i in range(shards - 2 *...  4.82 us
    ppermute x6, waiting for transfers between devices, swap(): return lax.ppermute(rows, 'head', partner)  4.4 us
    optimization_barrier x1, local copies, waits for them, and re-layouts, body(): mine, queries = lax.optimization_barrier((mine, queries))  3.91 us
    ppermute x3, starting transfers between devices, down(): lax.ppermute(rows, 'ctx', [(i + 2 * hops, i) for i in range(shards - 2 *...  3.88 us
    reshape x1, local copies, waits for them, and re-layouts, body(): grad_queries.reshape(tok_rows, heads, width).transpose(1, 2, 0)  3.1 us
  transfers between devices with their start and end apart: 15, of which 8 were waited for; matrix products, arithmetic and copies ran while one was open for 13% of the time, Pallas kernels for 17%

profile of v3, /device:TPU:0, one launch (start us, length us, event | category | flops | bytes accessed | tf_op | source)
XLA Modules:
  0.0 65.0 jit_solution(10539726183970149533)
XLA Ops:
  0.6 0.9 %dynamic-slice_bitcast_fusion.refs_0_ = bf16[1,288,128]{2,1,0:T(8,128)(2,1)S(1)} fusion(bf16[128,576]{0,1:T(8,128)(2,1)} %param.7, s32[]{:T(128)S(6)} %select_n.19), kind=kLoop, calls=%fused_computation.17 | loop fusion | bytes 147460 | tf_op jit(solution)/shard_map/broadcast_in_dim | solution.py:492
  1.5 6.9 %collective-permute-start.2 = (bf16[1,288,128]{2,1,0:T(8,128)(2,1)S(1)}, bf16[1,288,128]{2,1,0:T(8,128)(2,1)S(1)}, u32[]{:S(2)}, u32[]{:S(2)}) collective-permute-start(bf16[1,288,128]{2,1,0:T(8,128)(2,1)S(1)} %dynamic-slice_bitcast_fusion.refs_0_), channel_id=1, source_target_pairs={{0,24},{4,28},{1,25},{5,29},{2,26},{6,30},{3,27},{7,31}} | collective-permute-start | bytes 221192 | tf_op jit(solution)/shard_map/ppermute | solution.py:477
  8.5 1.3 %collective-permute-start.1 = (bf16[1,288,128]{2,1,0:T(8,128)(2,1)S(1)}, bf16[1,288,128]{2,1,0:T(8,128)(2,1)S(1)}, u32[]{:S(2)}, u32[]{:S(2)}) collective-permute-start(bf16[1,288,128]{2,1,0:T(8,128)(2,1)S(1)} %dynamic-slice_bitcast_fusion.refs_0_), channel_id=1, source_target_pairs={{0,8},{4,12},{8,16},{12,20},{16,24},{20,28},{1,9},{5,13},{9,17},{1... | collective-permute-start | bytes 221192 | tf_op jit(solution)/shard_map/ppermute | solution.py:477
  9.8 2.5 %collective-permute-start = (bf16[1,288,128]{2,1,0:T(8,128)(2,1)S(1)}, bf16[1,288,128]{2,1,0:T(8,128)(2,1)S(1)}, u32[]{:S(2)}, u32[]{:S(2)}) collective-permute-start(bf16[1,288,128]{2,1,0:T(8,128)(2,1)S(1)} %dynamic-slice_bitcast_fusion.refs_0_), channel_id=1, source_target_pairs={{0,16},{4,20},{8,24},{12,28},{1,17},{5,21},{9,25},{13,29},{2,18},{... | collective-permute-start | bytes 221192 | tf_op jit(solution)/shard_map/ppermute | solution.py:477
  12.3 0.7 %broadcast_add_fusion = s32[3]{0:T(128)S(1)} fusion(s32[3]{0:T(128)} %constant.39, s32[]{:T(128)} %axis_index.25), kind=kLoop, calls=%fused_computation.19 | loop fusion | flops 3 | bytes 28 | tf_op jit(solution)/shard_map/sub | solution.py:484
  12.9 0.7 %broadcast_add_fusion.1 = s32[4]{0:T(128)S(1)} fusion(s32[4]{0:T(128)} %constant.38, s32[]{:T(128)S(6)} %xor.3), kind=kLoop, calls=%fused_computation.20 | loop fusion | flops 4 | bytes 36 | tf_op jit(solution)/shard_map/sub | solution.py:483
  13.6 0.1 pad_add_fusion.place_ref
  13.7 0.0 copy-start.2
  13.7 0.7 %copy-done.2 = s32[128,8]{0,1:T(8,128)S(1)} copy-done((s32[128,8]{0,1:T(8,128)S(1)}, s32[128,8]{0,1:T(8,128)}, u32[]{:S(2)}) %copy-start.2) | copy-done | bytes 4120
  14.4 1.4 %table.1 = (f32[9,2048]{1,0:T(8,128)S(1)}, s32[3,7]{1,0:T(4,128)S(1)}) custom-call(s32[9]{0:T(128)S(1)} %pad_add_fusion.place_ref, s32[8,128]{1,0:T(8,128)S(1)} %bitcast.30), custom_call_target="tpu_custom_call" | custom-call | tf_op jit(solution)/shard_map/table/pallas_call | solution.py:322
  15.8 0.0 collective-permute-done.2.refs_3_
  15.8 0.0 collective-permute-done.1.refs_2_
  15.8 0.0 collective-permute-done.refs_1_
  15.8 0.0 copy-start.1
  15.8 0.1 collective-permute-start.3
  15.9 1.6 %collective-permute-start.4 = (bf16[4,288,128]{2,1,0:T(8,128)(2,1)S(1)}, bf16[4,288,128]{2,1,0:T(8,128)(2,1)}, u32[]{:S(2)}, u32[]{:S(2)}) collective-permute-start(bf16[4,288,128]{2,1,0:T(8,128)(2,1)S(1)} %join.1.mine_ref), channel_id=1, source_target_pairs={{0,4},{4,0},{8,12},{12,8},{16,20},{20,16},{24,28},{28,24},{1,5},{5... | collective-permute-start | bytes 884744 | tf_op jit(solution)/shard_map/ppermute | solution.py:498
  17.5 3.9 %copy.9 = bf16[128,16,576]{2,1,0:T(8,128)(2,1)S(1)} copy(bf16[128,16,576]{0,2,1:T(8,128)(2,1)} %param.6) | data formatting | bytes 4718592 | tf_op jit(solution)/shard_map/optimization_barrier | solution.py:497
  21.4 0.0 collective-permute-done.3.other_ref
  21.4 0.0 copy-done.1
  21.4 0.0 copy-start
  21.4 1.6 %copy-done = bf16[128,16,512]{2,1,0:T(8,128)(2,1)S(1)} copy-done((bf16[128,16,512]{2,1,0:T(8,128)(2,1)S(1)}, bf16[128,16,512]{2,1,0:T(8,128)(2,1)}, u32[]{:S(2)}) %copy-start) | copy-done | bytes 2097176
  23.0 2.6 %early_scores.1 = (bf16[2,320,576]{2,1,0:T(8,128)(2,1)S(1)}, f32[320,2048]{1,0:T(8,128)S(1)}, f32[320,2048]{1,0:T(8,128)S(1)}, bf16[2048,512]{1,0:T(8,128)(2,1)S(1)}) custom-call(s32[3,7]{1,0:T(4,128)S(1)} %get-tuple-element.47.want_ref, bf16[2048,576]{1,0:T(8,128)(2,1)S(1)} %bitcast.24, bf16[2048,512]{1,0:T(8,128)(2,1)S(1)} %bitcast.28, ...), custom_call_target="tpu_custom_call" | custom-call | flops 1426063360 | bytes 8912896 | tf_op jit(solution)/shard_map/early_scores/pallas_call | solution.py:356
  25.6 0.0 collective-permute-done.4.mine_ref
  25.6 0.2 collective-permute-start.5
  25.8 1.6 %collective-permute-done.5.other_ref = bf16[4,288,128]{2,1,0:T(8,128)(2,1)S(1)} collective-permute-done((bf16[4,288,128]{2,1,0:T(8,128)(2,1)}, bf16[4,288,128]{2,1,0:T(8,128)(2,1)S(1)}, u32[]{:S(2)}, u32[]{:S(2)}) %collective-permute-start.5) | collective-permute-done | bytes 294944 | tf_op jit(solution)/shard_map/ppermute | solution.py:474
  27.4 7.7 %scores.1 = (bf16[576,2048]{1,0:T(8,128)(2,1)S(1)}, bf16[576,2048]{1,0:T(8,128)(2,1)S(1)}, bf16[2,576,576]{2,1,0:T(8,128)(2,1)S(1)}, bf16[4,288,128]{2,1,0:T(8,1...) custom-call(s32[3,7]{1,0:T(4,128)S(1)} %get-tuple-element.47.want_re, ...), custom_call_target="tpu_custom_call" | custom-call | flops 5133828096 | bytes 8912896 | tf_op jit(solution)/shard_map/scores/pallas_call | solution.py:385
  35.2 0.2 collective-permute-start.6
  35.4 1.4 %collective-permute-done.6 = bf16[4,288,128]{2,1,0:T(8,128)(2,1)S(1)} collective-permute-done((bf16[4,288,128]{2,1,0:T(8,128)(2,1)S(1)}, bf16[4,288,128]{2,1,0:T(8,128)(2,1)S(1)}, u32[]{:S(2)}, u32[]{:S(2)}) %collective-permute-start.6) | collective-permute-done | bytes 294944 | tf_op jit(solution)/shard_map/ppermute | solution.py:474
  36.8 0.1 add_convert_fusion
  36.9 0.2 collective-permute-start.7
  37.1 1.3 %collective-permute-start.8 = (bf16[4,288,128]{2,1,0:T(8,128)(2,1)S(1)}, bf16[4,288,128]{2,1,0:T(8,128)(2,1)S(1)}, u32[]{:S(2)}, u32[]{:S(2)}) collective-permute-start(bf16[4,288,128]{2,1,0:T(8,128)(2,1)S(1)} %add_convert_fusion), channel_id=1, source_target_pairs={{0,4},{4,0},{8,12},{12,8},{16,20},{20,16},{24,28},{28,24},{1,5},{5... | collective-permute-start | bytes 884744 | tf_op jit(solution)/shard_map/ppermute | solution.py:510
  38.4 0.0 collective-permute-done.7
  38.4 1.6 %own_grads.1 = (bf16[1,288,128]{2,1,0:T(8,128)(2,1)S(1)}, bf16[1,288,128]{2,1,0:T(8,128)(2,1)S(1)}) custom-call(s32[3,7]{1,0:T(4,128)S(1)} %get-tuple-element.47.want_ref, bf16[2048,576]{1,0:T(8,128)(2,1)S(1)} %bitcast.26, bf16[2048,512]{1,0:T(8,128)(2,1)S(1)} %get-tuple-element.55.g_ref, bf16[576,2048]{1,0:T(8,128)(2,1)S(1)} %get-tuple-element.72.weights_ref, ...), custom_call_target="tpu_custom_call" | custom-call | flops 570425344 | bytes 8912896 | tf_op jit(solution)/shard_map/own_grads/pallas_call | solution.py:425
  40.0 0.2 collective-permute-start.9
  40.3 5.3 %outputs.1 = (bf16[2048,512]{1,0:T(8,128)(2,1)}, bf16[2048,576]{1,0:T(8,128)(2,1)S(1)}) custom-call(bf16[2,576,576]{2,1,0:T(8,128)(2,1)S(1)} %get-tuple-element.62.keys_ref, bf16[576,2048]{1,0:T(8,128)(2,1)S(1)} %get-tuple-element.72.weights_ref, bf16[576,2048]{1,0:T(8,128)(2,1)S(1)} %get-tuple-element.70.grads_ref), custom_call_target="tpu_custom_call" | custom-call | flops 2566914048 | bytes 8912896 | tf_op jit(solution)/shard_map/outputs/pallas_call | solution.py:444
  45.6 0.7 %collective-permute-done.8 = bf16[4,288,128]{2,1,0:T(8,128)(2,1)S(1)} collective-permute-done((bf16[4,288,128]{2,1,0:T(8,128)(2,1)S(1)}, bf16[4,288,128]{2,1,0:T(8,128)(2,1)S(1)}, u32[]{:S(2)}, u32[]{:S(2)}) %collective-permute-start.8) | collective-permute-done | bytes 294944 | tf_op jit(solution)/shard_map/ppermute | solution.py:510
  46.4 0.0 collective-permute-done.9
  46.4 0.1 fusion.7
  46.5 1.3 %collective-permute-start.10 = (bf16[288,128]{1,0:T(8,128)(2,1)S(1)}, bf16[288,128]{1,0:T(8,128)(2,1)S(1)}, u32[]{:S(2)}, u32[]{:S(2)}) collective-permute-start(bf16[288,128]{1,0:T(8,128)(2,1)S(1)} %get-tuple-element.81), channel_id=1, source_target_pairs={{16,0},{20,4},{24,8},{28,12},{17,1},{21,5},{25,9},{29,13},{18,2},{... | collective-permute-start | bytes 221192 | tf_op jit(solution)/shard_map/ppermute | solution.py:480
  47.8 1.3 %collective-permute-start.11 = (bf16[288,128]{1,0:T(8,128)(2,1)S(1)}, bf16[288,128]{1,0:T(8,128)(2,1)S(1)}, u32[]{:S(2)}, u32[]{:S(2)}) collective-permute-start(bf16[288,128]{1,0:T(8,128)(2,1)S(1)} %get-tuple-element.82), channel_id=1, source_target_pairs={{8,0},{12,4},{16,8},{20,12},{24,16},{28,20},{9,1},{13,5},{17,9},{2... | collective-permute-start | bytes 221192 | tf_op jit(solution)/shard_map/ppermute | solution.py:480
  49.1 1.3 %collective-permute-start.12 = (bf16[288,128]{1,0:T(8,128)(2,1)S(1)}, bf16[288,128]{1,0:T(8,128)(2,1)S(1)}, u32[]{:S(2)}, u32[]{:S(2)}) collective-permute-start(bf16[288,128]{1,0:T(8,128)(2,1)S(1)} %get-tuple-element.83), channel_id=1, source_target_pairs={{24,0},{28,4},{25,1},{29,5},{26,2},{30,6},{27,3},{31,7}} | collective-permute-start | bytes 221192 | tf_op jit(solution)/shard_map/ppermute | solution.py:480
  50.4 3.1 %copy.10 = bf16[128,16,576]{0,2,1:T(8,128)(2,1)} copy(bf16[128,16,576]{2,1,0:T(8,128)(2,1)S(1)} %bitcast.27) | data formatting | bytes 4718592 | tf_op jit(solution)/shard_map/reshape | solution.py:520
  53.5 0.9 %collective-permute-done.10 = bf16[288,128]{1,0:T(8,128)(2,1)S(1)} collective-permute-done((bf16[288,128]{1,0:T(8,128)(2,1)S(1)}, bf16[288,128]{1,0:T(8,128)(2,1)S(1)}, u32[]{:S(2)}, u32[]{:S(2)}) %collective-permute-start.10) | collective-permute-done | bytes 73760 | tf_op jit(solution)/shard_map/ppermute | solution.py:480
  54.4 0.4 collective-permute-done.11
  54.8 3.6 %collective-permute-done.12 = bf16[288,128]{1,0:T(8,128)(2,1)S(1)} collective-permute-done((bf16[288,128]{1,0:T(8,128)(2,1)S(1)}, bf16[288,128]{1,0:T(8,128)(2,1)S(1)}, u32[]{:S(2)}, u32[]{:S(2)}) %collective-permute-start.12) | collective-permute-done | bytes 73760 | tf_op jit(solution)/shard_map/ppermute | solution.py:480
  58.4 1.6 %collective-permute-start.13 = (bf16[288,128]{1,0:T(8,128)(2,1)S(1)}, bf16[288,128]{1,0:T(8,128)(2,1)S(1)}, u32[]{:S(2)}, u32[]{:S(2)}) collective-permute-start(bf16[288,128]{1,0:T(8,128)(2,1)S(1)} %add_convert_fusion.1), channel_id=1, source_target_pairs={{0,2},{1,3},{2,0},{3,1},{4,6},{5,7},{6,4},{7,5},{8,10},{9,11},{10,... | collective-permute-start | bytes 221192 | tf_op jit(solution)/shard_map/ppermute | solution.py:527
  60.0 2.8 %collective-permute-done.13 = bf16[288,128]{1,0:T(8,128)(2,1)S(1)} collective-permute-done((bf16[288,128]{1,0:T(8,128)(2,1)S(1)}, bf16[288,128]{1,0:T(8,128)(2,1)S(1)}, u32[]{:S(2)}, u32[]{:S(2)}) %collective-permute-start.13) | collective-permute-done | bytes 73760 | tf_op jit(solution)/shard_map/ppermute | solution.py:527
  62.8 0.1 collective-permute-start.14
  62.9 1.4 %collective-permute-done.14 = f32[288,128]{1,0:T(8,128)S(1)} collective-permute-done((f32[288,128]{1,0:T(8,128)S(1)}, f32[288,128]{1,0:T(8,128)S(1)}, u32[]{:S(2)}, u32[]{:S(2)}) %collective-permute-start.14) | collective-permute-done | bytes 147488 | tf_op jit(solution)/shard_map/ppermute | solution.py:474
  64.3 0.7 %fusion = f32[128,576]{0,1:T(8,128)} fusion(f32[288,128]{1,0:T(8,128)S(1)} %collective-permute-done.14, f32[288,128]{1,0:T(8,128)S(1)} %convert_add_fusion.1, pred[]{:T(512)S(6)} %eq.5), kind=kLoop, calls=%fused_computation.3 | loop fusion | flops 221184 | bytes 589825 | tf_op jit(solution)/shard_map/transpose | solution.py:538
  (5 shorter events, 0.2 us)
Async XLA Ops:
  1.5 14.2 %collective-permute-start.2 = (bf16[1,288,128]{2,1,0:T(8,128)(2,1)S(1)}, bf16[1,288,128]{2,1,0:T(8,128)(2,1)S(1)}, u32[]{:S(2)}, u32[]{:S(2)}) collective-permute-start(bf16[1,288,128]{2,1,0:T(8,128)(2,1)S(1)} %dynamic-slice_bitcast_fusion.refs_0_), channel_id=1, source_target_pairs={{0,24},{4,28},{1,25},{5,29},{2,26},{6,30},{3,27},{7,31}} | collective-permute-start | bytes 221192 | tf_op jit(solution)/shard_map/ppermute | solution.py:477
  8.5 7.3 %collective-permute-start.1 = (bf16[1,288,128]{2,1,0:T(8,128)(2,1)S(1)}, bf16[1,288,128]{2,1,0:T(8,128)(2,1)S(1)}, u32[]{:S(2)}, u32[]{:S(2)}) collective-permute-start(bf16[1,288,128]{2,1,0:T(8,128)(2,1)S(1)} %dynamic-slice_bitcast_fusion.refs_0_), channel_id=1, source_target_pairs={{0,8},{4,12},{8,16},{12,20},{16,24},{20,28},{1,9},{5,13},{9,17},{1... | collective-permute-start | bytes 221192 | tf_op jit(solution)/shard_map/ppermute | solution.py:477
  9.8 6.0 %collective-permute-start = (bf16[1,288,128]{2,1,0:T(8,128)(2,1)S(1)}, bf16[1,288,128]{2,1,0:T(8,128)(2,1)S(1)}, u32[]{:S(2)}, u32[]{:S(2)}) collective-permute-start(bf16[1,288,128]{2,1,0:T(8,128)(2,1)S(1)} %dynamic-slice_bitcast_fusion.refs_0_), channel_id=1, source_target_pairs={{0,16},{4,20},{8,24},{12,28},{1,17},{5,21},{9,25},{13,29},{2,18},{... | collective-permute-start | bytes 221192 | tf_op jit(solution)/shard_map/ppermute | solution.py:477
  13.7 0.7 %copy-start.2 = (s32[128,8]{0,1:T(8,128)S(1)}, s32[128,8]{0,1:T(8,128)}, u32[]{:S(2)}) copy-start(s32[128,8]{0,1:T(8,128)} %param.9) | copy-start | bytes 12292
  15.8 5.6 %copy-start.1 = (bf16[128,576]{0,1:T(8,128)(2,1)S(1)}, bf16[128,576]{0,1:T(8,128)(2,1)}, u32[]{:S(2)}) copy-start(bf16[128,576]{0,1:T(8,128)(2,1)} %param.7) | copy-start | bytes 442372
  15.8 5.6 %collective-permute-start.3 = (bf16[4,288,128]{2,1,0:T(8,128)(2,1)S(1)}, bf16[4,288,128]{2,1,0:T(8,128)(2,1)S(1)}, u32[]{:S(2)}, u32[]{:S(2)}) collective-permute-start(bf16[4,288,128]{2,1,0:T(8,128)(2,1)S(1)} %join.1.mine_ref), channel_id=1, source_target_pairs={{0,1},{1,0},{2,3},{3,2},{4,5},{5,4},{6,7},{7,6},{8,9},{9,8},{10,11... | collective-permute-start | bytes 884744 | tf_op jit(solution)/shard_map/ppermute | solution.py:474
  15.9 9.7 %collective-permute-start.4 = (bf16[4,288,128]{2,1,0:T(8,128)(2,1)S(1)}, bf16[4,288,128]{2,1,0:T(8,128)(2,1)}, u32[]{:S(2)}, u32[]{:S(2)}) collective-permute-start(bf16[4,288,128]{2,1,0:T(8,128)(2,1)S(1)} %join.1.mine_ref), channel_id=1, source_target_pairs={{0,4},{4,0},{8,12},{12,8},{16,20},{20,16},{24,28},{28,24},{1,5},{5... | collective-permute-start | bytes 884744 | tf_op jit(solution)/shard_map/ppermute | solution.py:498
  21.4 1.6 %copy-start = (bf16[128,16,512]{2,1,0:T(8,128)(2,1)S(1)}, bf16[128,16,512]{2,1,0:T(8,128)(2,1)}, u32[]{:S(2)}) copy-start(bf16[128,16,512]{2,1,0:T(8,128)(2,1)} %param.8) | copy-start | bytes 6291460
  25.6 1.9 %collective-permute-start.5 = (bf16[4,288,128]{2,1,0:T(8,128)(2,1)}, bf16[4,288,128]{2,1,0:T(8,128)(2,1)S(1)}, u32[]{:S(2)}, u32[]{:S(2)}) collective-permute-start(bf16[4,288,128]{2,1,0:T(8,128)(2,1)} %collective-permute-done.4.mine_ref), channel_id=1, source_target_pairs={{0,1},{1,0},{2,3},{3,2},{4,5},{5,4},{6,7},{7,6},{8,9},{9,8},{10,11... | collective-permute-start | bytes 884744 | tf_op jit(solution)/shard_map/ppermute | solution.py:474
  35.2 1.6 %collective-permute-start.6 = (bf16[4,288,128]{2,1,0:T(8,128)(2,1)S(1)}, bf16[4,288,128]{2,1,0:T(8,128)(2,1)S(1)}, u32[]{:S(2)}, u32[]{:S(2)}) collective-permute-start(bf16[4,288,128]{2,1,0:T(8,128)(2,1)S(1)} %get-tuple-element.64), channel_id=1, source_target_pairs={{0,1},{1,0},{2,3},{3,2},{4,5},{5,4},{6,7},{7,6},{8,9},{9,8},{10,11... | collective-permute-start | bytes 884744 | tf_op jit(solution)/shard_map/ppermute | solution.py:474
  36.9 1.5 %collective-permute-start.7 = (bf16[3,288,128]{2,1,0:T(8,128)(2,1)S(1)}, bf16[3,288,128]{2,1,0:T(8,128)(2,1)S(1)}, u32[]{:S(2)}, u32[]{:S(2)}) collective-permute-start(bf16[3,288,128]{2,1,0:T(8,128)(2,1)S(1)} %get-tuple-element.67), channel_id=1, source_target_pairs={{0,1},{1,0},{2,3},{3,2},{4,5},{5,4},{6,7},{7,6},{8,9},{9,8},{10,11... | collective-permute-start | bytes 663560 | tf_op jit(solution)/shard_map/ppermute | solution.py:474
  37.1 9.2 %collective-permute-start.8 = (bf16[4,288,128]{2,1,0:T(8,128)(2,1)S(1)}, bf16[4,288,128]{2,1,0:T(8,128)(2,1)S(1)}, u32[]{:S(2)}, u32[]{:S(2)}) collective-permute-start(bf16[4,288,128]{2,1,0:T(8,128)(2,1)S(1)} %add_convert_fusion), channel_id=1, source_target_pairs={{0,4},{4,0},{8,12},{12,8},{16,20},{20,16},{24,28},{28,24},{1,5},{5... | collective-permute-start | bytes 884744 | tf_op jit(solution)/shard_map/ppermute | solution.py:510
  40.0 6.4 %collective-permute-start.9 = (bf16[1,288,128]{2,1,0:T(8,128)(2,1)S(1)}, bf16[1,288,128]{2,1,0:T(8,128)(2,1)S(1)}, u32[]{:S(2)}, u32[]{:S(2)}) collective-permute-start(bf16[1,288,128]{2,1,0:T(8,128)(2,1)S(1)} %get-tuple-element.78), channel_id=1, source_target_pairs={{0,1},{1,0},{2,3},{3,2},{4,5},{5,4},{6,7},{7,6},{8,9},{9,8},{10,11... | collective-permute-start | bytes 221192 | tf_op jit(solution)/shard_map/ppermute | solution.py:474
  46.5 7.9 %collective-permute-start.10 = (bf16[288,128]{1,0:T(8,128)(2,1)S(1)}, bf16[288,128]{1,0:T(8,128)(2,1)S(1)}, u32[]{:S(2)}, u32[]{:S(2)}) collective-permute-start(bf16[288,128]{1,0:T(8,128)(2,1)S(1)} %get-tuple-element.81), channel_id=1, source_target_pairs={{16,0},{20,4},{24,8},{28,12},{17,1},{21,5},{25,9},{29,13},{18,2},{... | collective-permute-start | bytes 221192 | tf_op jit(solution)/shard_map/ppermute | solution.py:480
  47.8 6.9 %collective-permute-start.11 = (bf16[288,128]{1,0:T(8,128)(2,1)S(1)}, bf16[288,128]{1,0:T(8,128)(2,1)S(1)}, u32[]{:S(2)}, u32[]{:S(2)}) collective-permute-start(bf16[288,128]{1,0:T(8,128)(2,1)S(1)} %get-tuple-element.82), channel_id=1, source_target_pairs={{8,0},{12,4},{16,8},{20,12},{24,16},{28,20},{9,1},{13,5},{17,9},{2... | collective-permute-start | bytes 221192 | tf_op jit(solution)/shard_map/ppermute | solution.py:480
  49.1 9.2 %collective-permute-start.12 = (bf16[288,128]{1,0:T(8,128)(2,1)S(1)}, bf16[288,128]{1,0:T(8,128)(2,1)S(1)}, u32[]{:S(2)}, u32[]{:S(2)}) collective-permute-start(bf16[288,128]{1,0:T(8,128)(2,1)S(1)} %get-tuple-element.83), channel_id=1, source_target_pairs={{24,0},{28,4},{25,1},{29,5},{26,2},{30,6},{27,3},{31,7}} | collective-permute-start | bytes 221192 | tf_op jit(solution)/shard_map/ppermute | solution.py:480
  58.4 4.4 %collective-permute-start.13 = (bf16[288,128]{1,0:T(8,128)(2,1)S(1)}, bf16[288,128]{1,0:T(8,128)(2,1)S(1)}, u32[]{:S(2)}, u32[]{:S(2)}) collective-permute-start(bf16[288,128]{1,0:T(8,128)(2,1)S(1)} %add_convert_fusion.1), channel_id=1, source_target_pairs={{0,2},{1,3},{2,0},{3,1},{4,6},{5,7},{6,4},{7,5},{8,10},{9,11},{10,... | collective-permute-start | bytes 221192 | tf_op jit(solution)/shard_map/ppermute | solution.py:527
  62.8 1.4 %collective-permute-start.14 = (f32[288,128]{1,0:T(8,128)S(1)}, f32[288,128]{1,0:T(8,128)S(1)}, u32[]{:S(2)}, u32[]{:S(2)}) collective-permute-start(f32[288,128]{1,0:T(8,128)S(1)} %convert_add_fusion.1), channel_id=1, source_target_pairs={{0,1},{1,0},{2,3},{3,2},{4,5},{5,4},{6,7},{7,6},{8,9},{9,8},{10,11... | collective-permute-start | bytes 442376 | tf_op jit(solution)/shard_map/ppermute | solution.py:474

commit v4 on v3

--- a/solution.py
+++ b/solution.py
@@ -34,12 +34,12 @@
         pl.when(which == b)(functools.partial(tile, b))
 
 
-def spread_slots(dense_ref, acc_ref, want_ref, slots):
+def spread_slots(dense_ref, acc_ref, want_ref, first, count):
     dense_ref[...] = jnp.zeros_like(dense_ref)
     for b in range(acc_ref.shape[0]):
-        for at, slot in enumerate(slots):
-            offset = pl.multiple_of(want_ref[b, slot] * BLOCK, BLOCK)
-            dense_ref[at, pl.ds(offset, BLOCK), :] += acc_ref[b, slot * BLOCK : (slot + 1) * BLOCK, :]
+        for at in range(count):
+            offset = pl.multiple_of(want_ref[b, first + at] * BLOCK, BLOCK)
+            dense_ref[at, pl.ds(offset, BLOCK), :] += acc_ref[b, at * BLOCK : (at + 1) * BLOCK, :]
 
 
 def write_halves(dense_ref, at, my_half, keep_ref, send_ref):
@@ -141,7 +141,7 @@
     value_width = g_ref.shape[1]
     cross_rows = n_cross * BLOCK
     my_half = want_ref[blocks_here, 0]
-    far_rows = n_far * BLOCK
+    now_rows = (n_cross + 1) * BLOCK
 
     def start():
         place_slots(keys_ref, rows_ref, want_ref, 0, mine_ref, other_ref, 0, my_half)
@@ -200,8 +200,8 @@
             grads_ref[first : first + count, here] = (weights * (gw - row_delta)).astype(jnp.bfloat16)
 
     def gather(b, here):
-        query_part = dot(grads_ref[:far_rows, here], q_ref[here, :], NN) * softmax_scale
-        grad_part = dot(weights_ref[:far_rows, here], g_ref[here, :], NN)
+        query_part = dot(grads_ref[:now_rows, here], q_ref[here, :], NN) * softmax_scale
+        grad_part = dot(weights_ref[:now_rows, here], g_ref[here, :], NN)
         if steps == 1:
             acc_ref[b, :, :] = query_part
         else:
@@ -221,7 +221,7 @@
                 gather(b, slice(first, local + tile_rows))
 
     def end():
-        spread_slots(dense_ref, acc_ref, want_ref, range(n_far))
+        spread_slots(dense_ref, acc_ref, want_ref, 0, n_cross + 1)
         write_halves(dense_ref, 0, my_half, keep_ref, send_ref)
         write_halves(dense_ref, n_cross, my_half, late_keep_ref, late_send_ref)
 
@@ -230,21 +230,23 @@
     at_step(steps - 1, steps, end)
 
 
-def grad_kernel(n_far, blocks_here, heads, want_ref, q_ref, g_ref, weights_ref, grads_ref, keep_ref, send_ref, acc_ref, dense_ref):
+def grad_kernel(n_far, n_now, blocks_here, heads, want_ref, q_ref, g_ref, weights_ref, grads_ref, keep_ref, send_ref, acc_ref, dense_ref):
     value_width = g_ref.shape[1]
-    start = n_far * BLOCK
+    start = n_now * BLOCK
+    n_rest = n_far - n_now
     block_rows = BLOCK * heads
     for b in range(blocks_here):
-        count = (b + 1) * BLOCK
+        count = (n_rest + b + 1) * BLOCK
         here = slice(b * block_rows, (b + 1) * block_rows)
         acc_ref[b, :count, :] = dot(grads_ref[start : start + count, here], q_ref[here, :], NN) * softmax_scale
         acc_ref[b, :count, :value_width] += dot(weights_ref[start : start + count, here], g_ref[here, :], NN)
+    spread_slots(dense_ref, acc_ref, want_ref, n_now, n_rest)
     for j in range(blocks_here):
-        rows = slice(j * BLOCK, (j + 1) * BLOCK)
-        part = acc_ref[j, rows, :]
+        at = (n_rest + j) * BLOCK
+        part = acc_ref[j, at : at + BLOCK, :]
         for b in range(j + 1, blocks_here):
-            part = part + acc_ref[b, rows, :]
-        dense_ref[0, rows, :] = part
+            part = part + acc_ref[b, at : at + BLOCK, :]
+        dense_ref[n_rest, j * BLOCK : (j + 1) * BLOCK, :] = part
     write_halves(dense_ref, 0, want_ref[blocks_here, 0], keep_ref, send_ref)
 
 
@@ -286,7 +288,7 @@
     )
 
 
-def whole_call(kernel, in_specs, out_specs, out_shape, scratch, macs, moved, name, steps=1):
+def whole_call(kernel, in_specs, out_specs, out_shape, scratch, macs, moved, name, steps=1, wide=False):
     in_vmem = pl.BlockSpec(memory_space=pltpu.VMEM)
     if steps == 1:
         in_specs, out_specs, grid = [in_vmem] * len(in_specs), (in_vmem,) * len(out_specs), {}
@@ -299,7 +301,7 @@
         out_shape=out_shape,
         scratch_shapes=scratch,
         compiler_params=pltpu.CompilerParams(
-            vmem_limit_bytes=VMEM_BYTES if steps == 1 else WIDE_BYTES
+            vmem_limit_bytes=WIDE_BYTES if wide else VMEM_BYTES
         ),
         cost_estimate=pl.CostEstimate(flops=2 * macs, bytes_accessed=moved, transcendentals=0),
         name=name,
@@ -368,6 +370,7 @@
         rows * (width + value_width) * 4,
         "early_scores",
         steps,
+        steps > 1,
     )(want, query_rows, grad_rows, own, mine, other)
 
 
@@ -379,7 +382,7 @@
     keys = n_far * BLOCK + tok_rows
     tile_rows, steps = tiling(rows, keys, heads)
     now = jax.ShapeDtypeStruct((n_cross, width // 2, tok_rows), jnp.bfloat16)
-    late = jax.ShapeDtypeStruct((n_far - n_cross, width // 2, tok_rows), jnp.bfloat16)
+    late = jax.ShapeDtypeStruct((1, width // 2, tok_rows), jnp.bfloat16)
     early_keys = early[0].shape[1]
     key_shape = (blocks_here, keys, width)
     return whole_call(
@@ -406,34 +409,38 @@
             late,
         ),
         [
-            pltpu.VMEM((blocks_here, n_far * BLOCK, width), jnp.float32),
-            pltpu.VMEM((n_far, tok_rows, width), jnp.float32),
+            pltpu.VMEM((blocks_here, (n_cross + 1) * BLOCK, width), jnp.float32),
+            pltpu.VMEM((n_cross + 1, tok_rows, width), jnp.float32),
             pltpu.VMEM((n_cross, tok_rows, width), jnp.bfloat16),
         ],
         rows * keys * 2 * (width + value_width),
         rows * (width + value_width) * 4,
         "scores",
         steps,
+        steps > 1,
     )(want, query_rows, grad_rows, bias, *early, mine, other)
 
 
-def grad_call(want, query_rows, grad_rows, weights, grads, n_far, heads, tok_rows):
+def grad_call(want, query_rows, grad_rows, weights, grads, n_far, n_now, heads, tok_rows):
     rows, width = query_rows.shape
     value_width = grad_rows.shape[1]
     blocks_here = tok_rows // BLOCK
-    half = jax.ShapeDtypeStruct((1, width // 2, tok_rows), jnp.bfloat16)
+    n_rest = n_far - n_now
+    half = jax.ShapeDtypeStruct((n_rest + 1, width // 2, tok_rows), jnp.bfloat16)
     return whole_call(
-        functools.partial(grad_kernel, n_far, blocks_here, heads),
+        functools.partial(grad_kernel, n_far, n_now, blocks_here, heads),
         [None] * 4,
         [None] * 2,
         (half, half),
         [
-            pltpu.VMEM((blocks_here, tok_rows, width), jnp.float32),
-            pltpu.VMEM((1, tok_rows, width), jnp.float32),
+            pltpu.VMEM((blocks_here, n_rest * BLOCK + tok_rows, width), jnp.float32),
+            pltpu.VMEM((n_rest + 1, tok_rows, width), jnp.float32),
         ],
-        rows * tok_rows * (width + value_width),
+        rows * (n_rest * BLOCK + tok_rows) * (width + value_width),
         rows * (width + value_width) * 4,
         "own_grads",
+        1,
+        rows * weights.shape[0] > UNROLLED,
     )(want, query_rows, grad_rows, weights, grads)
 
 
@@ -479,7 +486,7 @@
     def down(rows, hops):
         return lax.ppermute(rows, "ctx", [(i + 2 * hops, i) for i in range(shards - 2 * hops)])
 
-    offsets = sorted(range(1, lines), key=lambda k: (k != 2, k))
+    offsets = list(range(1, lines))
     cross_target = (my_shard ^ 1) - 2 * jnp.array([0] + offsets, jnp.int32)
     direct_target = my_shard - 2 * jnp.array(offsets, jnp.int32)
     n_cross, n_far = lines, shards - 1
@@ -509,16 +516,19 @@
     moving, weights, late_send = lax.optimization_barrier((moving, weights, late_send))
     arrived = lax.ppermute(moving, "ctx", across).astype(jnp.float32)
     late_send, weights = lax.optimization_barrier((swap(late_send), weights))
-    own_keep, own_send = grad_call(want, query_rows, grad_rows, weights, grads, n_far, heads, tok_rows)
-    own_send, weights = lax.optimization_barrier((own_send, weights))
+    rest_keep, rest_send = grad_call(
+        want, query_rows, grad_rows, weights, grads, n_far, n_cross + 1, heads, tok_rows
+    )
+    rest_send, weights = lax.optimization_barrier((rest_send, weights))
     late = late_keep.astype(jnp.float32) + late_send.astype(jnp.float32)
-    own = own_keep.astype(jnp.float32) + swap(own_send).astype(jnp.float32)
+    rest = rest_keep.astype(jnp.float32) + swap(rest_send).astype(jnp.float32)
     attended, grad_queries = out_call(keys, weights, grads, n_far, heads, value_width)
-    leaving = [(late[i] + arrived[i + 1]).astype(jnp.bfloat16) for i in range(n_far - n_cross)]
-    total = own[0] + arrived[0]
+    direct = [late[0]] + [rest[i] for i in range(n_far - n_cross - 1)]
+    leaving = [(mine + arrived[i + 1]).astype(jnp.bfloat16) for i, mine in enumerate(direct)]
+    total = rest[n_far - n_cross - 1] + arrived[0]
     *leaving, total, grad_queries = lax.optimization_barrier((*leaving, total, grad_queries))
     grad_queries = grad_queries.reshape(tok_rows, heads, width).transpose(1, 2, 0)
-    for part in [down(rows, k) for rows, k in zip(leaving, offsets)]:
+    for part in [down(rows, k) for k, rows in sorted(zip(offsets, leaving), key=lambda item: -item[0])]:
         total = total + part.astype(jnp.float32)
     low = total.astype(jnp.bfloat16)
     low, grad_queries = lax.optimization_barrier((low, grad_queries))

time: 65.4 us -> 63.6 us (0.972)
  waiting for transfers between devices: 12.8 us -> 11.8 us
  other arithmetic: 2.45 us -> 1.78 us
  transfers between devices with their start and end apart: 15 -> 15, of which waited for: 8 -> 7; matrix products, arithmetic and copies ran while one was open for 13% -> 12% of each run, Pallas kernels for 17% -> 18%
where the time goes in v4:
time: 63.6 us; the launch traced here: 63.2 us
  starting transfers between devices  20 us (31%)
  Pallas kernels  18.6 us (29%)
  waiting for transfers between devices  11.8 us (19%)
  local copies, waits for them, and re-layouts  10.2 us (16%)
  other arithmetic  1.78 us (3%)
  between operations  0.88 us (1%)
    ppermute x3, starting transfers between devices, up(): lax.ppermute(rows, 'ctx', [(i, i + 2 * hops) for i in range(shards - 2 *...  10.7 us
    pallas_call x1, Pallas kernels, score_call(): whole_call(functools.partial(score_kernel, n_far, n_cross, blocks_here, h...  7.12 us
    pallas_call x1, Pallas kernels, out_call(): call(functools.partial(out_kernel, n_far, blocks_here, heads), rows // ti...  5.26 us
    ppermute x6, waiting for transfers between devices, swap(): return lax.ppermute(rows, 'head', partner)  4.41 us
    ppermute x3, waiting for transfers between devices, down(): lax.ppermute(rows, 'ctx', [(i + 2 * hops, i) for i in range(shards - 2 *...  4.2 us
    optimization_barrier x1, local copies, waits for them, and re-layouts, body(): mine, queries = lax.optimization_barrier((mine, queries))  3.91 us
    ppermute x3, starting transfers between devices, down(): lax.ppermute(rows, 'ctx', [(i + 2 * hops, i) for i in range(shards - 2 *...  3.88 us
    reshape x1, local copies, waits for them, and re-layouts, body(): grad_queries.reshape(tok_rows, heads, width).transpose(1, 2, 0)  3.1 us
  transfers between devices with their start and end apart: 15, of which 7 were waited for; matrix products, arithmetic and copies ran while one was open for 12% of the time, Pallas kernels for 18%

profile of v4, /device:TPU:0, one launch (start us, length us, event | category | flops | bytes accessed | tf_op | source)
XLA Modules:
  0.0 63.2 jit_solution(11511997237983530867)
XLA Ops:
  0.6 0.9 %dynamic-slice_bitcast_fusion.refs_0_ = bf16[1,288,128]{2,1,0:T(8,128)(2,1)S(1)} fusion(bf16[128,576]{0,1:T(8,128)(2,1)} %param.7, s32[]{:T(128)S(6)} %select_n.19), kind=kLoop, calls=%fused_computation.17 | loop fusion | bytes 147460 | tf_op jit(solution)/shard_map/broadcast_in_dim | solution.py:499
  1.5 6.9 %collective-permute-start.2 = (bf16[1,288,128]{2,1,0:T(8,128)(2,1)S(1)}, bf16[1,288,128]{2,1,0:T(8,128)(2,1)S(1)}, u32[]{:S(2)}, u32[]{:S(2)}) collective-permute-start(bf16[1,288,128]{2,1,0:T(8,128)(2,1)S(1)} %dynamic-slice_bitcast_fusion.refs_0_), channel_id=1, source_target_pairs={{0,24},{4,28},{1,25},{5,29},{2,26},{6,30},{3,27},{7,31}} | collective-permute-start | bytes 221192 | tf_op jit(solution)/shard_map/ppermute | solution.py:484
  8.5 1.3 %collective-permute-start.1 = (bf16[1,288,128]{2,1,0:T(8,128)(2,1)S(1)}, bf16[1,288,128]{2,1,0:T(8,128)(2,1)S(1)}, u32[]{:S(2)}, u32[]{:S(2)}) collective-permute-start(bf16[1,288,128]{2,1,0:T(8,128)(2,1)S(1)} %dynamic-slice_bitcast_fusion.refs_0_), channel_id=1, source_target_pairs={{0,16},{4,20},{8,24},{12,28},{1,17},{5,21},{9,25},{13,29},{2,18},{... | collective-permute-start | bytes 221192 | tf_op jit(solution)/shard_map/ppermute | solution.py:484
  9.8 2.5 %collective-permute-start = (bf16[1,288,128]{2,1,0:T(8,128)(2,1)S(1)}, bf16[1,288,128]{2,1,0:T(8,128)(2,1)S(1)}, u32[]{:S(2)}, u32[]{:S(2)}) collective-permute-start(bf16[1,288,128]{2,1,0:T(8,128)(2,1)S(1)} %dynamic-slice_bitcast_fusion.refs_0_), channel_id=1, source_target_pairs={{0,8},{4,12},{8,16},{12,20},{16,24},{20,28},{1,9},{5,13},{9,17},{1... | collective-permute-start | bytes 221192 | tf_op jit(solution)/shard_map/ppermute | solution.py:484
  12.3 0.7 %broadcast_add_fusion = s32[3]{0:T(128)S(1)} fusion(s32[3]{0:T(128)} %constant.36, s32[]{:T(128)} %axis_index.25), kind=kLoop, calls=%fused_computation.20 | loop fusion | flops 3 | bytes 28 | tf_op jit(solution)/shard_map/sub | solution.py:491
  13.0 0.1 pad_add_fusion.place_ref
  13.0 0.0 copy-start.2
  13.0 0.7 %copy-done.2 = s32[128,8]{0,1:T(8,128)S(1)} copy-done((s32[128,8]{0,1:T(8,128)S(1)}, s32[128,8]{0,1:T(8,128)}, u32[]{:S(2)}) %copy-start.2) | copy-done | bytes 4120
  13.7 1.4 %table.1 = (f32[9,2048]{1,0:T(8,128)S(1)}, s32[3,7]{1,0:T(4,128)S(1)}) custom-call(s32[9]{0:T(128)S(1)} %pad_add_fusion.place_ref, s32[8,128]{1,0:T(8,128)S(1)} %bitcast.30), custom_call_target="tpu_custom_call" | custom-call | tf_op jit(solution)/shard_map/table/pallas_call | solution.py:324
  15.1 0.0 collective-permute-done.2.refs_3_
  15.1 0.0 collective-permute-done.1.refs_2_
  15.1 0.0 collective-permute-done.refs_1_
  15.2 0.0 copy-start.1
  15.2 0.1 collective-permute-start.3
  15.3 1.6 %collective-permute-start.4 = (bf16[4,288,128]{2,1,0:T(8,128)(2,1)S(1)}, bf16[4,288,128]{2,1,0:T(8,128)(2,1)}, u32[]{:S(2)}, u32[]{:S(2)}) collective-permute-start(bf16[4,288,128]{2,1,0:T(8,128)(2,1)S(1)} %join.1.mine_ref), channel_id=1, source_target_pairs={{0,4},{4,0},{8,12},{12,8},{16,20},{20,16},{24,28},{28,24},{1,5},{5... | collective-permute-start | bytes 884744 | tf_op jit(solution)/shard_map/ppermute | solution.py:505
  16.8 3.9 %copy.9 = bf16[128,16,576]{2,1,0:T(8,128)(2,1)S(1)} copy(bf16[128,16,576]{0,2,1:T(8,128)(2,1)} %param.6) | data formatting | bytes 4718592 | tf_op jit(solution)/shard_map/optimization_barrier | solution.py:504
  20.7 0.0 collective-permute-done.3.other_ref
  20.8 0.0 copy-done.1
  20.8 0.0 copy-start
  20.8 1.6 %copy-done = bf16[128,16,512]{2,1,0:T(8,128)(2,1)S(1)} copy-done((bf16[128,16,512]{2,1,0:T(8,128)(2,1)S(1)}, bf16[128,16,512]{2,1,0:T(8,128)(2,1)}, u32[]{:S(2)}) %copy-start) | copy-done | bytes 2097176
  22.4 2.6 %early_scores.1 = (bf16[2,320,576]{2,1,0:T(8,128)(2,1)S(1)}, f32[320,2048]{1,0:T(8,128)S(1)}, f32[320,2048]{1,0:T(8,128)S(1)}, bf16[2048,512]{1,0:T(8,128)(2,1)S(1)}) custom-call(s32[3,7]{1,0:T(4,128)S(1)} %get-tuple-element.47.want_ref, bf16[2048,576]{1,0:T(8,128)(2,1)S(1)} %bitcast.24, bf16[2048,512]{1,0:T(8,128)(2,1)S(1)} %bitcast.28, ...), custom_call_target="tpu_custom_call" | custom-call | flops 1426063360 | bytes 8912896 | tf_op jit(solution)/shard_map/early_scores/pallas_call | solution.py:358
  24.9 0.0 collective-permute-done.4.mine_ref
  24.9 0.2 collective-permute-start.5
  25.2 1.6 %collective-permute-done.5.other_ref = bf16[4,288,128]{2,1,0:T(8,128)(2,1)S(1)} collective-permute-done((bf16[4,288,128]{2,1,0:T(8,128)(2,1)}, bf16[4,288,128]{2,1,0:T(8,128)(2,1)S(1)}, u32[]{:S(2)}, u32[]{:S(2)}) %collective-permute-start.5) | collective-permute-done | bytes 294944 | tf_op jit(solution)/shard_map/ppermute | solution.py:481
  26.8 7.1 %scores.1 = (bf16[576,2048]{1,0:T(8,128)(2,1)S(1)}, bf16[576,2048]{1,0:T(8,128)(2,1)S(1)}, bf16[2,576,576]{2,1,0:T(8,128)(2,1)S(1)}, bf16[4,288,128]{2,1,0:T(8,1...) custom-call(s32[3,7]{1,0:T(4,128)S(1)} %get-tuple-element.47.want_re, ...), custom_call_target="tpu_custom_call" | custom-call | flops 5133828096 | bytes 8912896 | tf_op jit(solution)/shard_map/scores/pallas_call | solution.py:388
  33.9 0.2 collective-permute-start.6
  34.2 1.4 %collective-permute-done.6 = bf16[4,288,128]{2,1,0:T(8,128)(2,1)S(1)} collective-permute-done((bf16[4,288,128]{2,1,0:T(8,128)(2,1)S(1)}, bf16[4,288,128]{2,1,0:T(8,128)(2,1)S(1)}, u32[]{:S(2)}, u32[]{:S(2)}) %collective-permute-start.6) | collective-permute-done | bytes 294944 | tf_op jit(solution)/shard_map/ppermute | solution.py:481
  35.6 0.1 add_convert_fusion
  35.7 0.2 collective-permute-start.7
  35.9 1.3 %collective-permute-start.8 = (bf16[4,288,128]{2,1,0:T(8,128)(2,1)S(1)}, bf16[4,288,128]{2,1,0:T(8,128)(2,1)S(1)}, u32[]{:S(2)}, u32[]{:S(2)}) collective-permute-start(bf16[4,288,128]{2,1,0:T(8,128)(2,1)S(1)} %add_convert_fusion), channel_id=1, source_target_pairs={{0,4},{4,0},{8,12},{12,8},{16,20},{20,16},{24,28},{28,24},{1,5},{5... | collective-permute-start | bytes 884744 | tf_op jit(solution)/shard_map/ppermute | solution.py:517
  37.2 0.0 collective-permute-done.7
  37.2 2.2 %own_grads.1 = (bf16[3,288,128]{2,1,0:T(8,128)(2,1)S(1)}, bf16[3,288,128]{2,1,0:T(8,128)(2,1)S(1)}) custom-call(s32[3,7]{1,0:T(4,128)S(1)} %get-tuple-element.47.want_ref, bf16[2048,576]{1,0:T(8,128)(2,1)S(1)} %bitcast.26, bf16[2048,512]{1,0:T(8,128)(2,1)S(1)} %get-tuple-element.55.g_ref, bf16[576,2048]{1,0:T(8,128)(2,1)S(1)} %get-tuple-element.72.weights_ref, ...), custom_call_target="tpu_custom_call" | custom-call | flops 1140850688 | bytes 8912896 | tf_op jit(solution)/shard_map/own_grads/pallas_call | solution.py:430
  39.4 0.1 collective-permute-start.9
  39.5 5.3 %outputs.1 = (bf16[2048,512]{1,0:T(8,128)(2,1)}, bf16[2048,576]{1,0:T(8,128)(2,1)S(1)}) custom-call(bf16[2,576,576]{2,1,0:T(8,128)(2,1)S(1)} %get-tuple-element.62.keys_ref, bf16[576,2048]{1,0:T(8,128)(2,1)S(1)} %get-tuple-element.72.weights_ref, bf16[576,2048]{1,0:T(8,128)(2,1)S(1)} %get-tuple-element.70.grads_ref), custom_call_target="tpu_custom_call" | custom-call | flops 2566914048 | bytes 8912896 | tf_op jit(solution)/shard_map/outputs/pallas_call | solution.py:451
  44.8 0.4 collective-permute-done.8
  45.2 0.0 collective-permute-done.9
  45.3 0.1 fusion.1
  45.3 1.3 %collective-permute-start.10 = (bf16[288,128]{1,0:T(8,128)(2,1)S(1)}, bf16[288,128]{1,0:T(8,128)(2,1)S(1)}, u32[]{:S(2)}, u32[]{:S(2)}) collective-permute-start(bf16[288,128]{1,0:T(8,128)(2,1)S(1)} %get-tuple-element.81), channel_id=1, source_target_pairs={{24,0},{28,4},{25,1},{29,5},{26,2},{30,6},{27,3},{31,7}} | collective-permute-start | bytes 221192 | tf_op jit(solution)/shard_map/ppermute | solution.py:487
  46.6 1.3 %collective-permute-start.11 = (bf16[288,128]{1,0:T(8,128)(2,1)S(1)}, bf16[288,128]{1,0:T(8,128)(2,1)S(1)}, u32[]{:S(2)}, u32[]{:S(2)}) collective-permute-start(bf16[288,128]{1,0:T(8,128)(2,1)S(1)} %get-tuple-element.82), channel_id=1, source_target_pairs={{16,0},{20,4},{24,8},{28,12},{17,1},{21,5},{25,9},{29,13},{18,2},{... | collective-permute-start | bytes 221192 | tf_op jit(solution)/shard_map/ppermute | solution.py:487
  47.9 1.3 %collective-permute-start.12 = (bf16[288,128]{1,0:T(8,128)(2,1)S(1)}, bf16[288,128]{1,0:T(8,128)(2,1)S(1)}, u32[]{:S(2)}, u32[]{:S(2)}) collective-permute-start(bf16[288,128]{1,0:T(8,128)(2,1)S(1)} %get-tuple-element.83), channel_id=1, source_target_pairs={{8,0},{12,4},{16,8},{20,12},{24,16},{28,20},{9,1},{13,5},{17,9},{2... | collective-permute-start | bytes 221192 | tf_op jit(solution)/shard_map/ppermute | solution.py:487
  49.2 3.1 %copy.10 = bf16[128,16,576]{0,2,1:T(8,128)(2,1)} copy(bf16[128,16,576]{2,1,0:T(8,128)(2,1)S(1)} %bitcast.27) | data formatting | bytes 4718592 | tf_op jit(solution)/shard_map/reshape | solution.py:530
  52.3 1.6 %collective-permute-done.10 = bf16[288,128]{1,0:T(8,128)(2,1)S(1)} collective-permute-done((bf16[288,128]{1,0:T(8,128)(2,1)S(1)}, bf16[288,128]{1,0:T(8,128)(2,1)S(1)}, u32[]{:S(2)}, u32[]{:S(2)}) %collective-permute-start.10) | collective-permute-done | bytes 73760 | tf_op jit(solution)/shard_map/ppermute | solution.py:487
  53.9 2.6 %collective-permute-done.11 = bf16[288,128]{1,0:T(8,128)(2,1)S(1)} collective-permute-done((bf16[288,128]{1,0:T(8,128)(2,1)S(1)}, bf16[288,128]{1,0:T(8,128)(2,1)S(1)}, u32[]{:S(2)}, u32[]{:S(2)}) %collective-permute-start.11) | collective-permute-done | bytes 73760 | tf_op jit(solution)/shard_map/ppermute | solution.py:487
  56.5 0.0 collective-permute-done.12
  56.6 1.6 %collective-permute-start.13 = (bf16[288,128]{1,0:T(8,128)(2,1)S(1)}, bf16[288,128]{1,0:T(8,128)(2,1)S(1)}, u32[]{:S(2)}, u32[]{:S(2)}) collective-permute-start(bf16[288,128]{1,0:T(8,128)(2,1)S(1)} %add_convert_fusion.1), channel_id=1, source_target_pairs={{0,2},{1,3},{2,0},{3,1},{4,6},{5,7},{6,4},{7,5},{8,10},{9,11},{10,... | collective-permute-start | bytes 221192 | tf_op jit(solution)/shard_map/ppermute | solution.py:537
  58.2 2.8 %collective-permute-done.13 = bf16[288,128]{1,0:T(8,128)(2,1)S(1)} collective-permute-done((bf16[288,128]{1,0:T(8,128)(2,1)S(1)}, bf16[288,128]{1,0:T(8,128)(2,1)S(1)}, u32[]{:S(2)}, u32[]{:S(2)}) %collective-permute-start.13) | collective-permute-done | bytes 73760 | tf_op jit(solution)/shard_map/ppermute | solution.py:537
  61.0 0.1 collective-permute-start.14
  61.1 1.4 %collective-permute-done.14 = f32[288,128]{1,0:T(8,128)S(1)} collective-permute-done((f32[288,128]{1,0:T(8,128)S(1)}, f32[288,128]{1,0:T(8,128)S(1)}, u32[]{:S(2)}, u32[]{:S(2)}) %collective-permute-start.14) | collective-permute-done | bytes 147488 | tf_op jit(solution)/shard_map/ppermute | solution.py:481
  62.5 0.7 %fusion = f32[128,576]{0,1:T(8,128)} fusion(f32[288,128]{1,0:T(8,128)S(1)} %collective-permute-done.14, f32[288,128]{1,0:T(8,128)S(1)} %convert_add_fusion.1, pred[]{:T(512)S(6)} %eq.5), kind=kLoop, calls=%fused_computation.3 | loop fusion | flops 221184 | bytes 589825 | tf_op jit(solution)/shard_map/transpose | solution.py:548
  (6 shorter events, 0.2 us)
Async XLA Ops:
  1.5 13.6 %collective-permute-start.2 = (bf16[1,288,128]{2,1,0:T(8,128)(2,1)S(1)}, bf16[1,288,128]{2,1,0:T(8,128)(2,1)S(1)}, u32[]{:S(2)}, u32[]{:S(2)}) collective-permute-start(bf16[1,288,128]{2,1,0:T(8,128)(2,1)S(1)} %dynamic-slice_bitcast_fusion.refs_0_), channel_id=1, source_target_pairs={{0,24},{4,28},{1,25},{5,29},{2,26},{6,30},{3,27},{7,31}} | collective-permute-start | bytes 221192 | tf_op jit(solution)/shard_map/ppermute | solution.py:484
  8.5 6.6 %collective-permute-start.1 = (bf16[1,288,128]{2,1,0:T(8,128)(2,1)S(1)}, bf16[1,288,128]{2,1,0:T(8,128)(2,1)S(1)}, u32[]{:S(2)}, u32[]{:S(2)}) collective-permute-start(bf16[1,288,128]{2,1,0:T(8,128)(2,1)S(1)} %dynamic-slice_bitcast_fusion.refs_0_), channel_id=1, source_target_pairs={{0,16},{4,20},{8,24},{12,28},{1,17},{5,21},{9,25},{13,29},{2,18},{... | collective-permute-start | bytes 221192 | tf_op jit(solution)/shard_map/ppermute | solution.py:484
  9.8 5.3 %collective-permute-start = (bf16[1,288,128]{2,1,0:T(8,128)(2,1)S(1)}, bf16[1,288,128]{2,1,0:T(8,128)(2,1)S(1)}, u32[]{:S(2)}, u32[]{:S(2)}) collective-permute-start(bf16[1,288,128]{2,1,0:T(8,128)(2,1)S(1)} %dynamic-slice_bitcast_fusion.refs_0_), channel_id=1, source_target_pairs={{0,8},{4,12},{8,16},{12,20},{16,24},{20,28},{1,9},{5,13},{9,17},{1... | collective-permute-start | bytes 221192 | tf_op jit(solution)/shard_map/ppermute | solution.py:484
  13.0 0.7 %copy-start.2 = (s32[128,8]{0,1:T(8,128)S(1)}, s32[128,8]{0,1:T(8,128)}, u32[]{:S(2)}) copy-start(s32[128,8]{0,1:T(8,128)} %param.9) | copy-start | bytes 12292
  15.2 5.6 %copy-start.1 = (bf16[128,576]{0,1:T(8,128)(2,1)S(1)}, bf16[128,576]{0,1:T(8,128)(2,1)}, u32[]{:S(2)}) copy-start(bf16[128,576]{0,1:T(8,128)(2,1)} %param.7) | copy-start | bytes 442372
  15.2 5.6 %collective-permute-start.3 = (bf16[4,288,128]{2,1,0:T(8,128)(2,1)S(1)}, bf16[4,288,128]{2,1,0:T(8,128)(2,1)S(1)}, u32[]{:S(2)}, u32[]{:S(2)}) collective-permute-start(bf16[4,288,128]{2,1,0:T(8,128)(2,1)S(1)} %join.1.mine_ref), channel_id=1, source_target_pairs={{0,1},{1,0},{2,3},{3,2},{4,5},{5,4},{6,7},{7,6},{8,9},{9,8},{10,11... | collective-permute-start | bytes 884744 | tf_op jit(solution)/shard_map/ppermute | solution.py:481
  15.3 9.7 %collective-permute-start.4 = (bf16[4,288,128]{2,1,0:T(8,128)(2,1)S(1)}, bf16[4,288,128]{2,1,0:T(8,128)(2,1)}, u32[]{:S(2)}, u32[]{:S(2)}) collective-permute-start(bf16[4,288,128]{2,1,0:T(8,128)(2,1)S(1)} %join.1.mine_ref), channel_id=1, source_target_pairs={{0,4},{4,0},{8,12},{12,8},{16,20},{20,16},{24,28},{28,24},{1,5},{5... | collective-permute-start | bytes 884744 | tf_op jit(solution)/shard_map/ppermute | solution.py:505
  20.8 1.6 %copy-start = (bf16[128,16,512]{2,1,0:T(8,128)(2,1)S(1)}, bf16[128,16,512]{2,1,0:T(8,128)(2,1)}, u32[]{:S(2)}) copy-start(bf16[128,16,512]{2,1,0:T(8,128)(2,1)} %param.8) | copy-start | bytes 6291460
  24.9 1.9 %collective-permute-start.5 = (bf16[4,288,128]{2,1,0:T(8,128)(2,1)}, bf16[4,288,128]{2,1,0:T(8,128)(2,1)S(1)}, u32[]{:S(2)}, u32[]{:S(2)}) collective-permute-start(bf16[4,288,128]{2,1,0:T(8,128)(2,1)} %collective-permute-done.4.mine_ref), channel_id=1, source_target_pairs={{0,1},{1,0},{2,3},{3,2},{4,5},{5,4},{6,7},{7,6},{8,9},{9,8},{10,11... | collective-permute-start | bytes 884744 | tf_op jit(solution)/shard_map/ppermute | solution.py:481
  33.9 1.6 %collective-permute-start.6 = (bf16[4,288,128]{2,1,0:T(8,128)(2,1)S(1)}, bf16[4,288,128]{2,1,0:T(8,128)(2,1)S(1)}, u32[]{:S(2)}, u32[]{:S(2)}) collective-permute-start(bf16[4,288,128]{2,1,0:T(8,128)(2,1)S(1)} %get-tuple-element.64), channel_id=1, source_target_pairs={{0,1},{1,0},{2,3},{3,2},{4,5},{5,4},{6,7},{7,6},{8,9},{9,8},{10,11... | collective-permute-start | bytes 884744 | tf_op jit(solution)/shard_map/ppermute | solution.py:481
  35.7 1.5 %collective-permute-start.7 = (bf16[1,288,128]{2,1,0:T(8,128)(2,1)S(1)}, bf16[1,288,128]{2,1,0:T(8,128)(2,1)S(1)}, u32[]{:S(2)}, u32[]{:S(2)}) collective-permute-start(bf16[1,288,128]{2,1,0:T(8,128)(2,1)S(1)} %get-tuple-element.67), channel_id=1, source_target_pairs={{0,1},{1,0},{2,3},{3,2},{4,5},{5,4},{6,7},{7,6},{8,9},{9,8},{10,11... | collective-permute-start | bytes 221192 | tf_op jit(solution)/shard_map/ppermute | solution.py:481
  35.9 9.3 %collective-permute-start.8 = (bf16[4,288,128]{2,1,0:T(8,128)(2,1)S(1)}, bf16[4,288,128]{2,1,0:T(8,128)(2,1)S(1)}, u32[]{:S(2)}, u32[]{:S(2)}) collective-permute-start(bf16[4,288,128]{2,1,0:T(8,128)(2,1)S(1)} %add_convert_fusion), channel_id=1, source_target_pairs={{0,4},{4,0},{8,12},{12,8},{16,20},{20,16},{24,28},{28,24},{1,5},{5... | collective-permute-start | bytes 884744 | tf_op jit(solution)/shard_map/ppermute | solution.py:517
  39.4 5.8 %collective-permute-start.9 = (bf16[3,288,128]{2,1,0:T(8,128)(2,1)S(1)}, bf16[3,288,128]{2,1,0:T(8,128)(2,1)S(1)}, u32[]{:S(2)}, u32[]{:S(2)}) collective-permute-start(bf16[3,288,128]{2,1,0:T(8,128)(2,1)S(1)} %get-tuple-element.78), channel_id=1, source_target_pairs={{0,1},{1,0},{2,3},{3,2},{4,5},{5,4},{6,7},{7,6},{8,9},{9,8},{10,11... | collective-permute-start | bytes 663560 | tf_op jit(solution)/shard_map/ppermute | solution.py:481
  45.3 8.6 %collective-permute-start.10 = (bf16[288,128]{1,0:T(8,128)(2,1)S(1)}, bf16[288,128]{1,0:T(8,128)(2,1)S(1)}, u32[]{:S(2)}, u32[]{:S(2)}) collective-permute-start(bf16[288,128]{1,0:T(8,128)(2,1)S(1)} %get-tuple-element.81), channel_id=1, source_target_pairs={{24,0},{28,4},{25,1},{29,5},{26,2},{30,6},{27,3},{31,7}} | collective-permute-start | bytes 221192 | tf_op jit(solution)/shard_map/ppermute | solution.py:487
  46.6 9.9 %collective-permute-start.11 = (bf16[288,128]{1,0:T(8,128)(2,1)S(1)}, bf16[288,128]{1,0:T(8,128)(2,1)S(1)}, u32[]{:S(2)}, u32[]{:S(2)}) collective-permute-start(bf16[288,128]{1,0:T(8,128)(2,1)S(1)} %get-tuple-element.82), channel_id=1, source_target_pairs={{16,0},{20,4},{24,8},{28,12},{17,1},{21,5},{25,9},{29,13},{18,2},{... | collective-permute-start | bytes 221192 | tf_op jit(solution)/shard_map/ppermute | solution.py:487
  47.9 8.6 %collective-permute-start.12 = (bf16[288,128]{1,0:T(8,128)(2,1)S(1)}, bf16[288,128]{1,0:T(8,128)(2,1)S(1)}, u32[]{:S(2)}, u32[]{:S(2)}) collective-permute-start(bf16[288,128]{1,0:T(8,128)(2,1)S(1)} %get-tuple-element.83), channel_id=1, source_target_pairs={{8,0},{12,4},{16,8},{20,12},{24,16},{28,20},{9,1},{13,5},{17,9},{2... | collective-permute-start | bytes 221192 | tf_op jit(solution)/shard_map/ppermute | solution.py:487
  56.6 4.4 %collective-permute-start.13 = (bf16[288,128]{1,0:T(8,128)(2,1)S(1)}, bf16[288,128]{1,0:T(8,128)(2,1)S(1)}, u32[]{:S(2)}, u32[]{:S(2)}) collective-permute-start(bf16[288,128]{1,0:T(8,128)(2,1)S(1)} %add_convert_fusion.1), channel_id=1, source_target_pairs={{0,2},{1,3},{2,0},{3,1},{4,6},{5,7},{6,4},{7,5},{8,10},{9,11},{10,... | collective-permute-start | bytes 221192 | tf_op jit(solution)/shard_map/ppermute | solution.py:537
  61.0 1.4 %collective-permute-start.14 = (f32[288,128]{1,0:T(8,128)S(1)}, f32[288,128]{1,0:T(8,128)S(1)}, u32[]{:S(2)}, u32[]{:S(2)}) collective-permute-start(f32[288,128]{1,0:T(8,128)S(1)} %convert_add_fusion.1), channel_id=1, source_target_pairs={{0,1},{1,0},{2,3},{3,2},{4,5},{5,4},{6,7},{7,6},{8,9},{9,8},{10,11... | collective-permute-start | bytes 442376 | tf_op jit(solution)/shard_map/ppermute | solution.py:481

commit v5 on v4

--- a/solution.py
+++ b/solution.py
@@ -8,7 +8,7 @@
 from jax.sharding import PartitionSpec as P
 
 BLOCK = 64
-SCORE_ROWS = 512
+SCORE_ROWS = 256
 OUT_ROWS = 1024
 MASKED = -1e30
 WIDE_ROWS = 256
@@ -35,11 +35,13 @@
 
 
 def spread_slots(dense_ref, acc_ref, want_ref, first, count):
-    dense_ref[...] = jnp.zeros_like(dense_ref)
-    for b in range(acc_ref.shape[0]):
-        for at in range(count):
-            offset = pl.multiple_of(want_ref[b, first + at] * BLOCK, BLOCK)
-            dense_ref[at, pl.ds(offset, BLOCK), :] += acc_ref[b, at * BLOCK : (at + 1) * BLOCK, :]
+    for at in range(count):
+        rows = slice(at * BLOCK, (at + 1) * BLOCK)
+        for j in range(dense_ref.shape[1] // BLOCK):
+            placed = 0.0
+            for b in range(acc_ref.shape[0]):
+                placed += jnp.where(want_ref[b, first + at] == j, acc_ref[b, rows, :], 0.0)
+            dense_ref[at, j * BLOCK : (j + 1) * BLOCK, :] = placed
 
 
 def write_halves(dense_ref, at, my_half, keep_ref, send_ref):

time: 63.6 us -> 63.3 us (level)
  no operation moved by 1% of the time
where the time goes in v5:
time: 63.3 us; the launch traced here: 62.8 us
  starting transfers between devices  19.9 us (31%)
  Pallas kernels  18.1 us (29%)
  waiting for transfers between devices  12 us (19%)
  local copies, waits for them, and re-layouts  10.2 us (16%)
  other arithmetic  1.78 us (3%)
  between operations  0.88 us (1%)
    ppermute x3, starting transfers between devices, up(): lax.ppermute(rows, 'ctx', [(i, i + 2 * hops) for i in range(shards - 2 *...  10.7 us
    pallas_call x1, Pallas kernels, score_call(): whole_call(functools.partial(score_kernel, n_far, n_cross, blocks_here, h...  6.72 us
    pallas_call x1, Pallas kernels, out_call(): call(functools.partial(out_kernel, n_far, blocks_here, heads), rows // ti...  5.26 us
    ppermute x6, waiting for transfers between devices, swap(): return lax.ppermute(rows, 'head', partner)  4.44 us
    ppermute x3, waiting for transfers between devices, down(): lax.ppermute(rows, 'ctx', [(i + 2 * hops, i) for i in range(shards - 2 *...  4.22 us
    optimization_barrier x1, local copies, waits for them, and re-layouts, body(): mine, queries = lax.optimization_barrier((mine, queries))  3.91 us
    ppermute x3, starting transfers between devices, down(): lax.ppermute(rows, 'ctx', [(i + 2 * hops, i) for i in range(shards - 2 *...  3.88 us
    reshape x1, local copies, waits for them, and re-layouts, body(): grad_queries.reshape(tok_rows, heads, width).transpose(1, 2, 0)  3.1 us
  transfers between devices with their start and end apart: 15, of which 7 were waited for; matrix products, arithmetic and copies ran while one was open for 12% of the time, Pallas kernels for 18%

profile of v5, /device:TPU:0, one launch (start us, length us, event | category | flops | bytes accessed | tf_op | source)
XLA Modules:
  0.0 62.8 jit_solution(6412285116401011166)
XLA Ops:
  0.6 0.9 %dynamic-slice_bitcast_fusion.refs_0_ = bf16[1,288,128]{2,1,0:T(8,128)(2,1)S(1)} fusion(bf16[128,576]{0,1:T(8,128)(2,1)} %param.7, s32[]{:T(128)S(6)} %select_n.19), kind=kLoop, calls=%fused_computation.17 | loop fusion | bytes 147460 | tf_op jit(solution)/shard_map/broadcast_in_dim | solution.py:501
  1.5 6.9 %collective-permute-start.2 = (bf16[1,288,128]{2,1,0:T(8,128)(2,1)S(1)}, bf16[1,288,128]{2,1,0:T(8,128)(2,1)S(1)}, u32[]{:S(2)}, u32[]{:S(2)}) collective-permute-start(bf16[1,288,128]{2,1,0:T(8,128)(2,1)S(1)} %dynamic-slice_bitcast_fusion.refs_0_), channel_id=1, source_target_pairs={{0,24},{4,28},{1,25},{5,29},{2,26},{6,30},{3,27},{7,31}} | collective-permute-start | bytes 221192 | tf_op jit(solution)/shard_map/ppermute | solution.py:486
  8.5 1.3 %collective-permute-start.1 = (bf16[1,288,128]{2,1,0:T(8,128)(2,1)S(1)}, bf16[1,288,128]{2,1,0:T(8,128)(2,1)S(1)}, u32[]{:S(2)}, u32[]{:S(2)}) collective-permute-start(bf16[1,288,128]{2,1,0:T(8,128)(2,1)S(1)} %dynamic-slice_bitcast_fusion.refs_0_), channel_id=1, source_target_pairs={{0,16},{4,20},{8,24},{12,28},{1,17},{5,21},{9,25},{13,29},{2,18},{... | collective-permute-start | bytes 221192 | tf_op jit(solution)/shard_map/ppermute | solution.py:486
  9.8 2.5 %collective-permute-start = (bf16[1,288,128]{2,1,0:T(8,128)(2,1)S(1)}, bf16[1,288,128]{2,1,0:T(8,128)(2,1)S(1)}, u32[]{:S(2)}, u32[]{:S(2)}) collective-permute-start(bf16[1,288,128]{2,1,0:T(8,128)(2,1)S(1)} %dynamic-slice_bitcast_fusion.refs_0_), channel_id=1, source_target_pairs={{0,8},{4,12},{8,16},{12,20},{16,24},{20,28},{1,9},{5,13},{9,17},{1... | collective-permute-start | bytes 221192 | tf_op jit(solution)/shard_map/ppermute | solution.py:486
  12.3 0.7 %broadcast_add_fusion = s32[3]{0:T(128)S(1)} fusion(s32[3]{0:T(128)} %constant.36, s32[]{:T(128)} %axis_index.25), kind=kLoop, calls=%fused_computation.20 | loop fusion | flops 3 | bytes 28 | tf_op jit(solution)/shard_map/sub | solution.py:493
  13.0 0.1 pad_add_fusion.place_ref
  13.0 0.0 copy-start.2
  13.0 0.7 %copy-done.2 = s32[128,8]{0,1:T(8,128)S(1)} copy-done((s32[128,8]{0,1:T(8,128)S(1)}, s32[128,8]{0,1:T(8,128)}, u32[]{:S(2)}) %copy-start.2) | copy-done | bytes 4120
  13.7 1.4 %table.1 = (f32[9,2048]{1,0:T(8,128)S(1)}, s32[3,7]{1,0:T(4,128)S(1)}) custom-call(s32[9]{0:T(128)S(1)} %pad_add_fusion.place_ref, s32[8,128]{1,0:T(8,128)S(1)} %bitcast.30), custom_call_target="tpu_custom_call" | custom-call | tf_op jit(solution)/shard_map/table/pallas_call | solution.py:326
  15.1 0.0 collective-permute-done.2.refs_3_
  15.1 0.0 collective-permute-done.1.refs_2_
  15.1 0.0 collective-permute-done.refs_1_
  15.2 0.0 copy-start.1
  15.2 0.1 collective-permute-start.3
  15.3 1.6 %collective-permute-start.4 = (bf16[4,288,128]{2,1,0:T(8,128)(2,1)S(1)}, bf16[4,288,128]{2,1,0:T(8,128)(2,1)}, u32[]{:S(2)}, u32[]{:S(2)}) collective-permute-start(bf16[4,288,128]{2,1,0:T(8,128)(2,1)S(1)} %join.1.mine_ref), channel_id=1, source_target_pairs={{0,4},{4,0},{8,12},{12,8},{16,20},{20,16},{24,28},{28,24},{1,5},{5... | collective-permute-start | bytes 884744 | tf_op jit(solution)/shard_map/ppermute | solution.py:507
  16.8 3.9 %copy.9 = bf16[128,16,576]{2,1,0:T(8,128)(2,1)S(1)} copy(bf16[128,16,576]{0,2,1:T(8,128)(2,1)} %param.6) | data formatting | bytes 4718592 | tf_op jit(solution)/shard_map/optimization_barrier | solution.py:506
  20.7 0.0 collective-permute-done.3.other_ref
  20.8 0.0 copy-done.1
  20.8 0.0 copy-start
  20.8 1.6 %copy-done = bf16[128,16,512]{2,1,0:T(8,128)(2,1)S(1)} copy-done((bf16[128,16,512]{2,1,0:T(8,128)(2,1)S(1)}, bf16[128,16,512]{2,1,0:T(8,128)(2,1)}, u32[]{:S(2)}) %copy-start) | copy-done | bytes 2097176
  22.4 2.6 %early_scores.1 = (bf16[2,320,576]{2,1,0:T(8,128)(2,1)S(1)}, f32[320,2048]{1,0:T(8,128)S(1)}, f32[320,2048]{1,0:T(8,128)S(1)}, bf16[2048,512]{1,0:T(8,128)(2,1)S(1)}) custom-call(s32[3,7]{1,0:T(4,128)S(1)} %get-tuple-element.47.want_ref, bf16[2048,576]{1,0:T(8,128)(2,1)S(1)} %bitcast.24, bf16[2048,512]{1,0:T(8,128)(2,1)S(1)} %bitcast.28, ...), custom_call_target="tpu_custom_call" | custom-call | flops 1426063360 | bytes 8912896 | tf_op jit(solution)/shard_map/early_scores/pallas_call | solution.py:360
  25.0 0.0 collective-permute-done.4.mine_ref
  25.0 0.2 collective-permute-start.5
  25.2 1.6 %collective-permute-done.5.other_ref = bf16[4,288,128]{2,1,0:T(8,128)(2,1)S(1)} collective-permute-done((bf16[4,288,128]{2,1,0:T(8,128)(2,1)}, bf16[4,288,128]{2,1,0:T(8,128)(2,1)S(1)}, u32[]{:S(2)}, u32[]{:S(2)}) %collective-permute-start.5) | collective-permute-done | bytes 294944 | tf_op jit(solution)/shard_map/ppermute | solution.py:483
  26.8 6.7 %scores.1 = (bf16[576,2048]{1,0:T(8,128)(2,1)S(1)}, bf16[576,2048]{1,0:T(8,128)(2,1)S(1)}, bf16[2,576,576]{2,1,0:T(8,128)(2,1)S(1)}, bf16[4,288,128]{2,1,0:T(8,1...) custom-call(s32[3,7]{1,0:T(4,128)S(1)} %get-tuple-element.47.want_re, ...), custom_call_target="tpu_custom_call" | custom-call | flops 5133828096 | bytes 8912896 | tf_op jit(solution)/shard_map/scores/pallas_call | solution.py:390
  33.5 0.2 collective-permute-start.6
  33.8 1.4 %collective-permute-done.6 = bf16[4,288,128]{2,1,0:T(8,128)(2,1)S(1)} collective-permute-done((bf16[4,288,128]{2,1,0:T(8,128)(2,1)S(1)}, bf16[4,288,128]{2,1,0:T(8,128)(2,1)S(1)}, u32[]{:S(2)}, u32[]{:S(2)}) %collective-permute-start.6) | collective-permute-done | bytes 294944 | tf_op jit(solution)/shard_map/ppermute | solution.py:483
  35.2 0.1 add_convert_fusion
  35.3 0.2 collective-permute-start.7
  35.5 1.3 %collective-permute-start.8 = (bf16[4,288,128]{2,1,0:T(8,128)(2,1)S(1)}, bf16[4,288,128]{2,1,0:T(8,128)(2,1)S(1)}, u32[]{:S(2)}, u32[]{:S(2)}) collective-permute-start(bf16[4,288,128]{2,1,0:T(8,128)(2,1)S(1)} %add_convert_fusion), channel_id=1, source_target_pairs={{0,4},{4,0},{8,12},{12,8},{16,20},{20,16},{24,28},{28,24},{1,5},{5... | collective-permute-start | bytes 884744 | tf_op jit(solution)/shard_map/ppermute | solution.py:519
  36.8 0.0 collective-permute-done.7
  36.8 2.1 %own_grads.1 = (bf16[3,288,128]{2,1,0:T(8,128)(2,1)S(1)}, bf16[3,288,128]{2,1,0:T(8,128)(2,1)S(1)}) custom-call(s32[3,7]{1,0:T(4,128)S(1)} %get-tuple-element.47.want_ref, bf16[2048,576]{1,0:T(8,128)(2,1)S(1)} %bitcast.26, bf16[2048,512]{1,0:T(8,128)(2,1)S(1)} %get-tuple-element.55.g_ref, bf16[576,2048]{1,0:T(8,128)(2,1)S(1)} %get-tuple-element.72.weights_ref, ...), custom_call_target="tpu_custom_call" | custom-call | flops 1140850688 | bytes 8912896 | tf_op jit(solution)/shard_map/own_grads/pallas_call | solution.py:432
  38.9 0.1 collective-permute-start.9
  39.0 5.3 %outputs.1 = (bf16[2048,512]{1,0:T(8,128)(2,1)}, bf16[2048,576]{1,0:T(8,128)(2,1)S(1)}) custom-call(bf16[2,576,576]{2,1,0:T(8,128)(2,1)S(1)} %get-tuple-element.62.keys_ref, bf16[576,2048]{1,0:T(8,128)(2,1)S(1)} %get-tuple-element.72.weights_ref, bf16[576,2048]{1,0:T(8,128)(2,1)S(1)} %get-tuple-element.70.grads_ref), custom_call_target="tpu_custom_call" | custom-call | flops 2566914048 | bytes 8912896 | tf_op jit(solution)/shard_map/outputs/pallas_call | solution.py:453
  44.3 0.5 collective-permute-done.8
  44.8 0.0 collective-permute-done.9
  44.9 0.1 fusion.1
  45.0 1.3 %collective-permute-start.10 = (bf16[288,128]{1,0:T(8,128)(2,1)S(1)}, bf16[288,128]{1,0:T(8,128)(2,1)S(1)}, u32[]{:S(2)}, u32[]{:S(2)}) collective-permute-start(bf16[288,128]{1,0:T(8,128)(2,1)S(1)} %get-tuple-element.81), channel_id=1, source_target_pairs={{24,0},{28,4},{25,1},{29,5},{26,2},{30,6},{27,3},{31,7}} | collective-permute-start | bytes 221192 | tf_op jit(solution)/shard_map/ppermute | solution.py:489
  46.3 1.3 %collective-permute-start.11 = (bf16[288,128]{1,0:T(8,128)(2,1)S(1)}, bf16[288,128]{1,0:T(8,128)(2,1)S(1)}, u32[]{:S(2)}, u32[]{:S(2)}) collective-permute-start(bf16[288,128]{1,0:T(8,128)(2,1)S(1)} %get-tuple-element.82), channel_id=1, source_target_pairs={{16,0},{20,4},{24,8},{28,12},{17,1},{21,5},{25,9},{29,13},{18,2},{... | collective-permute-start | bytes 221192 | tf_op jit(solution)/shard_map/ppermute | solution.py:489
  47.6 1.3 %collective-permute-start.12 = (bf16[288,128]{1,0:T(8,128)(2,1)S(1)}, bf16[288,128]{1,0:T(8,128)(2,1)S(1)}, u32[]{:S(2)}, u32[]{:S(2)}) collective-permute-start(bf16[288,128]{1,0:T(8,128)(2,1)S(1)} %get-tuple-element.83), channel_id=1, source_target_pairs={{8,0},{12,4},{16,8},{20,12},{24,16},{28,20},{9,1},{13,5},{17,9},{2... | collective-permute-start | bytes 221192 | tf_op jit(solution)/shard_map/ppermute | solution.py:489
  48.9 3.1 %copy.10 = bf16[128,16,576]{0,2,1:T(8,128)(2,1)} copy(bf16[128,16,576]{2,1,0:T(8,128)(2,1)S(1)} %bitcast.27) | data formatting | bytes 4718592 | tf_op jit(solution)/shard_map/reshape | solution.py:532
  52.0 1.7 %collective-permute-done.10 = bf16[288,128]{1,0:T(8,128)(2,1)S(1)} collective-permute-done((bf16[288,128]{1,0:T(8,128)(2,1)S(1)}, bf16[288,128]{1,0:T(8,128)(2,1)S(1)}, u32[]{:S(2)}, u32[]{:S(2)}) %collective-permute-start.10) | collective-permute-done | bytes 73760 | tf_op jit(solution)/shard_map/ppermute | solution.py:489
  53.6 2.5 %collective-permute-done.11 = bf16[288,128]{1,0:T(8,128)(2,1)S(1)} collective-permute-done((bf16[288,128]{1,0:T(8,128)(2,1)S(1)}, bf16[288,128]{1,0:T(8,128)(2,1)S(1)}, u32[]{:S(2)}, u32[]{:S(2)}) %collective-permute-start.11) | collective-permute-done | bytes 73760 | tf_op jit(solution)/shard_map/ppermute | solution.py:489
  56.2 0.0 collective-permute-done.12
  56.2 1.6 %collective-permute-start.13 = (bf16[288,128]{1,0:T(8,128)(2,1)S(1)}, bf16[288,128]{1,0:T(8,128)(2,1)S(1)}, u32[]{:S(2)}, u32[]{:S(2)}) collective-permute-start(bf16[288,128]{1,0:T(8,128)(2,1)S(1)} %add_convert_fusion.1), channel_id=1, source_target_pairs={{0,2},{1,3},{2,0},{3,1},{4,6},{5,7},{6,4},{7,5},{8,10},{9,11},{10,... | collective-permute-start | bytes 221192 | tf_op jit(solution)/shard_map/ppermute | solution.py:539
  57.8 2.9 %collective-permute-done.13 = bf16[288,128]{1,0:T(8,128)(2,1)S(1)} collective-permute-done((bf16[288,128]{1,0:T(8,128)(2,1)S(1)}, bf16[288,128]{1,0:T(8,128)(2,1)S(1)}, u32[]{:S(2)}, u32[]{:S(2)}) %collective-permute-start.13) | collective-permute-done | bytes 73760 | tf_op jit(solution)/shard_map/ppermute | solution.py:539
  60.7 0.1 collective-permute-start.14
  60.8 1.4 %collective-permute-done.14 = f32[288,128]{1,0:T(8,128)S(1)} collective-permute-done((f32[288,128]{1,0:T(8,128)S(1)}, f32[288,128]{1,0:T(8,128)S(1)}, u32[]{:S(2)}, u32[]{:S(2)}) %collective-permute-start.14) | collective-permute-done | bytes 147488 | tf_op jit(solution)/shard_map/ppermute | solution.py:483
  62.1 0.7 %fusion = f32[128,576]{0,1:T(8,128)} fusion(f32[288,128]{1,0:T(8,128)S(1)} %collective-permute-done.14, f32[288,128]{1,0:T(8,128)S(1)} %convert_add_fusion.1, pred[]{:T(512)S(6)} %eq.5), kind=kLoop, calls=%fused_computation.3 | loop fusion | flops 221184 | bytes 589825 | tf_op jit(solution)/shard_map/transpose | solution.py:550
  (6 shorter events, 0.2 us)
Async XLA Ops:
  1.5 13.6 %collective-permute-start.2 = (bf16[1,288,128]{2,1,0:T(8,128)(2,1)S(1)}, bf16[1,288,128]{2,1,0:T(8,128)(2,1)S(1)}, u32[]{:S(2)}, u32[]{:S(2)}) collective-permute-start(bf16[1,288,128]{2,1,0:T(8,128)(2,1)S(1)} %dynamic-slice_bitcast_fusion.refs_0_), channel_id=1, source_target_pairs={{0,24},{4,28},{1,25},{5,29},{2,26},{6,30},{3,27},{7,31}} | collective-permute-start | bytes 221192 | tf_op jit(solution)/shard_map/ppermute | solution.py:486
  8.5 6.6 %collective-permute-start.1 = (bf16[1,288,128]{2,1,0:T(8,128)(2,1)S(1)}, bf16[1,288,128]{2,1,0:T(8,128)(2,1)S(1)}, u32[]{:S(2)}, u32[]{:S(2)}) collective-permute-start(bf16[1,288,128]{2,1,0:T(8,128)(2,1)S(1)} %dynamic-slice_bitcast_fusion.refs_0_), channel_id=1, source_target_pairs={{0,16},{4,20},{8,24},{12,28},{1,17},{5,21},{9,25},{13,29},{2,18},{... | collective-permute-start | bytes 221192 | tf_op jit(solution)/shard_map/ppermute | solution.py:486
  9.8 5.3 %collective-permute-start = (bf16[1,288,128]{2,1,0:T(8,128)(2,1)S(1)}, bf16[1,288,128]{2,1,0:T(8,128)(2,1)S(1)}, u32[]{:S(2)}, u32[]{:S(2)}) collective-permute-start(bf16[1,288,128]{2,1,0:T(8,128)(2,1)S(1)} %dynamic-slice_bitcast_fusion.refs_0_), channel_id=1, source_target_pairs={{0,8},{4,12},{8,16},{12,20},{16,24},{20,28},{1,9},{5,13},{9,17},{1... | collective-permute-start | bytes 221192 | tf_op jit(solution)/shard_map/ppermute | solution.py:486
  13.0 0.7 %copy-start.2 = (s32[128,8]{0,1:T(8,128)S(1)}, s32[128,8]{0,1:T(8,128)}, u32[]{:S(2)}) copy-start(s32[128,8]{0,1:T(8,128)} %param.9) | copy-start | bytes 12292
  15.2 5.6 %copy-start.1 = (bf16[128,576]{0,1:T(8,128)(2,1)S(1)}, bf16[128,576]{0,1:T(8,128)(2,1)}, u32[]{:S(2)}) copy-start(bf16[128,576]{0,1:T(8,128)(2,1)} %param.7) | copy-start | bytes 442372
  15.2 5.6 %collective-permute-start.3 = (bf16[4,288,128]{2,1,0:T(8,128)(2,1)S(1)}, bf16[4,288,128]{2,1,0:T(8,128)(2,1)S(1)}, u32[]{:S(2)}, u32[]{:S(2)}) collective-permute-start(bf16[4,288,128]{2,1,0:T(8,128)(2,1)S(1)} %join.1.mine_ref), channel_id=1, source_target_pairs={{0,1},{1,0},{2,3},{3,2},{4,5},{5,4},{6,7},{7,6},{8,9},{9,8},{10,11... | collective-permute-start | bytes 884744 | tf_op jit(solution)/shard_map/ppermute | solution.py:483
  15.3 9.7 %collective-permute-start.4 = (bf16[4,288,128]{2,1,0:T(8,128)(2,1)S(1)}, bf16[4,288,128]{2,1,0:T(8,128)(2,1)}, u32[]{:S(2)}, u32[]{:S(2)}) collective-permute-start(bf16[4,288,128]{2,1,0:T(8,128)(2,1)S(1)} %join.1.mine_ref), channel_id=1, source_target_pairs={{0,4},{4,0},{8,12},{12,8},{16,20},{20,16},{24,28},{28,24},{1,5},{5... | collective-permute-start | bytes 884744 | tf_op jit(solution)/shard_map/ppermute | solution.py:507
  20.8 1.6 %copy-start = (bf16[128,16,512]{2,1,0:T(8,128)(2,1)S(1)}, bf16[128,16,512]{2,1,0:T(8,128)(2,1)}, u32[]{:S(2)}) copy-start(bf16[128,16,512]{2,1,0:T(8,128)(2,1)} %param.8) | copy-start | bytes 6291460
  25.0 1.9 %collective-permute-start.5 = (bf16[4,288,128]{2,1,0:T(8,128)(2,1)}, bf16[4,288,128]{2,1,0:T(8,128)(2,1)S(1)}, u32[]{:S(2)}, u32[]{:S(2)}) collective-permute-start(bf16[4,288,128]{2,1,0:T(8,128)(2,1)} %collective-permute-done.4.mine_ref), channel_id=1, source_target_pairs={{0,1},{1,0},{2,3},{3,2},{4,5},{5,4},{6,7},{7,6},{8,9},{9,8},{10,11... | collective-permute-start | bytes 884744 | tf_op jit(solution)/shard_map/ppermute | solution.py:483
  33.5 1.6 %collective-permute-start.6 = (bf16[4,288,128]{2,1,0:T(8,128)(2,1)S(1)}, bf16[4,288,128]{2,1,0:T(8,128)(2,1)S(1)}, u32[]{:S(2)}, u32[]{:S(2)}) collective-permute-start(bf16[4,288,128]{2,1,0:T(8,128)(2,1)S(1)} %get-tuple-element.64), channel_id=1, source_target_pairs={{0,1},{1,0},{2,3},{3,2},{4,5},{5,4},{6,7},{7,6},{8,9},{9,8},{10,11... | collective-permute-start | bytes 884744 | tf_op jit(solution)/shard_map/ppermute | solution.py:483
  35.3 1.5 %collective-permute-start.7 = (bf16[1,288,128]{2,1,0:T(8,128)(2,1)S(1)}, bf16[1,288,128]{2,1,0:T(8,128)(2,1)S(1)}, u32[]{:S(2)}, u32[]{:S(2)}) collective-permute-start(bf16[1,288,128]{2,1,0:T(8,128)(2,1)S(1)} %get-tuple-element.67), channel_id=1, source_target_pairs={{0,1},{1,0},{2,3},{3,2},{4,5},{5,4},{6,7},{7,6},{8,9},{9,8},{10,11... | collective-permute-start | bytes 221192 | tf_op jit(solution)/shard_map/ppermute | solution.py:483
  35.5 9.3 %collective-permute-start.8 = (bf16[4,288,128]{2,1,0:T(8,128)(2,1)S(1)}, bf16[4,288,128]{2,1,0:T(8,128)(2,1)S(1)}, u32[]{:S(2)}, u32[]{:S(2)}) collective-permute-start(bf16[4,288,128]{2,1,0:T(8,128)(2,1)S(1)} %add_convert_fusion), channel_id=1, source_target_pairs={{0,4},{4,0},{8,12},{12,8},{16,20},{20,16},{24,28},{28,24},{1,5},{5... | collective-permute-start | bytes 884744 | tf_op jit(solution)/shard_map/ppermute | solution.py:519
  38.9 5.9 %collective-permute-start.9 = (bf16[3,288,128]{2,1,0:T(8,128)(2,1)S(1)}, bf16[3,288,128]{2,1,0:T(8,128)(2,1)S(1)}, u32[]{:S(2)}, u32[]{:S(2)}) collective-permute-start(bf16[3,288,128]{2,1,0:T(8,128)(2,1)S(1)} %get-tuple-element.78), channel_id=1, source_target_pairs={{0,1},{1,0},{2,3},{3,2},{4,5},{5,4},{6,7},{7,6},{8,9},{9,8},{10,11... | collective-permute-start | bytes 663560 | tf_op jit(solution)/shard_map/ppermute | solution.py:483
  45.0 8.7 %collective-permute-start.10 = (bf16[288,128]{1,0:T(8,128)(2,1)S(1)}, bf16[288,128]{1,0:T(8,128)(2,1)S(1)}, u32[]{:S(2)}, u32[]{:S(2)}) collective-permute-start(bf16[288,128]{1,0:T(8,128)(2,1)S(1)} %get-tuple-element.81), channel_id=1, source_target_pairs={{24,0},{28,4},{25,1},{29,5},{26,2},{30,6},{27,3},{31,7}} | collective-permute-start | bytes 221192 | tf_op jit(solution)/shard_map/ppermute | solution.py:489
  46.3 9.9 %collective-permute-start.11 = (bf16[288,128]{1,0:T(8,128)(2,1)S(1)}, bf16[288,128]{1,0:T(8,128)(2,1)S(1)}, u32[]{:S(2)}, u32[]{:S(2)}) collective-permute-start(bf16[288,128]{1,0:T(8,128)(2,1)S(1)} %get-tuple-element.82), channel_id=1, source_target_pairs={{16,0},{20,4},{24,8},{28,12},{17,1},{21,5},{25,9},{29,13},{18,2},{... | collective-permute-start | bytes 221192 | tf_op jit(solution)/shard_map/ppermute | solution.py:489
  47.6 8.6 %collective-permute-start.12 = (bf16[288,128]{1,0:T(8,128)(2,1)S(1)}, bf16[288,128]{1,0:T(8,128)(2,1)S(1)}, u32[]{:S(2)}, u32[]{:S(2)}) collective-permute-start(bf16[288,128]{1,0:T(8,128)(2,1)S(1)} %get-tuple-element.83), channel_id=1, source_target_pairs={{8,0},{12,4},{16,8},{20,12},{24,16},{28,20},{9,1},{13,5},{17,9},{2... | collective-permute-start | bytes 221192 | tf_op jit(solution)/shard_map/ppermute | solution.py:489
  56.2 4.4 %collective-permute-start.13 = (bf16[288,128]{1,0:T(8,128)(2,1)S(1)}, bf16[288,128]{1,0:T(8,128)(2,1)S(1)}, u32[]{:S(2)}, u32[]{:S(2)}) collective-permute-start(bf16[288,128]{1,0:T(8,128)(2,1)S(1)} %add_convert_fusion.1), channel_id=1, source_target_pairs={{0,2},{1,3},{2,0},{3,1},{4,6},{5,7},{6,4},{7,5},{8,10},{9,11},{10,... | collective-permute-start | bytes 221192 | tf_op jit(solution)/shard_map/ppermute | solution.py:539
  60.7 1.4 %collective-permute-start.14 = (f32[288,128]{1,0:T(8,128)S(1)}, f32[288,128]{1,0:T(8,128)S(1)}, u32[]{:S(2)}, u32[]{:S(2)}) collective-permute-start(f32[288,128]{1,0:T(8,128)S(1)} %convert_add_fusion.1), channel_id=1, source_target_pairs={{0,1},{1,0},{2,3},{3,2},{4,5},{5,4},{6,7},{7,6},{8,9},{9,8},{10,11... | collective-permute-start | bytes 442376 | tf_op jit(solution)/shard_map/ppermute | solution.py:483

commit v6 on v5

--- a/solution.py
+++ b/solution.py
@@ -12,7 +12,7 @@
 OUT_ROWS = 1024
 MASKED = -1e30
 WIDE_ROWS = 256
-VMEM_BYTES = 32 * 1024 * 1024
+VMEM_BYTES = 20 * 1024 * 1024
 WIDE_BYTES = 60 * 1024 * 1024
 UNROLLED = 1 << 21
 

time: 63.3 us -> 63.3 us (level)
  no operation moved by 1% of the time
where the time goes in v6:
time: 63.3 us; the launch traced here: 62.8 us
  starting transfers between devices  19.9 us (31%)
  Pallas kernels  18.1 us (29%)
  waiting for transfers between devices  12 us (19%)
  local copies, waits for them, and re-layouts  10.2 us (16%)
  other arithmetic  1.79 us (3%)
  between operations  0.88 us (1%)
    ppermute x3, starting transfers between devices, up(): lax.ppermute(rows, 'ctx', [(i, i + 2 * hops) for i in range(shards - 2 *...  10.7 us
    pallas_call x1, Pallas kernels, score_call(): whole_call(functools.partial(score_kernel, n_far, n_cross, blocks_here, h...  6.72 us
    pallas_call x1, Pallas kernels, out_call(): call(functools.partial(out_kernel, n_far, blocks_here, heads), rows // ti...  5.26 us
    ppermute x6, waiting for transfers between devices, swap(): return lax.ppermute(rows, 'head', partner)  4.44 us
    ppermute x3, waiting for transfers between devices, down(): lax.ppermute(rows, 'ctx', [(i + 2 * hops, i) for i in range(shards - 2 *...  4.22 us
    optimization_barrier x1, local copies, waits for them, and re-layouts, body(): mine, queries = lax.optimization_barrier((mine, queries))  3.91 us
    ppermute x3, starting transfers between devices, down(): lax.ppermute(rows, 'ctx', [(i + 2 * hops, i) for i in range(shards - 2 *...  3.88 us
    reshape x1, local copies, waits for them, and re-layouts, body(): grad_queries.reshape(tok_rows, heads, width).transpose(1, 2, 0)  3.1 us
  transfers between devices with their start and end apart: 15, of which 7 were waited for; matrix products, arithmetic and copies ran while one was open for 12% of the time, Pallas kernels for 18%

profile of v6, /device:TPU:0, one launch (start us, length us, event | category | flops | bytes accessed | tf_op | source)
XLA Modules:
  0.0 62.8 jit_solution(3539250979912268331)
XLA Ops:
  0.6 0.9 %dynamic-slice_bitcast_fusion.refs_0_ = bf16[1,288,128]{2,1,0:T(8,128)(2,1)S(1)} fusion(bf16[128,576]{0,1:T(8,128)(2,1)} %param.7, s32[]{:T(128)S(6)} %select_n.19), kind=kLoop, calls=%fused_computation.17 | loop fusion | bytes 147460 | tf_op jit(solution)/shard_map/broadcast_in_dim | solution.py:501
  1.5 6.9 %collective-permute-start.2 = (bf16[1,288,128]{2,1,0:T(8,128)(2,1)S(1)}, bf16[1,288,128]{2,1,0:T(8,128)(2,1)S(1)}, u32[]{:S(2)}, u32[]{:S(2)}) collective-permute-start(bf16[1,288,128]{2,1,0:T(8,128)(2,1)S(1)} %dynamic-slice_bitcast_fusion.refs_0_), channel_id=1, source_target_pairs={{0,24},{4,28},{1,25},{5,29},{2,26},{6,30},{3,27},{7,31}} | collective-permute-start | bytes 221192 | tf_op jit(solution)/shard_map/ppermute | solution.py:486
  8.5 1.3 %collective-permute-start.1 = (bf16[1,288,128]{2,1,0:T(8,128)(2,1)S(1)}, bf16[1,288,128]{2,1,0:T(8,128)(2,1)S(1)}, u32[]{:S(2)}, u32[]{:S(2)}) collective-permute-start(bf16[1,288,128]{2,1,0:T(8,128)(2,1)S(1)} %dynamic-slice_bitcast_fusion.refs_0_), channel_id=1, source_target_pairs={{0,16},{4,20},{8,24},{12,28},{1,17},{5,21},{9,25},{13,29},{2,18},{... | collective-permute-start | bytes 221192 | tf_op jit(solution)/shard_map/ppermute | solution.py:486
  9.8 2.5 %collective-permute-start = (bf16[1,288,128]{2,1,0:T(8,128)(2,1)S(1)}, bf16[1,288,128]{2,1,0:T(8,128)(2,1)S(1)}, u32[]{:S(2)}, u32[]{:S(2)}) collective-permute-start(bf16[1,288,128]{2,1,0:T(8,128)(2,1)S(1)} %dynamic-slice_bitcast_fusion.refs_0_), channel_id=1, source_target_pairs={{0,8},{4,12},{8,16},{12,20},{16,24},{20,28},{1,9},{5,13},{9,17},{1... | collective-permute-start | bytes 221192 | tf_op jit(solution)/shard_map/ppermute | solution.py:486
  12.3 0.7 %broadcast_add_fusion = s32[3]{0:T(128)S(1)} fusion(s32[3]{0:T(128)} %constant.36, s32[]{:T(128)} %axis_index.25), kind=kLoop, calls=%fused_computation.20 | loop fusion | flops 3 | bytes 28 | tf_op jit(solution)/shard_map/sub | solution.py:493
  13.0 0.1 pad_add_fusion.place_ref
  13.0 0.0 copy-start.2
  13.0 0.7 %copy-done.2 = s32[128,8]{0,1:T(8,128)S(1)} copy-done((s32[128,8]{0,1:T(8,128)S(1)}, s32[128,8]{0,1:T(8,128)}, u32[]{:S(2)}) %copy-start.2) | copy-done | bytes 4120
  13.7 1.4 %table.1 = (f32[9,2048]{1,0:T(8,128)S(1)}, s32[3,7]{1,0:T(4,128)S(1)}) custom-call(s32[9]{0:T(128)S(1)} %pad_add_fusion.place_ref, s32[8,128]{1,0:T(8,128)S(1)} %bitcast.30), custom_call_target="tpu_custom_call" | custom-call | tf_op jit(solution)/shard_map/table/pallas_call | solution.py:326
  15.1 0.0 collective-permute-done.2.refs_3_
  15.1 0.0 collective-permute-done.1.refs_2_
  15.1 0.0 collective-permute-done.refs_1_
  15.2 0.0 copy-start.1
  15.2 0.1 collective-permute-start.3
  15.3 1.6 %collective-permute-start.4 = (bf16[4,288,128]{2,1,0:T(8,128)(2,1)S(1)}, bf16[4,288,128]{2,1,0:T(8,128)(2,1)}, u32[]{:S(2)}, u32[]{:S(2)}) collective-permute-start(bf16[4,288,128]{2,1,0:T(8,128)(2,1)S(1)} %join.1.mine_ref), channel_id=1, source_target_pairs={{0,4},{4,0},{8,12},{12,8},{16,20},{20,16},{24,28},{28,24},{1,5},{5... | collective-permute-start | bytes 884744 | tf_op jit(solution)/shard_map/ppermute | solution.py:507
  16.8 3.9 %copy.9 = bf16[128,16,576]{2,1,0:T(8,128)(2,1)S(1)} copy(bf16[128,16,576]{0,2,1:T(8,128)(2,1)} %param.6) | data formatting | bytes 4718592 | tf_op jit(solution)/shard_map/optimization_barrier | solution.py:506
  20.7 0.0 collective-permute-done.3.other_ref
  20.8 0.0 copy-done.1
  20.8 0.0 copy-start
  20.8 1.6 %copy-done = bf16[128,16,512]{2,1,0:T(8,128)(2,1)S(1)} copy-done((bf16[128,16,512]{2,1,0:T(8,128)(2,1)S(1)}, bf16[128,16,512]{2,1,0:T(8,128)(2,1)}, u32[]{:S(2)}) %copy-start) | copy-done | bytes 2097176
  22.4 2.6 %early_scores.1 = (bf16[2,320,576]{2,1,0:T(8,128)(2,1)S(1)}, f32[320,2048]{1,0:T(8,128)S(1)}, f32[320,2048]{1,0:T(8,128)S(1)}, bf16[2048,512]{1,0:T(8,128)(2,1)S(1)}) custom-call(s32[3,7]{1,0:T(4,128)S(1)} %get-tuple-element.47.want_ref, bf16[2048,576]{1,0:T(8,128)(2,1)S(1)} %bitcast.24, bf16[2048,512]{1,0:T(8,128)(2,1)S(1)} %bitcast.28, ...), custom_call_target="tpu_custom_call" | custom-call | flops 1426063360 | bytes 8912896 | tf_op jit(solution)/shard_map/early_scores/pallas_call | solution.py:360
  25.0 0.0 collective-permute-done.4.mine_ref
  25.0 0.2 collective-permute-start.5
  25.2 1.6 %collective-permute-done.5.other_ref = bf16[4,288,128]{2,1,0:T(8,128)(2,1)S(1)} collective-permute-done((bf16[4,288,128]{2,1,0:T(8,128)(2,1)}, bf16[4,288,128]{2,1,0:T(8,128)(2,1)S(1)}, u32[]{:S(2)}, u32[]{:S(2)}) %collective-permute-start.5) | collective-permute-done | bytes 294944 | tf_op jit(solution)/shard_map/ppermute | solution.py:483
  26.8 6.7 %scores.1 = (bf16[576,2048]{1,0:T(8,128)(2,1)S(1)}, bf16[576,2048]{1,0:T(8,128)(2,1)S(1)}, bf16[2,576,576]{2,1,0:T(8,128)(2,1)S(1)}, bf16[4,288,128]{2,1,0:T(8,1...) custom-call(s32[3,7]{1,0:T(4,128)S(1)} %get-tuple-element.47.want_re, ...), custom_call_target="tpu_custom_call" | custom-call | flops 5133828096 | bytes 8912896 | tf_op jit(solution)/shard_map/scores/pallas_call | solution.py:390
  33.5 0.2 collective-permute-start.6
  33.8 1.4 %collective-permute-done.6 = bf16[4,288,128]{2,1,0:T(8,128)(2,1)S(1)} collective-permute-done((bf16[4,288,128]{2,1,0:T(8,128)(2,1)S(1)}, bf16[4,288,128]{2,1,0:T(8,128)(2,1)S(1)}, u32[]{:S(2)}, u32[]{:S(2)}) %collective-permute-start.6) | collective-permute-done | bytes 294944 | tf_op jit(solution)/shard_map/ppermute | solution.py:483
  35.2 0.1 add_convert_fusion
  35.3 0.2 collective-permute-start.7
  35.5 1.3 %collective-permute-start.8 = (bf16[4,288,128]{2,1,0:T(8,128)(2,1)S(1)}, bf16[4,288,128]{2,1,0:T(8,128)(2,1)S(1)}, u32[]{:S(2)}, u32[]{:S(2)}) collective-permute-start(bf16[4,288,128]{2,1,0:T(8,128)(2,1)S(1)} %add_convert_fusion), channel_id=1, source_target_pairs={{0,4},{4,0},{8,12},{12,8},{16,20},{20,16},{24,28},{28,24},{1,5},{5... | collective-permute-start | bytes 884744 | tf_op jit(solution)/shard_map/ppermute | solution.py:519
  36.8 0.0 collective-permute-done.7
  36.8 2.1 %own_grads.1 = (bf16[3,288,128]{2,1,0:T(8,128)(2,1)S(1)}, bf16[3,288,128]{2,1,0:T(8,128)(2,1)S(1)}) custom-call(s32[3,7]{1,0:T(4,128)S(1)} %get-tuple-element.47.want_ref, bf16[2048,576]{1,0:T(8,128)(2,1)S(1)} %bitcast.26, bf16[2048,512]{1,0:T(8,128)(2,1)S(1)} %get-tuple-element.55.g_ref, bf16[576,2048]{1,0:T(8,128)(2,1)S(1)} %get-tuple-element.72.weights_ref, ...), custom_call_target="tpu_custom_call" | custom-call | flops 1140850688 | bytes 8912896 | tf_op jit(solution)/shard_map/own_grads/pallas_call | solution.py:432
  38.9 0.1 collective-permute-start.9
  39.0 5.3 %outputs.1 = (bf16[2048,512]{1,0:T(8,128)(2,1)}, bf16[2048,576]{1,0:T(8,128)(2,1)S(1)}) custom-call(bf16[2,576,576]{2,1,0:T(8,128)(2,1)S(1)} %get-tuple-element.62.keys_ref, bf16[576,2048]{1,0:T(8,128)(2,1)S(1)} %get-tuple-element.72.weights_ref, bf16[576,2048]{1,0:T(8,128)(2,1)S(1)} %get-tuple-element.70.grads_ref), custom_call_target="tpu_custom_call" | custom-call | flops 2566914048 | bytes 8912896 | tf_op jit(solution)/shard_map/outputs/pallas_call | solution.py:453
  44.3 0.5 collective-permute-done.8
  44.8 0.0 collective-permute-done.9
  44.9 0.1 fusion.1
  45.0 1.3 %collective-permute-start.10 = (bf16[288,128]{1,0:T(8,128)(2,1)S(1)}, bf16[288,128]{1,0:T(8,128)(2,1)S(1)}, u32[]{:S(2)}, u32[]{:S(2)}) collective-permute-start(bf16[288,128]{1,0:T(8,128)(2,1)S(1)} %get-tuple-element.81), channel_id=1, source_target_pairs={{24,0},{28,4},{25,1},{29,5},{26,2},{30,6},{27,3},{31,7}} | collective-permute-start | bytes 221192 | tf_op jit(solution)/shard_map/ppermute | solution.py:489
  46.3 1.3 %collective-permute-start.11 = (bf16[288,128]{1,0:T(8,128)(2,1)S(1)}, bf16[288,128]{1,0:T(8,128)(2,1)S(1)}, u32[]{:S(2)}, u32[]{:S(2)}) collective-permute-start(bf16[288,128]{1,0:T(8,128)(2,1)S(1)} %get-tuple-element.82), channel_id=1, source_target_pairs={{16,0},{20,4},{24,8},{28,12},{17,1},{21,5},{25,9},{29,13},{18,2},{... | collective-permute-start | bytes 221192 | tf_op jit(solution)/shard_map/ppermute | solution.py:489
  47.6 1.3 %collective-permute-start.12 = (bf16[288,128]{1,0:T(8,128)(2,1)S(1)}, bf16[288,128]{1,0:T(8,128)(2,1)S(1)}, u32[]{:S(2)}, u32[]{:S(2)}) collective-permute-start(bf16[288,128]{1,0:T(8,128)(2,1)S(1)} %get-tuple-element.83), channel_id=1, source_target_pairs={{8,0},{12,4},{16,8},{20,12},{24,16},{28,20},{9,1},{13,5},{17,9},{2... | collective-permute-start | bytes 221192 | tf_op jit(solution)/shard_map/ppermute | solution.py:489
  48.9 3.1 %copy.10 = bf16[128,16,576]{0,2,1:T(8,128)(2,1)} copy(bf16[128,16,576]{2,1,0:T(8,128)(2,1)S(1)} %bitcast.27) | data formatting | bytes 4718592 | tf_op jit(solution)/shard_map/reshape | solution.py:532
  52.0 1.7 %collective-permute-done.10 = bf16[288,128]{1,0:T(8,128)(2,1)S(1)} collective-permute-done((bf16[288,128]{1,0:T(8,128)(2,1)S(1)}, bf16[288,128]{1,0:T(8,128)(2,1)S(1)}, u32[]{:S(2)}, u32[]{:S(2)}) %collective-permute-start.10) | collective-permute-done | bytes 73760 | tf_op jit(solution)/shard_map/ppermute | solution.py:489
  53.6 2.5 %collective-permute-done.11 = bf16[288,128]{1,0:T(8,128)(2,1)S(1)} collective-permute-done((bf16[288,128]{1,0:T(8,128)(2,1)S(1)}, bf16[288,128]{1,0:T(8,128)(2,1)S(1)}, u32[]{:S(2)}, u32[]{:S(2)}) %collective-permute-start.11) | collective-permute-done | bytes 73760 | tf_op jit(solution)/shard_map/ppermute | solution.py:489
  56.2 0.0 collective-permute-done.12
  56.2 1.6 %collective-permute-start.13 = (bf16[288,128]{1,0:T(8,128)(2,1)S(1)}, bf16[288,128]{1,0:T(8,128)(2,1)S(1)}, u32[]{:S(2)}, u32[]{:S(2)}) collective-permute-start(bf16[288,128]{1,0:T(8,128)(2,1)S(1)} %add_convert_fusion.1), channel_id=1, source_target_pairs={{0,2},{1,3},{2,0},{3,1},{4,6},{5,7},{6,4},{7,5},{8,10},{9,11},{10,... | collective-permute-start | bytes 221192 | tf_op jit(solution)/shard_map/ppermute | solution.py:539
  57.8 2.9 %collective-permute-done.13 = bf16[288,128]{1,0:T(8,128)(2,1)S(1)} collective-permute-done((bf16[288,128]{1,0:T(8,128)(2,1)S(1)}, bf16[288,128]{1,0:T(8,128)(2,1)S(1)}, u32[]{:S(2)}, u32[]{:S(2)}) %collective-permute-start.13) | collective-permute-done | bytes 73760 | tf_op jit(solution)/shard_map/ppermute | solution.py:539
  60.7 0.1 collective-permute-start.14
  60.8 1.4 %collective-permute-done.14 = f32[288,128]{1,0:T(8,128)S(1)} collective-permute-done((f32[288,128]{1,0:T(8,128)S(1)}, f32[288,128]{1,0:T(8,128)S(1)}, u32[]{:S(2)}, u32[]{:S(2)}) %collective-permute-start.14) | collective-permute-done | bytes 147488 | tf_op jit(solution)/shard_map/ppermute | solution.py:483
  62.1 0.7 %fusion = f32[128,576]{0,1:T(8,128)} fusion(f32[288,128]{1,0:T(8,128)S(1)} %collective-permute-done.14, f32[288,128]{1,0:T(8,128)S(1)} %convert_add_fusion.1, pred[]{:T(512)S(6)} %eq.5), kind=kLoop, calls=%fused_computation.3 | loop fusion | flops 221184 | bytes 589825 | tf_op jit(solution)/shard_map/transpose | solution.py:550
  (6 shorter events, 0.2 us)
Async XLA Ops:
  1.5 13.6 %collective-permute-start.2 = (bf16[1,288,128]{2,1,0:T(8,128)(2,1)S(1)}, bf16[1,288,128]{2,1,0:T(8,128)(2,1)S(1)}, u32[]{:S(2)}, u32[]{:S(2)}) collective-permute-start(bf16[1,288,128]{2,1,0:T(8,128)(2,1)S(1)} %dynamic-slice_bitcast_fusion.refs_0_), channel_id=1, source_target_pairs={{0,24},{4,28},{1,25},{5,29},{2,26},{6,30},{3,27},{7,31}} | collective-permute-start | bytes 221192 | tf_op jit(solution)/shard_map/ppermute | solution.py:486
  8.5 6.6 %collective-permute-start.1 = (bf16[1,288,128]{2,1,0:T(8,128)(2,1)S(1)}, bf16[1,288,128]{2,1,0:T(8,128)(2,1)S(1)}, u32[]{:S(2)}, u32[]{:S(2)}) collective-permute-start(bf16[1,288,128]{2,1,0:T(8,128)(2,1)S(1)} %dynamic-slice_bitcast_fusion.refs_0_), channel_id=1, source_target_pairs={{0,16},{4,20},{8,24},{12,28},{1,17},{5,21},{9,25},{13,29},{2,18},{... | collective-permute-start | bytes 221192 | tf_op jit(solution)/shard_map/ppermute | solution.py:486
  9.8 5.3 %collective-permute-start = (bf16[1,288,128]{2,1,0:T(8,128)(2,1)S(1)}, bf16[1,288,128]{2,1,0:T(8,128)(2,1)S(1)}, u32[]{:S(2)}, u32[]{:S(2)}) collective-permute-start(bf16[1,288,128]{2,1,0:T(8,128)(2,1)S(1)} %dynamic-slice_bitcast_fusion.refs_0_), channel_id=1, source_target_pairs={{0,8},{4,12},{8,16},{12,20},{16,24},{20,28},{1,9},{5,13},{9,17},{1... | collective-permute-start | bytes 221192 | tf_op jit(solution)/shard_map/ppermute | solution.py:486
  13.0 0.7 %copy-start.2 = (s32[128,8]{0,1:T(8,128)S(1)}, s32[128,8]{0,1:T(8,128)}, u32[]{:S(2)}) copy-start(s32[128,8]{0,1:T(8,128)} %param.9) | copy-start | bytes 12292
  15.2 5.6 %copy-start.1 = (bf16[128,576]{0,1:T(8,128)(2,1)S(1)}, bf16[128,576]{0,1:T(8,128)(2,1)}, u32[]{:S(2)}) copy-start(bf16[128,576]{0,1:T(8,128)(2,1)} %param.7) | copy-start | bytes 442372
  15.2 5.6 %collective-permute-start.3 = (bf16[4,288,128]{2,1,0:T(8,128)(2,1)S(1)}, bf16[4,288,128]{2,1,0:T(8,128)(2,1)S(1)}, u32[]{:S(2)}, u32[]{:S(2)}) collective-permute-start(bf16[4,288,128]{2,1,0:T(8,128)(2,1)S(1)} %join.1.mine_ref), channel_id=1, source_target_pairs={{0,1},{1,0},{2,3},{3,2},{4,5},{5,4},{6,7},{7,6},{8,9},{9,8},{10,11... | collective-permute-start | bytes 884744 | tf_op jit(solution)/shard_map/ppermute | solution.py:483
  15.3 9.7 %collective-permute-start.4 = (bf16[4,288,128]{2,1,0:T(8,128)(2,1)S(1)}, bf16[4,288,128]{2,1,0:T(8,128)(2,1)}, u32[]{:S(2)}, u32[]{:S(2)}) collective-permute-start(bf16[4,288,128]{2,1,0:T(8,128)(2,1)S(1)} %join.1.mine_ref), channel_id=1, source_target_pairs={{0,4},{4,0},{8,12},{12,8},{16,20},{20,16},{24,28},{28,24},{1,5},{5... | collective-permute-start | bytes 884744 | tf_op jit(solution)/shard_map/ppermute | solution.py:507
  20.8 1.6 %copy-start = (bf16[128,16,512]{2,1,0:T(8,128)(2,1)S(1)}, bf16[128,16,512]{2,1,0:T(8,128)(2,1)}, u32[]{:S(2)}) copy-start(bf16[128,16,512]{2,1,0:T(8,128)(2,1)} %param.8) | copy-start | bytes 6291460
  25.0 1.9 %collective-permute-start.5 = (bf16[4,288,128]{2,1,0:T(8,128)(2,1)}, bf16[4,288,128]{2,1,0:T(8,128)(2,1)S(1)}, u32[]{:S(2)}, u32[]{:S(2)}) collective-permute-start(bf16[4,288,128]{2,1,0:T(8,128)(2,1)} %collective-permute-done.4.mine_ref), channel_id=1, source_target_pairs={{0,1},{1,0},{2,3},{3,2},{4,5},{5,4},{6,7},{7,6},{8,9},{9,8},{10,11... | collective-permute-start | bytes 884744 | tf_op jit(solution)/shard_map/ppermute | solution.py:483
  33.5 1.6 %collective-permute-start.6 = (bf16[4,288,128]{2,1,0:T(8,128)(2,1)S(1)}, bf16[4,288,128]{2,1,0:T(8,128)(2,1)S(1)}, u32[]{:S(2)}, u32[]{:S(2)}) collective-permute-start(bf16[4,288,128]{2,1,0:T(8,128)(2,1)S(1)} %get-tuple-element.64), channel_id=1, source_target_pairs={{0,1},{1,0},{2,3},{3,2},{4,5},{5,4},{6,7},{7,6},{8,9},{9,8},{10,11... | collective-permute-start | bytes 884744 | tf_op jit(solution)/shard_map/ppermute | solution.py:483
  35.3 1.5 %collective-permute-start.7 = (bf16[1,288,128]{2,1,0:T(8,128)(2,1)S(1)}, bf16[1,288,128]{2,1,0:T(8,128)(2,1)S(1)}, u32[]{:S(2)}, u32[]{:S(2)}) collective-permute-start(bf16[1,288,128]{2,1,0:T(8,128)(2,1)S(1)} %get-tuple-element.67), channel_id=1, source_target_pairs={{0,1},{1,0},{2,3},{3,2},{4,5},{5,4},{6,7},{7,6},{8,9},{9,8},{10,11... | collective-permute-start | bytes 221192 | tf_op jit(solution)/shard_map/ppermute | solution.py:483
  35.5 9.3 %collective-permute-start.8 = (bf16[4,288,128]{2,1,0:T(8,128)(2,1)S(1)}, bf16[4,288,128]{2,1,0:T(8,128)(2,1)S(1)}, u32[]{:S(2)}, u32[]{:S(2)}) collective-permute-start(bf16[4,288,128]{2,1,0:T(8,128)(2,1)S(1)} %add_convert_fusion), channel_id=1, source_target_pairs={{0,4},{4,0},{8,12},{12,8},{16,20},{20,16},{24,28},{28,24},{1,5},{5... | collective-permute-start | bytes 884744 | tf_op jit(solution)/shard_map/ppermute | solution.py:519
  38.9 5.9 %collective-permute-start.9 = (bf16[3,288,128]{2,1,0:T(8,128)(2,1)S(1)}, bf16[3,288,128]{2,1,0:T(8,128)(2,1)S(1)}, u32[]{:S(2)}, u32[]{:S(2)}) collective-permute-start(bf16[3,288,128]{2,1,0:T(8,128)(2,1)S(1)} %get-tuple-element.78), channel_id=1, source_target_pairs={{0,1},{1,0},{2,3},{3,2},{4,5},{5,4},{6,7},{7,6},{8,9},{9,8},{10,11... | collective-permute-start | bytes 663560 | tf_op jit(solution)/shard_map/ppermute | solution.py:483
  45.0 8.7 %collective-permute-start.10 = (bf16[288,128]{1,0:T(8,128)(2,1)S(1)}, bf16[288,128]{1,0:T(8,128)(2,1)S(1)}, u32[]{:S(2)}, u32[]{:S(2)}) collective-permute-start(bf16[288,128]{1,0:T(8,128)(2,1)S(1)} %get-tuple-element.81), channel_id=1, source_target_pairs={{24,0},{28,4},{25,1},{29,5},{26,2},{30,6},{27,3},{31,7}} | collective-permute-start | bytes 221192 | tf_op jit(solution)/shard_map/ppermute | solution.py:489
  46.3 9.9 %collective-permute-start.11 = (bf16[288,128]{1,0:T(8,128)(2,1)S(1)}, bf16[288,128]{1,0:T(8,128)(2,1)S(1)}, u32[]{:S(2)}, u32[]{:S(2)}) collective-permute-start(bf16[288,128]{1,0:T(8,128)(2,1)S(1)} %get-tuple-element.82), channel_id=1, source_target_pairs={{16,0},{20,4},{24,8},{28,12},{17,1},{21,5},{25,9},{29,13},{18,2},{... | collective-permute-start | bytes 221192 | tf_op jit(solution)/shard_map/ppermute | solution.py:489
  47.6 8.6 %collective-permute-start.12 = (bf16[288,128]{1,0:T(8,128)(2,1)S(1)}, bf16[288,128]{1,0:T(8,128)(2,1)S(1)}, u32[]{:S(2)}, u32[]{:S(2)}) collective-permute-start(bf16[288,128]{1,0:T(8,128)(2,1)S(1)} %get-tuple-element.83), channel_id=1, source_target_pairs={{8,0},{12,4},{16,8},{20,12},{24,16},{28,20},{9,1},{13,5},{17,9},{2... | collective-permute-start | bytes 221192 | tf_op jit(solution)/shard_map/ppermute | solution.py:489
  56.2 4.4 %collective-permute-start.13 = (bf16[288,128]{1,0:T(8,128)(2,1)S(1)}, bf16[288,128]{1,0:T(8,128)(2,1)S(1)}, u32[]{:S(2)}, u32[]{:S(2)}) collective-permute-start(bf16[288,128]{1,0:T(8,128)(2,1)S(1)} %add_convert_fusion.1), channel_id=1, source_target_pairs={{0,2},{1,3},{2,0},{3,1},{4,6},{5,7},{6,4},{7,5},{8,10},{9,11},{10,... | collective-permute-start | bytes 221192 | tf_op jit(solution)/shard_map/ppermute | solution.py:539
  60.7 1.4 %collective-permute-start.14 = (f32[288,128]{1,0:T(8,128)S(1)}, f32[288,128]{1,0:T(8,128)S(1)}, u32[]{:S(2)}, u32[]{:S(2)}) collective-permute-start(f32[288,128]{1,0:T(8,128)S(1)} %convert_add_fusion.1), channel_id=1, source_target_pairs={{0,1},{1,0},{2,3},{3,2},{4,5},{5,4},{6,7},{7,6},{8,9},{9,8},{10,11... | collective-permute-start | bytes 442376 | tf_op jit(solution)/shard_map/ppermute | solution.py:483
